TPU v7x, 32 devices: a whole 2x2x4 slice. The times are simulated.
32 devices in a mesh: row: 4 (over x, core), col: 8 (over z, y).
Axes of the slice: x: 2, y: 2, z: 4, core: 2. Of those that a mesh axis runs over, the one named last changes fastest.
Arguments:
- upper_blocks: float32 [32, 9, 128, 128], P(('row', 'col')), as said below
- members: int32 [32, 9], P(('row', 'col')), may hold values from -1 to 31, as said below
Outputs:
- purified_blocks: float32 [32, 9, 128, 128], P(('row', 'col'))
Inputs may be any that keep to these rules, and one draw needn't show every extreme that they name: `members`: write j = r * 8 + q. Slot 0 holds j; slots 1 to 4 hold the blocks r * 8 + (q + d) mod 8 for d = -1, 1, -2, 2 in that order; slot 5 holds the block for d equal to half of 8; slot 6 the block for d = 3 when q is even and d = -3 when q is odd; slots 3 to 6 may hold -1 for an absent block; slots 7 and 8 hold blocks p * 8 + q of two other values p. The pattern is symmetric: a lists b exactly when b lists a (slots 1 and 2, and 3 and 4, trade places; slots 5 and 6 keep theirs; slots 7 and 8 trade places), and the blocks of slots 7 and 8 of one column never list each other. Slots 0, 1, 2, 7 and 8 are always present, and some block column has all 9. Slot t of upper_blocks[j] holds the block in block row members[j, t] and block column j when members[j, t] >= 0 and members[j, t] <= j, and zeros otherwise; the slot 0 block is symmetric.
All inputs are finite; a program needn't handle non-finite values.
Results may differ from a plain program's by a relative error of at most 0.0003.
Values sent between devices are 32-bit elements; how exact they have to be, the bound alone decides.
No kernel may reach another device: no remote copies, remote signals or barrier semaphores. Data moves between devices by JAX's collectives and lax.ppermute only.
A program may use at most 128 MiB of HBM per device.

v0:
```python
import jax
import jax.numpy as jnp
from jax import lax
from jax.sharding import PartitionSpec as P

PURIFY = 3


highest = lax.Precision.HIGHEST


def assemble(own_list, member_cols, member_lists):
    slot_count = own_list.shape[0]
    block_width = member_cols.shape[-1]
    matches = (
        (member_lists[:, :, None] == own_list[None, None, :]) & (own_list >= 0)[None, None, :]
    ).astype(jnp.float32)
    upper_part = jnp.einsum("uts,utxy->suxy", matches, member_cols, precision=highest)
    off_diagonal = (1.0 - jnp.eye(slot_count, dtype=jnp.float32))[:, :, None, None]
    full_blocks = upper_part + jnp.transpose(upper_part, (1, 0, 3, 2)) * off_diagonal
    order_total = slot_count * block_width
    return jnp.transpose(full_blocks, (0, 2, 1, 3)).reshape(order_total, order_total)


def purify(blocks, list_values, own_list, same_row, cross_group, keep_mask):
    slot_count = own_list.shape[0]
    block_width = blocks.shape[-1]
    group_cols = lax.axis_size("col")
    cross_cols, cross_lists = (
        lax.all_gather(blocks, "row", axis=0, tiled=True),
        lax.all_gather(list_values, "row", axis=0, tiled=True),
    )
    group_rows = cross_cols.shape[0]
    row_ids = jnp.arange(group_rows, dtype=jnp.int32)
    cross_pick = (
        cross_group[:, None] & ((own_list // group_cols)[:, None] == row_ids[None, :])
    ).astype(jnp.float32)
    group_blocks, group_lists = (
        lax.all_gather(blocks, "col", axis=0, tiled=True),
        lax.all_gather(list_values, "col", axis=0, tiled=True),
    )
    col_ids = jnp.arange(group_cols, dtype=jnp.int32)
    near_pick = (same_row[:, None] & ((own_list % group_cols)[:, None] == col_ids[None, :])).astype(
        jnp.float32
    )
    near_cols = jnp.einsum("ui,ikxy->ukxy", near_pick, group_blocks, precision=highest)
    near_lists = jnp.einsum("ui,ik->uk", near_pick, group_lists, precision=highest)
    member_cols = near_cols + jnp.einsum("ui,ikxy->ukxy", cross_pick, cross_cols, precision=highest)
    member_lists = (
        near_lists + jnp.einsum("ui,ik->uk", cross_pick, cross_lists, precision=highest)
    ).astype(jnp.int32)
    submatrix = assemble(own_list, member_cols, member_lists)
    first_cols = submatrix[:, :block_width]
    square_cols = jnp.dot(
        submatrix, first_cols, precision=highest, preferred_element_type=jnp.float32
    )
    cube_cols = jnp.dot(
        submatrix, square_cols, precision=highest, preferred_element_type=jnp.float32
    )
    low_local = jnp.trace(first_cols[:block_width] - square_cols[:block_width])
    high_local = jnp.trace(square_cols[:block_width] - cube_cols[:block_width])
    low_trace, high_trace = lax.psum((low_local, high_local), ("row", "col"))
    purity_coef = high_trace / low_trace
    columns = (
        (1.0 - 2.0 * purity_coef) * first_cols + (1.0 + purity_coef) * square_cols - cube_cols
    ) / (1.0 - purity_coef)
    fresh = columns.reshape(slot_count, block_width, block_width) * keep_mask[:, None, None]
    return fresh[None]


def body(upper_blocks, members):
    group_cols = lax.axis_size("col")
    own_list = members[0]
    own_index = own_list[0]
    own_row = own_index // group_cols
    own_col = own_index % group_cols
    present = own_list >= 0
    same_row = present & (own_list // group_cols == own_row)
    cross_group = present & (own_list // group_cols != own_row) & (own_list % group_cols == own_col)
    keep_mask = (present & (own_list <= own_index)).astype(jnp.float32)
    list_values = members.astype(jnp.float32)
    blocks = upper_blocks
    for repeat in range(PURIFY):
        blocks = purify(blocks, list_values, own_list, same_row, cross_group, keep_mask)
    return blocks


def solution(mesh):
    return jax.shard_map(
        body,
        mesh=mesh,
        in_specs=(P(("row", "col"), None, None, None), P(("row", "col"), None)),
        out_specs=P(("row", "col"), None, None, None),
        check_vma=False,
    )
```

profile of v0, /device:TPU:0, one launch (start us, length us, event | category | flops | bytes accessed | tf_op | source)
XLA Modules:
  0.0 711.3 jit_solution(6609119066385612552)
XLA Ops:
  6.5 0.0 all-gather.11.cloned.1.call-start
  6.5 0.7 all-gather.11.cloned.1.call-update
  7.3 0.0 all-gather.9.cloned.1.call-start
  7.3 0.7 all-gather.9.cloned.1.call-update
  8.0 0.0 all-gather.15.cloned.1.call-start
  10.7 0.7 convert_bitcast_fusion
  11.3 5.9 all-gather.1
  17.3 21.2 %all-gather = f32[8,1,9]{2,1,0:T(1,128)S(1)} all-gather(f32[1,1,9]{2,1,0:T(1,128)S(1)} %convert_bitcast_fusion), channel_id=1, replica_groups=mesh['row'=4,'col'=8] {'col'}, dimensions={0}, use_global_device_ids=true | all-gather | bytes 324 | tf_op jit(solution)/shard_map/all_gather | solution.py:40
  38.5 0.7 compare_and_fusion.5
  39.2 1.3 and_convert_fusion
  40.5 0.2 fusion.76
  40.7 0.2 fusion.27
  40.9 9.3 %fusion.25 = f32[9,9,128,128]{3,0,2,1:T(8,128)} fusion(f32[4,9,128,128]{3,2,1,0:T(8,128)} %all-gather.11.cloned.1.call-done, pred[9,4]{0,1:T(4,128)(4,1)S(1)} %fusion.68), kind=kOutput, calls=%fused_computation.25 | convolution fusion | flops 63700992 | bytes 7667748 | tf_op jit(solution)/shard_map/ui,ikxy->ukxy/dot_general | solution.py:48
  50.2 67.6 %all-gather.9.cloned.1.call-done = f32[8,9,128,128]{3,2,1,0:T(8,128)} async-done(((f32[1,9,128,128]{3,2,1,0:T(8,128)}), f32[8,9,128,128]{3,2,1,0:T(8,128)}) %all-gather.9.cloned.1.call-update) | async-done | bytes 4718608 | tf_op jit(solution)/shard_map/all_gather | solution.py:39
  117.8 9.7 %fusion.12 = f32[9,9,128,128]{3,0,2,1:T(8,128)S(1)} fusion(f32[9,9,128,128]{3,0,2,1:T(8,128)} %fusion.25, f32[8,9,128,128]{3,2,1,0:T(8,128)} %all-gather.9.cloned.1.call-done, s32[9]{0:T(128)S(1)} %get-tuple-element.24, pred[9]{0:T(512)(128)(4,1)S(1)} %get-tuple-element.17), kind=kOutput, calls=%fused_computation.18 | convolution fusion | flops 128729232 | bytes 15335469 | tf_op jit(solution)/shard_map/ui,ikxy->ukxy/dot_general | solution.py:46
  127.6 0.0 copy-done.3
  127.6 15.2 %fusion.4 = f32[9,128,128,9]{2,3,1,0:T(8,128)} fusion(f32[9,9,128,128]{3,0,2,1:T(8,128)S(1)} %fusion.12, s32[9,9]{1,0:T(8,128)S(1)} %fusion.27, s32[9]{0:T(128)S(1)} %bitcast.113, pred[9]{0:T(512)(128)(4,1)S(1)} %get-tuple-element.22), kind=kOutput, calls=%fused_computation.7 | convolution fusion | flops 143328688 | bytes 10617201 | tf_op jit(solution)/shard_map/uts,utxy->suxy/dot_general | solution.py:18
  142.8 17.1 %copy.15 = f32[9,128,128,9]{1,0,2,3:T(8,128)} copy(f32[9,128,128,9]{2,3,1,0:T(8,128)} %fusion.4) | data formatting | bytes 10616832 | tf_op jit(solution)/shard_map/uts,utxy->suxy/dot_general | solution.py:18
  159.9 11.3 %bitcast_add_fusion.2 = f32[9,128,9,128]{1,2,3,0:T(8,128)} fusion(f32[9,128,128,9]{1,0,2,3:T(8,128)} %copy.15, f32[9,128,128,9]{2,3,1,0:T(8,128)} %fusion.4, f32[9,9]{1,0:T(8,128)S(1)} %convert_subtract_fusion), kind=kLoop, calls=%fused_computation.2 | loop fusion | flops 2654208 | bytes 15925572 | tf_op jit(solution)/shard_map/add | solution.py:20
  171.1 9.6 %copy.16 = f32[9,128,9,128]{3,2,1,0:T(8,128)} copy(f32[9,128,9,128]{1,2,3,0:T(8,128)} %bitcast_add_fusion.2) | data formatting | bytes 10616832 | tf_op jit(solution)/shard_map/add | solution.py:20
  180.8 6.3 copy.62
  187.1 4.4 fusion.32
  191.5 4.4 fusion.77
  196.0 0.6 fusion.46
  196.6 47.6 %all-reduce.2 = (f32[]{:T(128)}, f32[]{:T(128)}) all-reduce(f32[]{:T(128)} %get-tuple-element.10, f32[]{:T(128)} %get-tuple-element.9), channel_id=1, replica_groups=mesh['row'=4,'col'=8] {'row','col'}, use_global_device_ids=true, to_apply=%region_1.2 | all-reduce | flops 2 | bytes 16 | tf_op jit(solution)/shard_map/psum | solution.py:62
  245.6 1.2 subtract_divide_fusion.2
  246.7 0.9 broadcast_multiply_fusion.2
  247.6 0.0 all-gather.15.cloned.1.call-update
  247.7 0.0 all-gather.13.cloned.1.call-start
  247.7 0.5 all-gather.13.cloned.1.call-update
  248.2 0.0 all-gather.19.cloned.1.call-start
  248.3 24.6 %all-gather.15.cloned.1.call-done = f32[4,9,128,128]{3,2,1,0:T(8,128)} async-done(((f32[1,9,128,128]{3,2,1,0:T(8,128)}), f32[4,9,128,128]{3,2,1,0:T(8,128)}) %all-gather.15.cloned.1.call-update) | async-done | bytes 2359312 | tf_op jit(solution)/shard_map/all_gather | solution.py:30
  272.9 9.3 %fusion.23 = f32[9,9,128,128]{3,0,2,1:T(8,128)} fusion(f32[4,9,128,128]{3,2,1,0:T(8,128)} %all-gather.15.cloned.1.call-done, pred[9,4]{0,1:T(4,128)(4,1)S(1)} %fusion.68), kind=kOutput, calls=%fused_computation.23 | convolution fusion | flops 63700992 | bytes 7667748 | tf_op jit(solution)/shard_map/ui,ikxy->ukxy/dot_general | solution.py:48
  282.2 72.6 %all-gather.13.cloned.1.call-done = f32[8,9,128,128]{3,2,1,0:T(8,128)} async-done(((f32[1,9,128,128]{3,2,1,0:T(8,128)}), f32[8,9,128,128]{3,2,1,0:T(8,128)}) %all-gather.13.cloned.1.call-update) | async-done | bytes 4718608 | tf_op jit(solution)/shard_map/all_gather | solution.py:39
  354.9 9.7 %fusion.15 = f32[9,9,128,128]{3,0,2,1:T(8,128)S(1)} fusion(f32[9,9,128,128]{3,0,2,1:T(8,128)} %fusion.23, f32[8,9,128,128]{3,2,1,0:T(8,128)} %all-gather.13.cloned.1.call-done, s32[9]{0:T(128)S(1)} %get-tuple-element.24, pred[9]{0:T(512)(128)(4,1)S(1)} %get-tuple-element.17), kind=kOutput, calls=%fused_computation.19 | convolution fusion | flops 128729232 | bytes 15335469 | tf_op jit(solution)/shard_map/ui,ikxy->ukxy/dot_general | solution.py:46
  364.6 15.2 %fusion.2 = f32[9,128,128,9]{2,3,1,0:T(8,128)} fusion(f32[9,9,128,128]{3,0,2,1:T(8,128)S(1)} %fusion.15, s32[9,9]{1,0:T(8,128)S(1)} %fusion.27, s32[9]{0:T(128)S(1)} %bitcast.114, pred[9]{0:T(512)(128)(4,1)S(1)} %get-tuple-element.22), kind=kOutput, calls=%fused_computation.5 | convolution fusion | flops 143328688 | bytes 10617201 | tf_op jit(solution)/shard_map/uts,utxy->suxy/dot_general | solution.py:18
  379.8 17.2 %copy.20 = f32[9,128,128,9]{1,0,2,3:T(8,128)} copy(f32[9,128,128,9]{2,3,1,0:T(8,128)} %fusion.2) | data formatting | bytes 10616832 | tf_op jit(solution)/shard_map/uts,utxy->suxy/dot_general | solution.py:18
  397.0 11.3 %bitcast_add_fusion.1 = f32[9,128,9,128]{1,2,3,0:T(8,128)} fusion(f32[9,128,128,9]{1,0,2,3:T(8,128)} %copy.20, f32[9,128,128,9]{2,3,1,0:T(8,128)} %fusion.2, f32[9,9]{1,0:T(8,128)S(1)} %convert_subtract_fusion), kind=kLoop, calls=%fused_computation.1 | loop fusion | flops 2654208 | bytes 15925572 | tf_op jit(solution)/shard_map/add | solution.py:20
  408.3 9.6 %copy.21 = f32[9,128,9,128]{3,2,1,0:T(8,128)} copy(f32[9,128,9,128]{1,2,3,0:T(8,128)} %bitcast_add_fusion.1) | data formatting | bytes 10616832 | tf_op jit(solution)/shard_map/add | solution.py:20
  417.9 6.3 copy.61
  424.2 4.4 fusion.30
  428.7 4.4 fusion.78
  433.1 0.6 fusion.42
  433.8 38.8 %all-reduce.1 = (f32[]{:T(128)}, f32[]{:T(128)}) all-reduce(f32[]{:T(128)} %get-tuple-element.8, f32[]{:T(128)} %get-tuple-element.7), channel_id=1, replica_groups=mesh['row'=4,'col'=8] {'row','col'}, use_global_device_ids=true, to_apply=%region_5.6 | all-reduce | flops 2 | bytes 16 | tf_op jit(solution)/shard_map/psum | solution.py:62
  474.0 1.2 subtract_divide_fusion.1
  475.1 0.9 broadcast_multiply_fusion.1
  476.1 0.0 all-gather.19.cloned.1.call-update
  476.1 0.0 all-gather.17.cloned.1.call-start
  476.1 0.5 all-gather.17.cloned.1.call-update
  476.7 24.7 %all-gather.19.cloned.1.call-done = f32[4,9,128,128]{3,2,1,0:T(8,128)} async-done(((f32[1,9,128,128]{3,2,1,0:T(8,128)}), f32[4,9,128,128]{3,2,1,0:T(8,128)}) %all-gather.19.cloned.1.call-update) | async-done | bytes 2359312 | tf_op jit(solution)/shard_map/all_gather | solution.py:30
  501.3 9.3 %fusion.21 = f32[9,9,128,128]{3,0,2,1:T(8,128)} fusion(f32[4,9,128,128]{3,2,1,0:T(8,128)} %all-gather.19.cloned.1.call-done, pred[9,4]{0,1:T(4,128)(4,1)S(1)} %fusion.68), kind=kOutput, calls=%fused_computation.21 | convolution fusion | flops 63700992 | bytes 7667748 | tf_op jit(solution)/shard_map/ui,ikxy->ukxy/dot_general | solution.py:48
  510.6 72.6 %all-gather.17.cloned.1.call-done = f32[8,9,128,128]{3,2,1,0:T(8,128)} async-done(((f32[1,9,128,128]{3,2,1,0:T(8,128)}), f32[8,9,128,128]{3,2,1,0:T(8,128)}) %all-gather.17.cloned.1.call-update) | async-done | bytes 4718608 | tf_op jit(solution)/shard_map/all_gather | solution.py:39
  583.3 9.7 %fusion.18 = f32[9,9,128,128]{3,0,2,1:T(8,128)S(1)} fusion(f32[9,9,128,128]{3,0,2,1:T(8,128)} %fusion.21, f32[8,9,128,128]{3,2,1,0:T(8,128)} %all-gather.17.cloned.1.call-done, s32[9]{0:T(128)S(1)} %get-tuple-element.24, pred[9]{0:T(512)(128)(4,1)S(1)} %get-tuple-element.17), kind=kOutput, calls=%fused_computation.20 | convolution fusion | flops 128729232 | bytes 15335469 | tf_op jit(solution)/shard_map/ui,ikxy->ukxy/dot_general | solution.py:46
  593.0 15.2 %fusion = f32[9,128,128,9]{2,3,1,0:T(8,128)} fusion(f32[9,9,128,128]{3,0,2,1:T(8,128)S(1)} %fusion.18, s32[9,9]{1,0:T(8,128)S(1)} %fusion.27, s32[9]{0:T(128)S(1)} %bitcast.115, pred[9]{0:T(512)(128)(4,1)S(1)} %get-tuple-element.22), kind=kOutput, calls=%fused_computation.3 | convolution fusion | flops 143328688 | bytes 10617201 | tf_op jit(solution)/shard_map/uts,utxy->suxy/dot_general | solution.py:18
  608.2 16.9 %copy.25 = f32[9,128,128,9]{1,0,2,3:T(8,128)} copy(f32[9,128,128,9]{2,3,1,0:T(8,128)} %fusion) | data formatting | bytes 10616832 | tf_op jit(solution)/shard_map/uts,utxy->suxy/dot_general | solution.py:18
  625.1 11.3 %bitcast_add_fusion = f32[9,128,9,128]{1,2,3,0:T(8,128)} fusion(f32[9,128,128,9]{1,0,2,3:T(8,128)} %copy.25, f32[9,128,128,9]{2,3,1,0:T(8,128)} %fusion, f32[9,9]{1,0:T(8,128)S(1)} %convert_subtract_fusion), kind=kLoop, calls=%fused_computation | loop fusion | flops 2654208 | bytes 15925572 | tf_op jit(solution)/shard_map/add | solution.py:20
  636.3 9.8 %copy.26 = f32[9,128,9,128]{3,2,1,0:T(8,128)} copy(f32[9,128,9,128]{1,2,3,0:T(8,128)} %bitcast_add_fusion) | data formatting | bytes 10616832 | tf_op jit(solution)/shard_map/add | solution.py:20
  646.2 6.3 copy.60
  652.5 4.4 fusion.28
  656.9 4.4 fusion.79
  661.4 0.6 fusion.38
  662.0 38.6 %all-reduce = (f32[]{:T(128)}, f32[]{:T(128)}) all-reduce(f32[]{:T(128)} %get-tuple-element.6, f32[]{:T(128)} %get-tuple-element.5), channel_id=1, replica_groups=mesh['row'=4,'col'=8] {'row','col'}, use_global_device_ids=true, to_apply=%region_9.10 | all-reduce | flops 2 | bytes 16 | tf_op jit(solution)/shard_map/psum | solution.py:62
  702.0 1.2 subtract_divide_fusion
  703.2 0.9 broadcast_multiply_fusion
  (10 shorter events, 0.0 us)
Async XLA Ops:
  6.5 34.4 %all-gather.11.cloned.1.call-start = ((), (), s32[]{:S(2)}) async-start(), calls=%async_computation.1 | async-start | bytes 2949120 | tf_op jit(solution)/shard_map/all_gather | solution.py:30
  7.3 110.6 %all-gather.9.cloned.1.call-start = ((), (), s32[]{:S(2)}) async-start(), calls=%async_computation | async-start | bytes 5308416 | tf_op jit(solution)/shard_map/all_gather | solution.py:39
  8.0 264.9 %all-gather.15.cloned.1.call-start = ((), (), s32[]{:S(2)}) async-start(), calls=%async_computation.3 | async-start | bytes 2949120 | tf_op jit(solution)/shard_map/all_gather | solution.py:30
  50.2 77.3 %copy-start.3 = (s32[1,9]{1,0:T(1,128)S(1)}, s32[1,9]{1,0:T(1,128)}, u32[]{:S(2)}) copy-start(s32[1,9]{1,0:T(1,128)} %param.3) | copy-start | bytes 112
  187.1 8.9 %copy-start.1 = (f32[144,8,9,128]{3,1,2,0:T(8,128)}, f32[144,8,9,128]{3,1,2,0:T(8,128)S(1)}, u32[]{:S(2)}) copy-start(f32[144,8,9,128]{3,1,2,0:T(8,128)S(1)} %copy.62) | copy-start | bytes 15925252
  247.7 107.2 %all-gather.13.cloned.1.call-start = ((), (), s32[]{:S(2)}) async-start(), calls=%async_computation.2 | async-start | bytes 5308416 | tf_op jit(solution)/shard_map/all_gather | solution.py:39
  248.2 253.1 %all-gather.19.cloned.1.call-start = ((), (), s32[]{:S(2)}) async-start(), calls=%async_computation.5 | async-start | bytes 2949120 | tf_op jit(solution)/shard_map/all_gather | solution.py:30
  424.2 8.9 %copy-start.2 = (f32[144,8,9,128]{3,1,2,0:T(8,128)}, f32[144,8,9,128]{3,1,2,0:T(8,128)S(1)}, u32[]{:S(2)}) copy-start(f32[144,8,9,128]{3,1,2,0:T(8,128)S(1)} %copy.61) | copy-start | bytes 15925252
  476.1 107.2 %all-gather.17.cloned.1.call-start = ((), (), s32[]{:S(2)}) async-start(), calls=%async_computation.4 | async-start | bytes 5308416 | tf_op jit(solution)/shard_map/all_gather | solution.py:39
  652.5 8.9 %copy-start = (f32[144,8,9,128]{3,1,2,0:T(8,128)}, f32[144,8,9,128]{3,1,2,0:T(8,128)S(1)}, u32[]{:S(2)}) copy-start(f32[144,8,9,128]{3,1,2,0:T(8,128)S(1)} %copy.60) | copy-start | bytes 15925252
Sparse Core Ops, SparseCore 0:
  8.9 26.7 all-gather.10
  37.9 79.8 all-gather.8
  247.8 25.0 all-gather.14
  274.9 79.8 all-gather.12
  476.2 25.0 all-gather.18
  503.3 79.8 all-gather.16
where the time goes:
time: 721 us; the launch traced here: 711 us
  waiting for transfers between devices  265 us (37%)
  blocking collectives  152 us (21%)
  matrix products  130 us (18%)
  local copies, waits for them, and re-layouts  99.2 us (14%)
  other arithmetic  44.7 us (6%)
  between operations  20.8 us (3%)
    all_gather x3, waiting for transfers between devices, purify(): lax.all_gather(blocks, 'col', axis=0, tiled=True)  213 us
    psum x3, blocking collectives, purify(): low_trace, high_trace = lax.psum((low_local, high_local), ('row', 'col'))  125 us
    dot_general x3, local copies, waits for them, and re-layouts, assemble(): jnp.einsum('uts,utxy->suxy', matches, member_cols, precision=highest)  51.2 us
    all_gather x3, waiting for transfers between devices, purify(): lax.all_gather(blocks, 'row', axis=0, tiled=True)  49.3 us
    dot_general x3, matrix products, assemble(): jnp.einsum('uts,utxy->suxy', matches, member_cols, precision=highest)  45.5 us
    add x3, other arithmetic, assemble(): upper_part + jnp.transpose(upper_part, (1, 0, 3, 2)) * off_diagonal  33.9 us
    dot_general x3, matrix products, purify(): jnp.einsum('ui,ikxy->ukxy', near_pick, group_blocks, precision=highest)  29.2 us
    add x3, local copies, waits for them, and re-layouts, assemble(): upper_part + jnp.transpose(upper_part, (1, 0, 3, 2)) * off_diagonal  29 us
  transfers between devices with their start and end apart: 6, of which 5 were waited for; matrix products, arithmetic and copies ran while one was open for 4% of the time, Pallas kernels for 0%

commit v1 on v0

v1 whole, which is shorter than its diff:
```python
import functools
import math

import jax
import jax.numpy as jnp
from jax import lax
from jax.experimental import pallas as pl
from jax.experimental.pallas import tpu as pltpu
from jax.sharding import PartitionSpec as P

PURIFY = 3
BW = 128
TILE = 256
NEAR = 7
PACK = BW + 8
SPARE = 8 * 1024 * 1024
MOST = 60 * 1024 * 1024

f32 = jnp.float32
bf16 = jnp.bfloat16


def offsets(q, nq):
    return [0, -1, 1, -2, 2, nq // 2, 3 if q % 2 == 0 else -3]


@functools.lru_cache
def pattern(nq):
    pairs = [(q, q) for q in range(nq)]
    for b in range(nq):
        for d in offsets(b, nq)[1:]:
            a = (b + d) % nq
            if a < b:
                pairs.append((a, b))
    return tuple(pairs)


@functools.lru_cache
def pair_index(nq):
    return {pair: i for i, pair in enumerate(pattern(nq))}


def slot_of(a, b, nq):
    return [(b + d) % nq for d in offsets(b, nq)].index(a)


@functools.lru_cache
def tiles(nq):
    index = pair_index(nq)
    n = nq * BW // TILE
    per = TILE // BW

    def live(i, j):
        lo, hi = min(i, j), max(i, j)
        return any(
            (a, b) in index or (b, a) in index
            for a in range(lo * per, (lo + 1) * per)
            for b in range(hi * per, (hi + 1) * per)
        )

    out = []
    for i in range(n):
        for j in range(i, n):
            if live(i, j):
                inner = [k for k in range(n) if live(i, k) and live(k, j)]
                out.append((i, j, inner))
    return out


def split(x):
    hi = x.astype(bf16)
    return hi, (x - hi.astype(f32)).astype(bf16)


def mm(a, b):
    return jnp.dot(a, b, preferred_element_type=f32)


def dot3(ah, al, bh, bl):
    return mm(ah, bh) + (mm(ah, bl) + mm(al, bh))


def dotf(a, b):
    return dot3(*split(a), *split(b))


def row_col():
    return (
        lax.broadcasted_iota(jnp.int32, (BW, BW), 0),
        lax.broadcasted_iota(jnp.int32, (BW, BW), 1),
    )


def total(x):
    s = jnp.sum(jnp.sum(x, axis=0, keepdims=True), axis=1, keepdims=True)
    return jnp.broadcast_to(s, (1, BW))


def pack_pair(ref, first, second):
    i, j = row_col()
    ref[0:BW, :] = jnp.where(i <= j, first, second)
    ref[BW : BW + 1, :] = jnp.sum(jnp.where(i == j, second, 0.0), axis=0, keepdims=True)


def unpack_pair(block, diagonal):
    i, j = row_col()
    flipped = block.T
    first = jnp.where(i <= j, block, flipped)
    second = jnp.where(i > j, block, jnp.where(i == j, diagonal, flipped))
    return first, second


def at(q):
    return pl.ds(pl.multiple_of(q * BW, BW), BW)


def cut(q):
    return slice(q * BW, (q + 1) * BW)


def put_dense(hi_ref, lo_ref, a, b, block):
    hi, lo = split(block)
    hi_ref[cut(a), cut(b)] = hi
    lo_ref[cut(a), cut(b)] = lo
    if a != b:
        hi, lo = split(block.T)
        hi_ref[cut(b), cut(a)] = hi
        lo_ref[cut(b), cut(a)] = lo


def clear_unlinked(hi_ref, lo_ref, nq):
    index = pair_index(nq)
    zero = jnp.zeros((BW, BW), bf16)
    for a in range(nq):
        for b in range(nq):
            if (min(a, b), max(a, b)) not in index:
                hi_ref[cut(a), cut(b)] = zero
                lo_ref[cut(a), cut(b)] = zero


def tile_products(ah, al, bh, bl, nq):
    index = pair_index(nq)
    per = TILE // BW
    n = nq * BW // TILE
    for i, j, inner in tiles(nq):
        rows, cols = slice(i * TILE, (i + 1) * TILE), slice(j * TILE, (j + 1) * TILE)
        if len(inner) == n:
            acc = dot3(ah[rows, :], al[rows, :], bh[:, cols], bl[:, cols])
        else:
            acc = None
            for k in inner:
                mid = slice(k * TILE, (k + 1) * TILE)
                part = dot3(ah[rows, mid], al[rows, mid], bh[mid, cols], bl[mid, cols])
                acc = part if acc is None else acc + part
        for x in range(per):
            for y in range(per):
                a, b = i * per + x, j * per + y
                if (a, b) in index:
                    yield (a, b), acc[cut(x), cut(y)]


def square_part(nq, q, own_pack, m_ref, mh, ml, link, s_ref, sh, sl, out_ref):
    index = pair_index(nq)
    clear_unlinked(sh, sl, nq)
    trace = jnp.zeros((BW, BW), f32)
    norm = jnp.zeros((BW, BW), f32)
    inner = jnp.zeros((BW, BW), f32)
    i, j = row_col()
    for (a, b), block in tile_products(mh, ml, mh, ml, nq):
        if a != b:
            block = block * link[a : a + 1, cut(b)]
        at_list = index[(a, b)]
        s_ref[at_list] = block
        put_dense(sh, sl, a, b, block)
        own = m_ref[at_list]
        if a == b:
            trace = trace + own
            norm = norm + own * own
            inner = inner + own * block
        else:
            norm = norm + 2.0 * (own * own)
            inner = inner + 2.0 * (own * block)
    g, e = unpack_pair(own_pack[0:BW, :], own_pack[BW : BW + 1, :])
    d = m_ref[q]
    dg = dotf(d, g)
    s0 = s_ref[q] + g
    k0 = dot3(mh[at(q), :], ml[at(q), :], sh[:, at(q)], sl[:, at(q)]) + (dg + dg.T) + e
    pack_pair(out_ref, s0, k0)
    out_ref[BW + 1 : BW + 2, :] = total(jnp.where(i == j, trace, 0.0))
    out_ref[BW + 2 : BW + 3, :] = total(norm)
    out_ref[BW + 3 : BW + 4, :] = total(inner)
    out_ref[BW + 4 : BW + 8, :] = jnp.zeros((4, BW), f32)


def first_kernel(nq, ids, near, own_pack, m_ref, mh, ml, link, s_ref, sh, sl, out_ref):
    q = ids[1]
    clear_unlinked(mh, ml, nq)
    link[...] = jnp.zeros_like(link)
    for (a, b), place in pair_index(nq).items():
        t = slot_of(a, b, nq)
        block = near[b, cut(t), :]
        m_ref[place] = block
        put_dense(mh, ml, a, b, block)
    for a in range(nq):
        present = jnp.where(near[a, NEAR * BW : NEAR * BW + 1, :] >= 0.0, 1.0, 0.0)
        for t, d in enumerate(offsets(a, nq)):
            b = (a + d) % nq
            link[a : a + 1, cut(b)] = jnp.broadcast_to(present[:, t : t + 1], (1, BW))
    square_part(nq, q, own_pack, m_ref, mh, ml, link, s_ref, sh, sl, out_ref)


def assemble(nq, q, coef, packs, x_ref, y_ref, m_old, held, m_ref, mh, ml):
    index = pair_index(nq)
    c = coef[0:1, :]
    inv = coef[1:2, :]
    for k in range(nq):
        held[k ^ q] = packs[k][...]
    clear_unlinked(mh, ml, nq)
    for b in range(nq):
        g, e = unpack_pair(held[b, 0:BW, :], held[b, BW : BW + 1, :])
        gh, gl = split(g)
        for (a, b2), place in index.items():
            if b2 != b:
                continue
            fix = dot3(*split(m_old[place]), gh, gl)
            block = x_ref[place] + c * y_ref[place]
            if a == b:
                block = block + (1.0 + c) * g - (fix + fix.T + e)
            else:
                block = block - fix
            block = block * inv
            m_ref[place] = block
            put_dense(mh, ml, a, b, block)


def next_kernel(nq, ids, coef, *refs):
    packs, own_pack, refs = refs[:nq], refs[nq], refs[nq + 1 :]
    x_ref, y_ref, m_old, link, m_ref, mh, ml, s_ref, sh, sl, out_ref, held = refs
    q = ids[1]
    assemble(nq, q, coef, packs, x_ref, y_ref, m_old, held, m_ref, mh, ml)
    square_part(nq, q, own_pack, m_ref, mh, ml, link, s_ref, sh, sl, out_ref)


def cube_kernel(nq, m_ref, mh, ml, s_ref, sh, sl, link, x_ref, y_ref):
    index = pair_index(nq)
    for (a, b), block in tile_products(mh, ml, sh, sl, nq):
        if a != b:
            block = block * link[a : a + 1, cut(b)]
        place = index[(a, b)]
        m, s = m_ref[place], s_ref[place]
        x_ref[place] = (m + s) - block
        y_ref[place] = s - 2.0 * m


def edge_ends(lists, nq, e):
    far = lax.div(lists[e, 8], jnp.int32(nq))
    return jnp.minimum(far, e), jnp.maximum(far, e)


def cross_tail(nr, nq, ids, lists, d_ref, u_ref, su_ref, v_ref, pack_ref):
    r = ids[0]
    norm = jnp.zeros((BW, BW), f32)
    inner = jnp.zeros((BW, BW), f32)
    for e in range(nr):
        lo, hi = edge_ends(lists, nq, e)
        u = u_ref[e]
        uh, ul = split(u)
        dlo = split(d_ref[lo])
        su = dot3(uh, ul, *split(d_ref[hi])) + dot3(*dlo, uh, ul)
        su_ref[e] = su
        v_ref[e] = dot3(*dlo, *split(su))
        norm = norm + u * u
        inner = inner + u * su
    g_sum = jnp.zeros((BW, BW), f32)
    e_sum = jnp.zeros((BW, BW), f32)
    for slot in (7, 8):
        far = lax.div(lists[r, slot], jnp.int32(nq))
        u = u_ref[r if slot == 8 else far]
        flipped = u.T
        mine = r > far
        cu = split(jnp.where(mine, u, flipped))
        cut_ = split(jnp.where(mine, flipped, u))
        g_sum = g_sum + dot3(*cut_, *cu)
        t = dot3(*split(d_ref[far]), *cu)
        e_sum = e_sum + dot3(*cut_, *split(t))
    pack_pair(pack_ref, g_sum, e_sum)
    pack_ref[BW + 1 : BW + 2, :] = 2.0 * total(norm)
    pack_ref[BW + 2 : BW + 3, :] = 3.0 * total(inner)
    pack_ref[BW + 3 : BW + 8, :] = jnp.zeros((5, BW), f32)


def cross_first_kernel(nr, nq, ids, lists, row, d_ref, u_ref, su_ref, v_ref, pack_ref):
    for e in range(nr):
        d_ref[e] = row[e, cut(0), :]
    for e in range(nr):
        far = lax.div(lists[e, 8], jnp.int32(nq))
        here = row[e, cut(2), :]
        there = row[far, cut(1), :]
        u_ref[e] = jnp.where(far < e, here, there)
    cross_tail(nr, nq, ids, lists, d_ref, u_ref, su_ref, v_ref, pack_ref)


def coefficient(nr, nq, q, rows, packs, held):
    for k in range(nq):
        held[k ^ q] = packs[k][BW : BW + 8, :]
    trace = rows[0, BW + 1 : BW + 2, :]
    norm = rows[0, BW + 2 : BW + 3, :]
    inner = rows[0, BW + 3 : BW + 4, :]
    for r in range(1, nr):
        trace = trace + rows[r, BW + 1 : BW + 2, :]
        norm = norm + rows[r, BW + 2 : BW + 3, :]
        inner = inner + rows[r, BW + 3 : BW + 4, :]
    for k in range(nq):
        norm = norm + held[k, 1:2, :]
        inner = inner + held[k, 2:3, :]
    c = (norm - inner) / (trace - norm)
    return c, 1.0 / (1.0 - c)


def cross_kernel(nr, nq, ids, lists, rows, *refs):
    packs, refs = refs[:nq], refs[nq:]
    d_old, u_old, su_old, v_old, coef, d_ref, u_ref, su_ref, v_ref, pack_ref, held = refs
    c, inv = coefficient(nr, nq, ids[1], rows, packs, held)
    coef[0:1, :] = c
    coef[1:2, :] = inv
    coef[2:8, :] = jnp.zeros((6, BW), f32)
    for r in range(nr):
        s0, k0 = unpack_pair(rows[r, 0:BW, :], rows[r, BW : BW + 1, :])
        d = d_old[r]
        d_ref[r] = ((1.0 - 2.0 * c) * d + (1.0 + c) * s0 - k0) * inv
    for e in range(nr):
        lo, hi = edge_ends(lists, nq, e)
        s0, _ = unpack_pair(rows[hi, 0:BW, :], rows[hi, BW : BW + 1, :])
        u, su = u_old[e], su_old[e]
        k = dotf(u, s0) + v_old[e]
        u_ref[e] = ((1.0 - 2.0 * c) * u + (1.0 + c) * su - k) * inv
    cross_tail(nr, nq, ids, lists, d_ref, u_ref, su_ref, v_ref, pack_ref)


def last_kernel(nr, nq, ids, lists, coef, *refs):
    packs, refs = refs[:nq], refs[nq:]
    own_pack, x_old, y_old, m_old, link, d_ref, u_ref, su_ref, v_ref = refs[:9]
    x_out, y_out, sums, held, m_ref, mh, ml, col, sq, sqh, sql = refs[9:]
    r, q = ids[0], ids[1]
    assemble(nq, q, coef, packs, x_old, y_old, m_old, held, m_ref, mh, ml)
    g, e = unpack_pair(own_pack[0:BW, :], own_pack[BW : BW + 1, :])
    sq[...] = dot3(mh[...], ml[...], mh[:, at(q)], ml[:, at(q)])
    for a in range(nq):
        sq[cut(a), :] = sq[cut(a), :] * link[a : a + 1, at(q)]
    sq[at(q), :] = sq[at(q), :] + g
    hi, lo = split(sq[...])
    sqh[...] = hi
    sql[...] = lo
    d = m_ref[q]
    s0 = sq[at(q), :]
    col[...] = dot3(mh[...], ml[...], hi, lo)
    k0 = col[at(q), :] + dotf(g, d) + e
    i, j = row_col()
    sums[0:1, :] = total(jnp.where(i == j, d - s0, 0.0))
    sums[1:2, :] = total(jnp.where(i == j, s0 - k0, 0.0))
    sums[2:8, :] = jnp.zeros((6, BW), f32)
    x_out[0] = (d + s0) - k0
    y_out[0] = s0 - 2.0 * d
    for t in range(1, NEAR):
        if t < 6:
            a = lax.rem(q + jnp.int32(offsets(0, nq)[t] + nq), jnp.int32(nq))
        else:
            step = jnp.where(lax.rem(q, jnp.int32(2)) == 0, 3, nq - 3)
            a = lax.rem(q + step, jnp.int32(nq))
        m = mh[at(a), at(q)].astype(f32) + ml[at(a), at(q)].astype(f32)
        s = sq[at(a), :]
        x_out[t] = (m + s) - col[at(a), :]
        y_out[t] = s - 2.0 * m
    sh, sl = split(s0)
    for t in (7, 8):
        far = lax.div(lists[r, t], jnp.int32(nq))
        edge = r if t == 8 else far
        u, su = u_ref[edge], su_ref[edge]
        k = dot3(*split(u), sh, sl) + v_ref[edge]
        x_out[t] = (u + su) - k
        y_out[t] = su - 2.0 * u


def finish_kernel(slots, lists, ids, parts, x_ref, y_ref, out_ref):
    sums = jnp.sum(parts[...], axis=0, keepdims=True)
    half = BW // 2
    low = jnp.broadcast_to(sums[:, 0:1], (1, BW))
    high = jnp.broadcast_to(sums[:, half : half + 1], (1, BW))
    c = high / low
    inv = 1.0 / (1.0 - c)
    r = ids[0]
    own = lists[r, 0]
    for t in range(slots):
        a = lists[r, t]
        keep = jnp.logical_and(a >= 0, a <= own)
        out_ref[0, t] = jnp.where(keep, (x_ref[t] + c * y_ref[t]) * inv, 0.0)


def room(args, outs, scratch):
    sizes = [math.prod(a.shape) * a.dtype.itemsize for a in args]
    sizes += [math.prod(s) * jnp.dtype(d).itemsize for s, d in outs]
    sizes += [math.prod(s.shape) * jnp.dtype(s.dtype).itemsize for s in scratch]
    return min(sum(sizes) + SPARE, MOST)


def call(kernel, outs, args, scalars, scratch=(), flops=0):
    specs = [
        pl.BlockSpec(memory_space=pltpu.SMEM if i < scalars else pltpu.VMEM)
        for i in range(len(args))
    ]
    return pl.pallas_call(
        kernel,
        out_shape=[jax.ShapeDtypeStruct(s, d) for s, d in outs],
        in_specs=specs,
        out_specs=[pl.BlockSpec(memory_space=pltpu.VMEM) for _ in outs],
        scratch_shapes=list(scratch),
        compiler_params=pltpu.CompilerParams(vmem_limit_bytes=room(args, outs, scratch)),
        cost_estimate=pl.CostEstimate(flops=flops, bytes_accessed=0, transcendentals=0),
    )(*args)


def spread(x, nq):
    return [x] + [
        lax.ppermute(x, "col", [(i, i ^ k) for i in range(nq)]) for k in range(1, nq)
    ]


def body(upper_blocks, members):
    nr, nq = lax.axis_size("row"), lax.axis_size("col")
    blocks = upper_blocks[0]
    slots = blocks.shape[0]
    order = nq * BW
    npair = len(pattern(nq))
    ids = jnp.stack([lax.axis_index("row"), lax.axis_index("col")]).astype(jnp.int32)

    flat = blocks.reshape(slots * BW, BW)
    names = jnp.pad(members.astype(f32), ((0, 7), (0, BW - slots)))
    row_part = jnp.concatenate([flat[:BW], flat[NEAR * BW :], names])
    near_part = jnp.concatenate([flat[: NEAR * BW], names])
    row = lax.all_gather(row_part, "row", axis=0)
    near = lax.all_gather(near_part, "col", axis=0)
    lists = row[:, 3 * BW, :slots].astype(jnp.int32)

    listed = (npair, BW, BW)
    dense = (order, order)
    edges = (nr, BW, BW)
    pack = (PACK, BW)
    cross_outs = [(edges, f32)] * 4 + [(pack, f32)]
    square_outs = [(listed, f32), (dense, bf16), (dense, bf16), (pack, f32)]

    d, u, su, v, own = call(
        functools.partial(cross_first_kernel, nr, nq), cross_outs, (ids, lists, row), 2
    )
    packs = spread(own, nq)
    m, mh, ml, link, s, sh, sl, tell = call(
        functools.partial(first_kernel, nq),
        [(listed, f32), (dense, bf16), (dense, bf16), ((nq, order), f32)] + square_outs,
        (ids, near, own),
        1,
    )
    for step in range(PURIFY - 1):
        rows = lax.all_gather(tell, "row", axis=0)
        x, y = call(
            functools.partial(cube_kernel, nq),
            [(listed, f32)] * 2,
            (m, mh, ml, s, sh, sl, link),
            0,
        )
        coef, d, u, su, v, own = call(
            functools.partial(cross_kernel, nr, nq),
            [((8, BW), f32)] + cross_outs,
            (ids, lists, rows, *packs, d, u, su, v),
            2,
            [pltpu.VMEM((nq, 8, BW), f32)],
        )
        old = packs
        if step < PURIFY - 2:
            packs = spread(own, nq)
            m, mh, ml, s, sh, sl, tell = call(
                functools.partial(next_kernel, nq),
                [(listed, f32), (dense, bf16), (dense, bf16)] + square_outs,
                (ids, coef, *old, own, x, y, m, link),
                1,
                [pltpu.VMEM((nq, PACK, BW), f32)],
            )
    strip = (order, BW)
    xo, yo, sums = call(
        functools.partial(last_kernel, nr, nq),
        [((slots, BW, BW), f32)] * 2 + [((8, BW), f32)],
        (ids, lists, coef, *old, own, x, y, m, link, d, u, su, v),
        2,
        [
            pltpu.VMEM((nq, PACK, BW), f32),
            pltpu.VMEM(listed, f32),
            pltpu.VMEM(dense, bf16),
            pltpu.VMEM(dense, bf16),
            pltpu.VMEM(strip, f32),
            pltpu.VMEM(strip, f32),
            pltpu.VMEM(strip, bf16),
            pltpu.VMEM(strip, bf16),
        ],
    )
    lane = jnp.arange(BW) < BW // 2
    mine = jnp.where(lane, sums[0], sums[1])
    parts = lax.all_to_all(
        jnp.broadcast_to(mine[None], (nr * nq, BW)), ("row", "col"), 0, 0, tiled=True
    )
    (out,) = call(
        functools.partial(finish_kernel, slots),
        [((1, slots, BW, BW), f32)],
        (lists, ids, parts, xo, yo),
        2,
    )
    return out


def solution(mesh):
    return jax.shard_map(
        body,
        mesh=mesh,
        in_specs=(P(("row", "col"), None, None, None), P(("row", "col"), None)),
        out_specs=P(("row", "col"), None, None, None),
        check_vma=False,
    )
```

time: 721 us -> 172 us (0.24); the launches traced: 711 us -> 171 us
  waiting for transfers between devices: 265 us -> 57 us
  matrix products: 130 us -> 0 us
  blocking collectives: 152 us -> 32.8 us
  local copies, waits for them, and re-layouts: 99.2 us -> 3.13 us
  other arithmetic: 44.7 us -> 1.63 us
  Pallas kernels: 0 us -> 40.6 us
  starting transfers between devices: 0.2 us -> 22.6 us
    all_gather x6 -> x1, waiting for transfers between devices: 262 us -> 56.9 us  [body(): near = lax.all_gather(near_part, 'col', axis=0)]
    dot_general x17 -> x0, matrix products: 130 us -> none  [the longest x3 45.5 us: assemble(): jnp.einsum('uts,utxy->suxy', matches, member_cols, precision=highest)]
    psum x3 -> x0, blocking collectives: 125 us -> none  [purify(): low_trace, high_trace = lax.psum((low_local, high_local), ('row', 'col'))]
    dot_general x3 -> x0, local copies, waits for them, and re-layouts: 51.2 us -> none  [assemble(): jnp.einsum('uts,utxy->suxy', matches, member_cols, precision=highest)]
    pallas_call x0 -> x9, Pallas kernels: none -> 40.6 us  [call(): pl.pallas_call(kernel, out_shape=[jax.ShapeDtypeStruct(s, d) for s, d in...]
    add x3 -> x0, other arithmetic: 33.9 us -> none  [assemble(): upper_part + jnp.transpose(upper_part, (1, 0, 3, 2)) * off_diagonal]
    add x3 -> x0, local copies, waits for them, and re-layouts: 29 us -> none  [assemble(): upper_part + jnp.transpose(upper_part, (1, 0, 3, 2)) * off_diagonal]
    ppermute x0 -> x14, starting transfers between devices: none -> 22.6 us  [spread(): lax.ppermute(x, 'col', [(i, i ^ k) for i in range(nq)])]
  transfers between devices with their start and end apart: 6 -> 15, of which waited for: 5 -> 1; matrix products, arithmetic and copies ran while one was open for 4% -> 0% of each run, Pallas kernels for 0% -> 15%
where the time goes in v1:
time: 172 us; the launch traced here: 171 us
  waiting for transfers between devices  57 us (33%)
  Pallas kernels  40.6 us (24%)
  blocking collectives  32.8 us (19%)
  starting transfers between devices  22.6 us (13%)
  between operations  13.6 us (8%)
  local copies, waits for them, and re-layouts  3.13 us (2%)
    all_gather x1, waiting for transfers between devices, body(): near = lax.all_gather(near_part, 'col', axis=0)  56.9 us
    pallas_call x9, Pallas kernels, call(): pl.pallas_call(kernel, out_shape=[jax.ShapeDtypeStruct(s, d) for s, d in...  40.6 us
    ppermute x14, starting transfers between devices, spread(): lax.ppermute(x, 'col', [(i, i ^ k) for i in range(nq)])  22.6 us
    all_gather x2, blocking collectives, body(): rows = lax.all_gather(tell, 'row', axis=0)  11.8 us
    all_to_all x1, blocking collectives, body(): lax.all_to_all(jnp.broadcast_to(mine[None], (nr * nq, BW)), ('row', 'col'...  10.9 us
    all_gather x1, blocking collectives, body(): row = lax.all_gather(row_part, 'row', axis=0)  10.1 us
  transfers between devices with their start and end apart: 15, of which 1 were waited for; matrix products, arithmetic and copies ran while one was open for 0% of the time, Pallas kernels for 15%

profile of v1, /device:TPU:0, one launch (start us, length us, event | category | flops | bytes accessed | tf_op | source)
XLA Modules:
  0.0 171.3 jit_solution(18365214307106418742)
XLA Ops:
  6.5 0.0 copy-start.1
  6.5 0.0 slice-start
  6.5 0.0 all-gather.6.cloned.1.call-start
  6.5 0.7 convert_element_type.10
  7.3 1.0 slice.32
  8.3 0.8 pad_maximum_fusion
  9.1 0.0 all-gather.6.cloned.1.call-update
  9.2 0.1 pad_add_fusion.ids
  9.2 0.0 copy-done.1
  9.2 0.0 slice-done
  9.3 10.1 %all-gather = f32[1568,128]{1,0:T(8,128)S(1)} all-gather(f32[392,128]{1,0:T(8,128)S(1)} %pad_maximum_fusion.1), channel_id=2, replica_groups=mesh['row'=4,'col'=8] {'row'}, dimensions={0}, use_global_device_ids=true | all-gather | bytes 1003520 | tf_op jit(solution)/shard_map/all_gather | solution.py:440
  19.4 2.0 %shard_map.28 = (f32[4,128,128]{2,1,0:T(8,128)S(1)}, f32[4,128,128]{2,1,0:T(8,128)S(1)}, f32[4,128,128]{2,1,0:T(8,128)S(1)}, f32[4,128,128]{2,1,0:T(8,128)S(1)}, f32[136,128]{1,0:T(8,128)S(1)}) custom-call(s32[2]{0:T(128)S(1)} %pad_add_fusion.ids, s32[4,9]{1,0:T(4,128)S(1)} %bitcast.19, f32[4,392,128]{2,1,0:T(8,128)S(1)} %bitcast.16), custom_call_target="tpu_custom_call" | custom-call | tf_op jit(solution)/shard_map/pallas_call | solution.py:411
  21.4 1.6 collective-permute-start
  23.0 1.6 collective-permute-start.1
  24.6 0.4 collective-permute-start.2
  25.0 2.6 %collective-permute-start.3 = (f32[136,128]{1,0:T(8,128)S(1)}, f32[136,128]{1,0:T(8,128)S(1)}, u32[]{:S(2)}, u32[]{:S(2)}) collective-permute-start(f32[136,128]{1,0:T(8,128)S(1)} %get-tuple-element.44.own_pack.refs_0_), channel_id=1, source_target_pairs={{0,4},{1,5},{2,6},{3,7},{4,0},{5,1},{6,2},{7,3},{8,12},{9,13},{10,... | collective-permute-start | bytes 208904 | tf_op jit(solution)/shard_map/ppermute | solution.py:424
  27.6 1.3 collective-permute-start.4
  28.9 56.9 %all-gather.6.cloned.1.call-done = f32[7232,128]{1,0:T(8,128)} async-done(((f32[904,128]{1,0:T(8,128)}), f32[7232,128]{1,0:T(8,128)}) %all-gather.6.cloned.1.call-update) | async-done | bytes 3702800 | tf_op jit(solution)/shard_map/all_gather | solution.py:441
  85.8 0.0 copy-start
  85.8 2.0 %copy-done = f32[7232,128]{1,0:T(8,128)S(1)} copy-done((f32[7232,128]{1,0:T(8,128)S(1)}, f32[7232,128]{1,0:T(8,128)}, u32[]{:S(2)}) %copy-start) | copy-done | bytes 3702808
  87.8 6.6 %shard_map.29 = (f32[32,128,128]{2,1,0:T(8,128)S(1)}, bf16[1024,1024]{1,0:T(8,128)(2,1)S(1)}, bf16[1024,1024]{1,0:T(8,128)(2,1)S(1)}, f32[8,1024]{1,0:T(8,128)S(...) custom-call(s32[2]{0:T(128)S(1)} %pad_add_fusion.ids, ...), custom_call_target="tpu_custom_call" | custom-call | tf_op jit(solution)/shard_map/pallas_call | solution.py:411
  94.4 0.0 collective-permute-done.refs_1_
  94.4 1.8 %collective-permute-start.5 = (f32[136,128]{1,0:T(8,128)S(1)}, f32[136,128]{1,0:T(8,128)S(1)}, u32[]{:S(2)}, u32[]{:S(2)}) collective-permute-start(f32[136,128]{1,0:T(8,128)S(1)} %get-tuple-element.44.own_pack.refs_0_), channel_id=1, source_target_pairs={{0,6},{1,7},{2,4},{3,5},{4,2},{5,3},{6,0},{7,1},{8,14},{9,15},{10,... | collective-permute-start | bytes 208904 | tf_op jit(solution)/shard_map/ppermute | solution.py:424
  96.2 0.0 collective-permute-done.1.refs_2_
  96.2 2.1 %collective-permute-start.6 = (f32[136,128]{1,0:T(8,128)S(1)}, f32[136,128]{1,0:T(8,128)S(1)}, u32[]{:S(2)}, u32[]{:S(2)}) collective-permute-start(f32[136,128]{1,0:T(8,128)S(1)} %get-tuple-element.44.own_pack.refs_0_), channel_id=1, source_target_pairs={{0,7},{1,6},{2,5},{3,4},{4,3},{5,2},{6,1},{7,0},{8,15},{9,14},{10,... | collective-permute-start | bytes 208904 | tf_op jit(solution)/shard_map/ppermute | solution.py:424
  98.3 6.0 %all-gather.2 = f32[544,128]{1,0:T(8,128)S(1)} all-gather(f32[136,128]{1,0:T(8,128)S(1)} %get-tuple-element.45), channel_id=4, replica_groups=mesh['row'=4,'col'=8] {'row'}, dimensions={0}, use_global_device_ids=true | all-gather | bytes 348160 | tf_op jit(solution)/shard_map/all_gather | solution.py:462
  104.3 0.0 collective-permute-done.2.refs_3_
  104.3 0.0 collective-permute-done.3.refs_4_
  104.3 0.0 collective-permute-done.4.refs_5_
  104.3 0.0 collective-permute-done.5.refs_6_
  104.3 0.0 collective-permute-done.6.refs_7_
  104.3 2.3 %shard_map.30 = (f32[8,128]{1,0:T(8,128)S(1)}, f32[4,128,128]{2,1,0:T(8,128)S(1)}, f32[4,128,128]{2,1,0:T(8,128)S(1)}, f32[4,128,128]{2,1,0:T(8,128)S(1)}, f32[4...) custom-call(s32[2]{0:T(128)S(1)} %pad_add_fusion.ids, s32[4,9]{1,0:T(4,128)S(1)} %bitcast.20, f32[4,136,128]{2,1,0:T(8,128)S(1)} %bitcast.17, ...), custom_call_target="tpu_custom_call" | custom-call | tf_op jit(solution)/shard_map/pallas_call | solution.py:411
  106.6 0.1 collective-permute-start.10
  106.7 3.8 %collective-permute-start.11 = (f32[136,128]{1,0:T(8,128)S(1)}, f32[136,128]{1,0:T(8,128)S(1)}, u32[]{:S(2)}, u32[]{:S(2)}) collective-permute-start(f32[136,128]{1,0:T(8,128)S(1)} %get-tuple-element.51.refs_8_.refs_0_), channel_id=1, source_target_pairs={{0,5},{1,4},{2,7},{3,6},{4,1},{5,0},{6,3},{7,2},{8,13},{9,12},{10,... | collective-permute-start | bytes 208904 | tf_op jit(solution)/shard_map/ppermute | solution.py:424
  110.5 1.8 %collective-permute-start.12 = (f32[136,128]{1,0:T(8,128)S(1)}, f32[136,128]{1,0:T(8,128)S(1)}, u32[]{:S(2)}, u32[]{:S(2)}) collective-permute-start(f32[136,128]{1,0:T(8,128)S(1)} %get-tuple-element.51.refs_8_.refs_0_), channel_id=1, source_target_pairs={{0,6},{1,7},{2,4},{3,5},{4,2},{5,3},{6,0},{7,1},{8,14},{9,15},{10,... | collective-permute-start | bytes 208904 | tf_op jit(solution)/shard_map/ppermute | solution.py:424
  112.3 2.1 %collective-permute-start.13 = (f32[136,128]{1,0:T(8,128)S(1)}, f32[136,128]{1,0:T(8,128)S(1)}, u32[]{:S(2)}, u32[]{:S(2)}) collective-permute-start(f32[136,128]{1,0:T(8,128)S(1)} %get-tuple-element.51.refs_8_.refs_0_), channel_id=1, source_target_pairs={{0,7},{1,6},{2,5},{3,4},{4,3},{5,2},{6,1},{7,0},{8,15},{9,14},{10,... | collective-permute-start | bytes 208904 | tf_op jit(solution)/shard_map/ppermute | solution.py:424
  114.4 1.5 collective-permute-start.7
  115.8 4.4 %shard_map.31 = (f32[32,128,128]{2,1,0:T(8,128)S(1)}, f32[32,128,128]{2,1,0:T(8,128)S(1)}) custom-call(f32[32,128,128]{2,1,0:T(8,128)S(1)} %get-tuple-element.52.m_ref.refs_11_, bf16[1024,1024]{1,0:T(8,128)(2,1)S(1)} %get-tuple-element.53.mh, bf16[1024,1024]{1,0:T(8,128)(2,1)S(1)} %get-tuple-element.54.ml, f32[32,128,128]{2,1,0:T(8,128)S(1)} %get-tuple-element.55.s_ref, ...), custom_call_target="tpu_custom_call" | custom-call | tf_op jit(solution)/shard_map/pallas_call | solution.py:411
  120.2 7.5 %shard_map.32 = (f32[32,128,128]{2,1,0:T(8,128)S(1)}, bf16[1024,1024]{1,0:T(8,128)(2,1)S(1)}, bf16[1024,1024]{1,0:T(8,128)(2,1)S(1)}, f32[32,128,128]{2,1,0:T(8,...) custom-call(s32[2]{0:T(128)S(1)} %pad_add_fusion.ids, ...), custom_call_target="tpu_custom_call" | custom-call | tf_op jit(solution)/shard_map/pallas_call | solution.py:411
  127.7 4.7 %shard_map.34 = (f32[32,128,128]{2,1,0:T(8,128)S(1)}, f32[32,128,128]{2,1,0:T(8,128)S(1)}) custom-call(f32[32,128,128]{2,1,0:T(8,128)S(1)} %get-tuple-element.68.m_ref.refs_11_, bf16[1024,1024]{1,0:T(8,128)(2,1)S(1)} %get-tuple-element.69.mh, bf16[1024,1024]{1,0:T(8,128)(2,1)S(1)} %get-tuple-element.70.ml, f32[32,128,128]{2,1,0:T(8,128)S(1)} %get-tuple-element.71.s_ref, ...), custom_call_target="tpu_custom_call" | custom-call | tf_op jit(solution)/shard_map/pallas_call | solution.py:411
  132.4 0.0 collective-permute-done.10.refs_4_
  132.4 0.1 collective-permute-start.8
  132.5 0.0 collective-permute-done.11.refs_5_
  132.5 2.0 %collective-permute-start.9 = (f32[136,128]{1,0:T(8,128)S(1)}, f32[136,128]{1,0:T(8,128)S(1)}, u32[]{:S(2)}, u32[]{:S(2)}) collective-permute-start(f32[136,128]{1,0:T(8,128)S(1)} %get-tuple-element.51.refs_8_.refs_0_), channel_id=1, source_target_pairs={{0,3},{1,2},{2,1},{3,0},{4,7},{5,6},{6,5},{7,4},{8,11},{9,10},{10,... | collective-permute-start | bytes 208904 | tf_op jit(solution)/shard_map/ppermute | solution.py:424
  134.5 5.8 %all-gather.3 = f32[544,128]{1,0:T(8,128)S(1)} all-gather(f32[136,128]{1,0:T(8,128)S(1)} %get-tuple-element.61), channel_id=5, replica_groups=mesh['row'=4,'col'=8] {'row'}, dimensions={0}, use_global_device_ids=true | all-gather | bytes 348160 | tf_op jit(solution)/shard_map/all_gather | solution.py:462
  140.3 0.0 collective-permute-done.12.refs_6_
  140.3 0.0 collective-permute-done.13.refs_7_
  140.3 0.0 collective-permute-done.7.refs_1_
  140.3 0.0 collective-permute-done.8.refs_2_
  140.3 0.0 collective-permute-done.9.refs_3_
  140.4 2.3 %shard_map.33 = (f32[8,128]{1,0:T(8,128)S(1)}, f32[4,128,128]{2,1,0:T(8,128)S(1)}, f32[4,128,128]{2,1,0:T(8,128)S(1)}, f32[4,128,128]{2,1,0:T(8,128)S(1)}, f32[4...) custom-call(s32[2]{0:T(128)S(1)} %pad_add_fusion.ids, s32[4,9]{1,0:T(4,128)S(1)} %bitcast.21, f32[4,136,128]{2,1,0:T(8,128)S(1)} %bitcast.18, ...), custom_call_target="tpu_custom_call" | custom-call | tf_op jit(solution)/shard_map/pallas_call | solution.py:411
  142.7 9.3 %shard_map.35 = (f32[9,128,128]{2,1,0:T(8,128)S(1)}, f32[9,128,128]{2,1,0:T(8,128)S(1)}, f32[8,128]{1,0:T(8,128)S(1)}) custom-call(s32[2]{0:T(128)S(1)} %pad_add_fusion.ids, s32[4,9]{1,0:T(4,128)S(1)} %bitcast.22, f32[8,128]{1,0:T(8,128)S(1)} %get-tuple-element.66.coef, f32[136,128]{1,0:T(8,128)S(1)} %get-tuple-element.51.refs_8_.refs_0_, ...), custom_call_target="tpu_custom_call" | custom-call | tf_op jit(solution)/shard_map/pallas_call | solution.py:411
  152.0 10.9 %all_to_all.8 = f32[32,1,128]{2,1,0:T(1,128)S(1)} all-to-all(f32[32,1,128]{2,1,0:T(1,128)S(1)} %broadcast_in_dim.2), channel_id=1, replica_groups=mesh['row'=4,'col'=8] {'row','col'}, dimensions={0} | all-to-all | bytes 32768 | tf_op jit(solution)/shard_map/all_to_all | solution.py:505
  162.9 1.6 shard_map.36
  (6 shorter events, 0.1 us)
Async XLA Ops:
  6.5 2.7 %copy-start.1 = (f32[1,9,128,128]{3,2,1,0:T(8,128)S(1)}, f32[1,9,128,128]{3,2,1,0:T(8,128)}, u32[]{:S(2)}) copy-start(f32[1,9,128,128]{3,2,1,0:T(8,128)} %param.2) | copy-start | bytes 1769476
  6.5 2.7 %slice-start = ((f32[1,9,128,128]{3,2,1,0:T(8,128)}), f32[1,2,128,128]{3,2,1,0:T(8,128)S(1)}, s32[]{:S(2)}) async-start(f32[1,9,128,128]{3,2,1,0:T(8,128)} %param.2), calls=%async_computation.2 | async-start | bytes 262144 | tf_op jit(solution)/shard_map/slice | solution.py:438
  6.5 79.2 %all-gather.6.cloned.1.call-start = ((), (), s32[]{:S(2)}) async-start(), calls=%async_computation.1 | async-start | bytes 4165632 | tf_op jit(solution)/shard_map/all_gather | solution.py:441
  21.4 73.0 %collective-permute-start = (f32[136,128]{1,0:T(8,128)S(1)}, f32[136,128]{1,0:T(8,128)S(1)}, u32[]{:S(2)}, u32[]{:S(2)}) collective-permute-start(f32[136,128]{1,0:T(8,128)S(1)} %get-tuple-element.44.own_pack.refs_0_), channel_id=1, source_target_pairs={{0,1},{1,0},{2,3},{3,2},{4,5},{5,4},{6,7},{7,6},{8,9},{9,8},{10,11... | collective-permute-start | bytes 208904 | tf_op jit(solution)/shard_map/ppermute | solution.py:424
  23.0 73.2 %collective-permute-start.1 = (f32[136,128]{1,0:T(8,128)S(1)}, f32[136,128]{1,0:T(8,128)S(1)}, u32[]{:S(2)}, u32[]{:S(2)}) collective-permute-start(f32[136,128]{1,0:T(8,128)S(1)} %get-tuple-element.44.own_pack.refs_0_), channel_id=1, source_target_pairs={{0,2},{1,3},{2,0},{3,1},{4,6},{5,7},{6,4},{7,5},{8,10},{9,11},{10,... | collective-permute-start | bytes 208904 | tf_op jit(solution)/shard_map/ppermute | solution.py:424
  24.6 79.7 %collective-permute-start.2 = (f32[136,128]{1,0:T(8,128)S(1)}, f32[136,128]{1,0:T(8,128)S(1)}, u32[]{:S(2)}, u32[]{:S(2)}) collective-permute-start(f32[136,128]{1,0:T(8,128)S(1)} %get-tuple-element.44.own_pack.refs_0_), channel_id=1, source_target_pairs={{0,3},{1,2},{2,1},{3,0},{4,7},{5,6},{6,5},{7,4},{8,11},{9,10},{10,... | collective-permute-start | bytes 208904 | tf_op jit(solution)/shard_map/ppermute | solution.py:424
  25.0 79.3 %collective-permute-start.3 = (f32[136,128]{1,0:T(8,128)S(1)}, f32[136,128]{1,0:T(8,128)S(1)}, u32[]{:S(2)}, u32[]{:S(2)}) collective-permute-start(f32[136,128]{1,0:T(8,128)S(1)} %get-tuple-element.44.own_pack.refs_0_), channel_id=1, source_target_pairs={{0,4},{1,5},{2,6},{3,7},{4,0},{5,1},{6,2},{7,3},{8,12},{9,13},{10,... | collective-permute-start | bytes 208904 | tf_op jit(solution)/shard_map/ppermute | solution.py:424
  27.6 76.7 %collective-permute-start.4 = (f32[136,128]{1,0:T(8,128)S(1)}, f32[136,128]{1,0:T(8,128)S(1)}, u32[]{:S(2)}, u32[]{:S(2)}) collective-permute-start(f32[136,128]{1,0:T(8,128)S(1)} %get-tuple-element.44.own_pack.refs_0_), channel_id=1, source_target_pairs={{0,5},{1,4},{2,7},{3,6},{4,1},{5,0},{6,3},{7,2},{8,13},{9,12},{10,... | collective-permute-start | bytes 208904 | tf_op jit(solution)/shard_map/ppermute | solution.py:424
  85.8 2.0 %copy-start = (f32[7232,128]{1,0:T(8,128)S(1)}, f32[7232,128]{1,0:T(8,128)}, u32[]{:S(2)}) copy-start(f32[7232,128]{1,0:T(8,128)} %all-gather.6.cloned.1.call-done) | copy-start | bytes 11108356
  94.4 9.9 %collective-permute-start.5 = (f32[136,128]{1,0:T(8,128)S(1)}, f32[136,128]{1,0:T(8,128)S(1)}, u32[]{:S(2)}, u32[]{:S(2)}) collective-permute-start(f32[136,128]{1,0:T(8,128)S(1)} %get-tuple-element.44.own_pack.refs_0_), channel_id=1, source_target_pairs={{0,6},{1,7},{2,4},{3,5},{4,2},{5,3},{6,0},{7,1},{8,14},{9,15},{10,... | collective-permute-start | bytes 208904 | tf_op jit(solution)/shard_map/ppermute | solution.py:424
  96.2 8.1 %collective-permute-start.6 = (f32[136,128]{1,0:T(8,128)S(1)}, f32[136,128]{1,0:T(8,128)S(1)}, u32[]{:S(2)}, u32[]{:S(2)}) collective-permute-start(f32[136,128]{1,0:T(8,128)S(1)} %get-tuple-element.44.own_pack.refs_0_), channel_id=1, source_target_pairs={{0,7},{1,6},{2,5},{3,4},{4,3},{5,2},{6,1},{7,0},{8,15},{9,14},{10,... | collective-permute-start | bytes 208904 | tf_op jit(solution)/shard_map/ppermute | solution.py:424
  106.6 25.8 %collective-permute-start.10 = (f32[136,128]{1,0:T(8,128)S(1)}, f32[136,128]{1,0:T(8,128)S(1)}, u32[]{:S(2)}, u32[]{:S(2)}) collective-permute-start(f32[136,128]{1,0:T(8,128)S(1)} %get-tuple-element.51.refs_8_.refs_0_), channel_id=1, source_target_pairs={{0,4},{1,5},{2,6},{3,7},{4,0},{5,1},{6,2},{7,3},{8,12},{9,13},{10,... | collective-permute-start | bytes 208904 | tf_op jit(solution)/shard_map/ppermute | solution.py:424
  106.7 25.8 %collective-permute-start.11 = (f32[136,128]{1,0:T(8,128)S(1)}, f32[136,128]{1,0:T(8,128)S(1)}, u32[]{:S(2)}, u32[]{:S(2)}) collective-permute-start(f32[136,128]{1,0:T(8,128)S(1)} %get-tuple-element.51.refs_8_.refs_0_), channel_id=1, source_target_pairs={{0,5},{1,4},{2,7},{3,6},{4,1},{5,0},{6,3},{7,2},{8,13},{9,12},{10,... | collective-permute-start | bytes 208904 | tf_op jit(solution)/shard_map/ppermute | solution.py:424
  110.5 29.8 %collective-permute-start.12 = (f32[136,128]{1,0:T(8,128)S(1)}, f32[136,128]{1,0:T(8,128)S(1)}, u32[]{:S(2)}, u32[]{:S(2)}) collective-permute-start(f32[136,128]{1,0:T(8,128)S(1)} %get-tuple-element.51.refs_8_.refs_0_), channel_id=1, source_target_pairs={{0,6},{1,7},{2,4},{3,5},{4,2},{5,3},{6,0},{7,1},{8,14},{9,15},{10,... | collective-permute-start | bytes 208904 | tf_op jit(solution)/shard_map/ppermute | solution.py:424
  112.3 28.0 %collective-permute-start.13 = (f32[136,128]{1,0:T(8,128)S(1)}, f32[136,128]{1,0:T(8,128)S(1)}, u32[]{:S(2)}, u32[]{:S(2)}) collective-permute-start(f32[136,128]{1,0:T(8,128)S(1)} %get-tuple-element.51.refs_8_.refs_0_), channel_id=1, source_target_pairs={{0,7},{1,6},{2,5},{3,4},{4,3},{5,2},{6,1},{7,0},{8,15},{9,14},{10,... | collective-permute-start | bytes 208904 | tf_op jit(solution)/shard_map/ppermute | solution.py:424
  114.4 26.0 %collective-permute-start.7 = (f32[136,128]{1,0:T(8,128)S(1)}, f32[136,128]{1,0:T(8,128)S(1)}, u32[]{:S(2)}, u32[]{:S(2)}) collective-permute-start(f32[136,128]{1,0:T(8,128)S(1)} %get-tuple-element.51.refs_8_.refs_0_), channel_id=1, source_target_pairs={{0,1},{1,0},{2,3},{3,2},{4,5},{5,4},{6,7},{7,6},{8,9},{9,8},{10,11... | collective-permute-start | bytes 208904 | tf_op jit(solution)/shard_map/ppermute | solution.py:424
  132.4 7.9 %collective-permute-start.8 = (f32[136,128]{1,0:T(8,128)S(1)}, f32[136,128]{1,0:T(8,128)S(1)}, u32[]{:S(2)}, u32[]{:S(2)}) collective-permute-start(f32[136,128]{1,0:T(8,128)S(1)} %get-tuple-element.51.refs_8_.refs_0_), channel_id=1, source_target_pairs={{0,2},{1,3},{2,0},{3,1},{4,6},{5,7},{6,4},{7,5},{8,10},{9,11},{10,... | collective-permute-start | bytes 208904 | tf_op jit(solution)/shard_map/ppermute | solution.py:424
  132.5 7.8 %collective-permute-start.9 = (f32[136,128]{1,0:T(8,128)S(1)}, f32[136,128]{1,0:T(8,128)S(1)}, u32[]{:S(2)}, u32[]{:S(2)}) collective-permute-start(f32[136,128]{1,0:T(8,128)S(1)} %get-tuple-element.51.refs_8_.refs_0_), channel_id=1, source_target_pairs={{0,3},{1,2},{2,1},{3,0},{4,7},{5,6},{6,5},{7,4},{8,11},{9,10},{10,... | collective-permute-start | bytes 208904 | tf_op jit(solution)/shard_map/ppermute | solution.py:424
Sparse Core Ops, SparseCore 0:
  9.5 76.1 all-gather.5

commit v2 on v1

--- a/solution.py
+++ b/solution.py
@@ -67,6 +67,28 @@
     return out
 
 
+SHARE = 4
+
+
+@functools.lru_cache
+def shares(nq):
+    stored = []
+    for b in range(nq):
+        slots = [t for t, d in enumerate(offsets(b, nq)) if (b + d) % nq <= b]
+        stored.append(slots)
+    keep = [slots[:SHARE] for slots in stored]
+    give = [slots[SHARE:] for slots in stored]
+    donors = sorted((b for b in range(nq) if give[b]), key=lambda b: (-len(give[b]), -b))
+    takers = sorted((b for b in range(nq) if len(keep[b]) < SHARE), key=lambda b: len(keep[b]))
+    moves = list(zip(donors, takers))
+    pair = lambda b, t: ((b + offsets(b, nq)[t]) % nq, b)
+    held = [[pair(b, t) for t in keep[b]] for b in range(nq)]
+    for donor, taker in moves:
+        held[taker] += [pair(donor, t) for t in give[donor]]
+    assert len(donors) == len(takers) and all(len(h) == SHARE for h in held)
+    return keep, give, moves, held
+
+
 def split(x):
     hi = x.astype(bf16)
     return hi, (x - hi.astype(f32)).astype(bf16)
@@ -116,6 +138,18 @@
 
 def cut(q):
     return slice(q * BW, (q + 1) * BW)
+
+
+def settle(nq, q, parts, held, rows=slice(None)):
+    if len(parts) == 1:
+        for k in range(nq):
+            held[k] = parts[0][k, rows, :]
+        return
+    half = nq // 2
+    for k in range(half):
+        for side in range(2):
+            source = lax.rem((q ^ side) + (nq - 2 * k), jnp.int32(nq))
+            held[source] = parts[half * side + k][rows, :]
 
 
 def put_dense(hi_ref, lo_ref, a, b, block):
@@ -192,17 +226,62 @@
     out_ref[BW + 4 : BW + 8, :] = jnp.zeros((4, BW), f32)
 
 
-def first_kernel(nq, ids, near, own_pack, m_ref, mh, ml, link, s_ref, sh, sl, out_ref):
+def choose(q, values):
+    out = jnp.int32(values[0])
+    for i, v in enumerate(values[1:], 1):
+        if v != values[0]:
+            out = jnp.where(q == i, jnp.int32(v), out)
+    return out
+
+
+def prepare_kernel(nq, width, ids, names, blocks, near, extra, row):
     q = ids[1]
+    keep, give, _, _ = shares(nq)
+    lane = lax.broadcasted_iota(jnp.int32, (1, BW), 1)
+    listed = jnp.zeros((1, BW), f32)
+    for t in range(names.shape[1]):
+        listed = jnp.where(lane == t, names[0, t].astype(f32), listed)
+    listed = jnp.broadcast_to(listed, (8, BW))
+    for i in range(SHARE):
+        near[cut(i), :] = blocks[choose(q, [k[min(i, len(k) - 1)] for k in keep])]
+    near[SHARE * BW :, :] = listed
+    for i in range(width):
+        extra[cut(i), :] = blocks[choose(q, [(g + [0] * width)[i] for g in give])]
+    for i, t in enumerate((0, NEAR, NEAR + 1)):
+        row[cut(i), :] = blocks[t]
+    row[3 * BW :, :] = listed
+
+
+def share_kernel(nq, width, ids, near, moved, own_pack, out):
+    q = ids[1]
+    count = choose(q, [len(k) for k in shares(nq)[0]])
+    out[0 : SHARE * BW + 8, :] = near[...]
+    out[SHARE * BW + 8 :, :] = own_pack[...]
+    for i in range(1, SHARE):
+
+        @pl.when(i >= count)
+        def _():
+            out[cut(i), :] = moved[pl.ds(pl.multiple_of((i - count) * BW, BW), BW), :]
+
+
+def first_kernel(nq, ids, *refs):
+    parts, refs = refs[:nq], refs[nq:]
+    own_pack, m_ref, mh, ml, link, s_ref, sh, sl, out_ref, packs, near = refs
+    q = ids[1]
+    settle(nq, q, parts, near)
+    for b in range(nq):
+        packs[b] = near[b, SHARE * BW + 8 :, :]
     clear_unlinked(mh, ml, nq)
     link[...] = jnp.zeros_like(link)
-    for (a, b), place in pair_index(nq).items():
-        t = slot_of(a, b, nq)
-        block = near[b, cut(t), :]
-        m_ref[place] = block
-        put_dense(mh, ml, a, b, block)
+    index = pair_index(nq)
+    for b, pairs in enumerate(shares(nq)[3]):
+        for i, pair in enumerate(pairs):
+            block = near[b, cut(i), :]
+            m_ref[index[pair]] = block
+            put_dense(mh, ml, *pair, block)
     for a in range(nq):
-        present = jnp.where(near[a, NEAR * BW : NEAR * BW + 1, :] >= 0.0, 1.0, 0.0)
+        listed = near[a, SHARE * BW : SHARE * BW + 1, :]
+        present = jnp.where(listed >= 0.0, 1.0, 0.0)
         for t, d in enumerate(offsets(a, nq)):
             b = (a + d) % nq
             link[a : a + 1, cut(b)] = jnp.broadcast_to(present[:, t : t + 1], (1, BW))
@@ -213,8 +292,7 @@
     index = pair_index(nq)
     c = coef[0:1, :]
     inv = coef[1:2, :]
-    for k in range(nq):
-        held[k ^ q] = packs[k][...]
+    settle(nq, q, packs, held)
     clear_unlinked(mh, ml, nq)
     for b in range(nq):
         g, e = unpack_pair(held[b, 0:BW, :], held[b, BW : BW + 1, :])
@@ -233,8 +311,8 @@
             put_dense(mh, ml, a, b, block)
 
 
-def next_kernel(nq, ids, coef, *refs):
-    packs, own_pack, refs = refs[:nq], refs[nq], refs[nq + 1 :]
+def next_kernel(nq, count, ids, coef, *refs):
+    packs, own_pack, refs = refs[:count], refs[count], refs[count + 1 :]
     x_ref, y_ref, m_old, link, m_ref, mh, ml, s_ref, sh, sl, out_ref, held = refs
     q = ids[1]
     assemble(nq, q, coef, packs, x_ref, y_ref, m_old, held, m_ref, mh, ml)
@@ -252,8 +330,12 @@
         y_ref[place] = s - 2.0 * m
 
 
-def edge_ends(lists, nq, e):
-    far = lax.div(lists[e, 8], jnp.int32(nq))
+def far_row(lists, r, nq, e, slot):
+    return lax.div(lists[e ^ r, slot], jnp.int32(nq))
+
+
+def edge_ends(lists, r, nq, e):
+    far = far_row(lists, r, nq, e, 8)
     return jnp.minimum(far, e), jnp.maximum(far, e)
 
 
@@ -262,7 +344,7 @@
     norm = jnp.zeros((BW, BW), f32)
     inner = jnp.zeros((BW, BW), f32)
     for e in range(nr):
-        lo, hi = edge_ends(lists, nq, e)
+        lo, hi = edge_ends(lists, r, nq, e)
         u = u_ref[e]
         uh, ul = split(u)
         dlo = split(d_ref[lo])
@@ -274,7 +356,7 @@
     g_sum = jnp.zeros((BW, BW), f32)
     e_sum = jnp.zeros((BW, BW), f32)
     for slot in (7, 8):
-        far = lax.div(lists[r, slot], jnp.int32(nq))
+        far = far_row(lists, r, nq, r, slot)
         u = u_ref[r if slot == 8 else far]
         flipped = u.T
         mine = r > far
@@ -289,11 +371,16 @@
     pack_ref[BW + 3 : BW + 8, :] = jnp.zeros((5, BW), f32)
 
 
-def cross_first_kernel(nr, nq, ids, lists, row, d_ref, u_ref, su_ref, v_ref, pack_ref):
+def cross_first_kernel(nr, nq, ids, lists, *refs):
+    parts, refs = refs[:nr], refs[nr:]
+    d_ref, u_ref, su_ref, v_ref, pack_ref, row = refs
+    r = ids[0]
+    for k in range(nr):
+        row[k ^ r] = parts[k][...]
     for e in range(nr):
         d_ref[e] = row[e, cut(0), :]
     for e in range(nr):
-        far = lax.div(lists[e, 8], jnp.int32(nq))
+        far = far_row(lists, r, nq, e, 8)
         here = row[e, cut(2), :]
         there = row[far, cut(1), :]
         u_ref[e] = jnp.where(far < e, here, there)
@@ -301,8 +388,7 @@
 
 
 def coefficient(nr, nq, q, rows, packs, held):
-    for k in range(nq):
-        held[k ^ q] = packs[k][BW : BW + 8, :]
+    settle(nq, q, packs, held, slice(BW, BW + 8))
     trace = rows[0, BW + 1 : BW + 2, :]
     norm = rows[0, BW + 2 : BW + 3, :]
     inner = rows[0, BW + 3 : BW + 4, :]
@@ -317,19 +403,22 @@
     return c, 1.0 / (1.0 - c)
 
 
-def cross_kernel(nr, nq, ids, lists, rows, *refs):
-    packs, refs = refs[:nq], refs[nq:]
-    d_old, u_old, su_old, v_old, coef, d_ref, u_ref, su_ref, v_ref, pack_ref, held = refs
+def cross_kernel(nr, nq, count, ids, lists, *refs):
+    parts, packs, refs = refs[:nr], refs[nr : nr + count], refs[nr + count :]
+    d_old, u_old, su_old, v_old, coef, d_ref, u_ref, su_ref, v_ref, pack_ref, held, rows = refs
+    r = ids[0]
+    for k in range(nr):
+        rows[k ^ r] = parts[k][...]
     c, inv = coefficient(nr, nq, ids[1], rows, packs, held)
     coef[0:1, :] = c
     coef[1:2, :] = inv
     coef[2:8, :] = jnp.zeros((6, BW), f32)
-    for r in range(nr):
-        s0, k0 = unpack_pair(rows[r, 0:BW, :], rows[r, BW : BW + 1, :])
-        d = d_old[r]
-        d_ref[r] = ((1.0 - 2.0 * c) * d + (1.0 + c) * s0 - k0) * inv
+    for p in range(nr):
+        s0, k0 = unpack_pair(rows[p, 0:BW, :], rows[p, BW : BW + 1, :])
+        d = d_old[p]
+        d_ref[p] = ((1.0 - 2.0 * c) * d + (1.0 + c) * s0 - k0) * inv
     for e in range(nr):
-        lo, hi = edge_ends(lists, nq, e)
+        lo, hi = edge_ends(lists, r, nq, e)
         s0, _ = unpack_pair(rows[hi, 0:BW, :], rows[hi, BW : BW + 1, :])
         u, su = u_old[e], su_old[e]
         k = dotf(u, s0) + v_old[e]
@@ -337,8 +426,8 @@
     cross_tail(nr, nq, ids, lists, d_ref, u_ref, su_ref, v_ref, pack_ref)
 
 
-def last_kernel(nr, nq, ids, lists, coef, *refs):
-    packs, refs = refs[:nq], refs[nq:]
+def last_kernel(nr, nq, count, ids, lists, coef, *refs):
+    packs, refs = refs[:count], refs[count:]
     own_pack, x_old, y_old, m_old, link, d_ref, u_ref, su_ref, v_ref = refs[:9]
     x_out, y_out, sums, held, m_ref, mh, ml, col, sq, sqh, sql = refs[9:]
     r, q = ids[0], ids[1]
@@ -373,7 +462,7 @@
         y_out[t] = s - 2.0 * m
     sh, sl = split(s0)
     for t in (7, 8):
-        far = lax.div(lists[r, t], jnp.int32(nq))
+        far = far_row(lists, r, nq, r, t)
         edge = r if t == 8 else far
         u, su = u_ref[edge], su_ref[edge]
         k = dot3(*split(u), sh, sl) + v_ref[edge]
@@ -388,10 +477,9 @@
     high = jnp.broadcast_to(sums[:, half : half + 1], (1, BW))
     c = high / low
     inv = 1.0 / (1.0 - c)
-    r = ids[0]
-    own = lists[r, 0]
+    own = lists[0, 0]
     for t in range(slots):
-        a = lists[r, t]
+        a = lists[0, t]
         keep = jnp.logical_and(a >= 0, a <= own)
         out_ref[0, t] = jnp.where(keep, (x_ref[t] + c * y_ref[t]) * inv, 0.0)
 
@@ -419,10 +507,30 @@
     )(*args)
 
 
-def spread(x, nq):
+def spread(x, axis, size):
     return [x] + [
-        lax.ppermute(x, "col", [(i, i ^ k) for i in range(nq)]) for k in range(1, nq)
+        lax.ppermute(x, axis, [(i, i ^ k) for i in range(size)]) for k in range(1, size)
     ]
+
+
+def gather_near(near, extra, own_pack, ids, width, nq):
+    moved = lax.ppermute(extra, "col", shares(nq)[2])
+    (own,) = call(
+        functools.partial(share_kernel, nq, width),
+        [((near.shape[0] + PACK, BW), f32)],
+        (ids, near, moved, own_pack),
+        1,
+    )
+    return gather(own, nq)
+
+
+def gather(x, nq):
+    here = [x] + [
+        lax.ppermute(x, "col", [(i, (i + 2 * k) % nq) for i in range(nq)])
+        for k in range(1, nq // 2)
+    ]
+    there = [lax.ppermute(y, "col", [(i, i ^ 1) for i in range(nq)]) for y in here]
+    return here + there
 
 
 def body(upper_blocks, members):
@@ -433,14 +541,18 @@
     npair = len(pattern(nq))
     ids = jnp.stack([lax.axis_index("row"), lax.axis_index("col")]).astype(jnp.int32)
 
-    flat = blocks.reshape(slots * BW, BW)
-    names = jnp.pad(members.astype(f32), ((0, 7), (0, BW - slots)))
-    row_part = jnp.concatenate([flat[:BW], flat[NEAR * BW :], names])
-    near_part = jnp.concatenate([flat[: NEAR * BW], names])
-    row = lax.all_gather(row_part, "row", axis=0)
-    near = lax.all_gather(near_part, "col", axis=0)
-    lists = row[:, 3 * BW, :slots].astype(jnp.int32)
-
+    width = max(len(g) for g in shares(nq)[1])
+    share = (SHARE * BW + 8, BW)
+    near, extra, row_part = call(
+        functools.partial(prepare_kernel, nq, width),
+        [(share, f32), ((width * BW, BW), f32), ((3 * BW + 8, BW), f32)],
+        (ids, members, blocks),
+        2,
+    )
+    row = spread(row_part, "row", nr)
+    lists = jnp.concatenate([x[3 * BW : 3 * BW + 1, :slots] for x in row]).astype(jnp.int32)
+
+    square_flops = 6 * order**3
     listed = (npair, BW, BW)
     dense = (order, order)
     edges = (nr, BW, BW)
@@ -449,43 +561,52 @@
     square_outs = [(listed, f32), (dense, bf16), (dense, bf16), (pack, f32)]
 
     d, u, su, v, own = call(
-        functools.partial(cross_first_kernel, nr, nq), cross_outs, (ids, lists, row), 2
-    )
-    packs = spread(own, nq)
-    m, mh, ml, link, s, sh, sl, tell = call(
+        functools.partial(cross_first_kernel, nr, nq), cross_outs, (ids, lists, *row), 2,
+        [pltpu.VMEM((nr, 3 * BW + 8, BW), f32)],
+    )
+    nears = gather_near(near, extra, own, ids, width, nq)
+    m, mh, ml, link, s, sh, sl, tell, packs = call(
         functools.partial(first_kernel, nq),
-        [(listed, f32), (dense, bf16), (dense, bf16), ((nq, order), f32)] + square_outs,
-        (ids, near, own),
+        [(listed, f32), (dense, bf16), (dense, bf16), ((nq, order), f32)]
+        + square_outs
+        + [((nq,) + pack, f32)],
+        (ids, *nears, own),
         1,
-    )
+        [pltpu.VMEM((nq,) + nears[0].shape, f32)],
+        flops=square_flops,
+    )
+    packs = [packs]
     for step in range(PURIFY - 1):
-        rows = lax.all_gather(tell, "row", axis=0)
+        rows = spread(tell, "row", nr)
         x, y = call(
             functools.partial(cube_kernel, nq),
             [(listed, f32)] * 2,
             (m, mh, ml, s, sh, sl, link),
             0,
+            flops=square_flops,
         )
         coef, d, u, su, v, own = call(
-            functools.partial(cross_kernel, nr, nq),
+            functools.partial(cross_kernel, nr, nq, len(packs)),
             [((8, BW), f32)] + cross_outs,
-            (ids, lists, rows, *packs, d, u, su, v),
+            (ids, lists, *rows, *packs, d, u, su, v),
             2,
-            [pltpu.VMEM((nq, 8, BW), f32)],
+            [pltpu.VMEM((nq, 8, BW), f32), pltpu.VMEM((nr, PACK, BW), f32)],
+            flops=square_flops // 4,
         )
         old = packs
         if step < PURIFY - 2:
-            packs = spread(own, nq)
+            packs = gather(own, nq)
             m, mh, ml, s, sh, sl, tell = call(
-                functools.partial(next_kernel, nq),
+                functools.partial(next_kernel, nq, len(old)),
                 [(listed, f32), (dense, bf16), (dense, bf16)] + square_outs,
                 (ids, coef, *old, own, x, y, m, link),
                 1,
                 [pltpu.VMEM((nq, PACK, BW), f32)],
+                flops=square_flops,
             )
     strip = (order, BW)
     xo, yo, sums = call(
-        functools.partial(last_kernel, nr, nq),
+        functools.partial(last_kernel, nr, nq, len(old)),
         [((slots, BW, BW), f32)] * 2 + [((8, BW), f32)],
         (ids, lists, coef, *old, own, x, y, m, link, d, u, su, v),
         2,

time: 172 us -> 127 us (0.74)
  blocking collectives: 32.8 us -> 10.1 us
  between operations: 13.6 us -> 0.21 us
  waiting for transfers between devices: 57 us -> 45 us
  starting transfers between devices: 22.6 us -> 27.4 us
    all_gather x1 -> x0, waiting for transfers between devices: 56.9 us -> none  [body(): near = lax.all_gather(near_part, 'col', axis=0)]
    ppermute x14 -> x24, waiting for transfers between devices: 0.04 us -> 45 us  [the longest x6 28.1 us: gather(): lax.ppermute(x, 'col', [(i, (i + 2 * k) % nq) for i in range(nq)])]
    all_gather x3 -> x0, blocking collectives: 21.9 us -> none  [the longest x2 11.8 us: body(): rows = lax.all_gather(tell, 'row', axis=0)]
    ppermute x14 -> x24, starting transfers between devices: 22.6 us -> 27.4 us  [the longest x6 12.6 us: gather(): lax.ppermute(x, 'col', [(i, (i + 2 * k) % nq) for i in range(nq)])]
    pallas_call x9 -> x11, Pallas kernels: 40.6 us -> 42.3 us  [call(): pl.pallas_call(kernel, out_shape=[jax.ShapeDtypeStruct(s, d) for s, d in...]
  transfers between devices with their start and end apart: 15 -> 24, of which waited for: 1 -> 7; matrix products, arithmetic and copies ran while one was open for 0% -> 0% of each run, Pallas kernels for 15% -> 9%
where the time goes in v2:
time: 127 us
  waiting for transfers between devices  45 us (35%)
  Pallas kernels  42.3 us (33%)
  starting transfers between devices  27.4 us (22%)
  blocking collectives  10.1 us (8%)
  local copies, waits for them, and re-layouts  1.74 us (1%)
    pallas_call x11, Pallas kernels, call(): pl.pallas_call(kernel, out_shape=[jax.ShapeDtypeStruct(s, d) for s, d in...  42.3 us
    ppermute x6, waiting for transfers between devices, gather(): lax.ppermute(x, 'col', [(i, (i + 2 * k) % nq) for i in range(nq)])  28.1 us
    ppermute x6, starting transfers between devices, gather(): lax.ppermute(x, 'col', [(i, (i + 2 * k) % nq) for i in range(nq)])  12.6 us
    all_to_all x1, blocking collectives, body(): lax.all_to_all(jnp.broadcast_to(mine[None], (nr * nq, BW)), ('row', 'col'...  10.1 us
    ppermute x8, waiting for transfers between devices, gather(): lax.ppermute(y, 'col', [(i, i ^ 1) for i in range(nq)])  8.62 us
    ppermute x9, waiting for transfers between devices, spread(): lax.ppermute(x, axis, [(i, i ^ k) for i in range(size)])  8.25 us
    ppermute x8, starting transfers between devices, gather(): lax.ppermute(y, 'col', [(i, i ^ 1) for i in range(nq)])  6.91 us
    ppermute x9, starting transfers between devices, spread(): lax.ppermute(x, axis, [(i, i ^ k) for i in range(size)])  6.6 us
  transfers between devices with their start and end apart: 24, of which 7 were waited for; matrix products, arithmetic and copies ran while one was open for 0% of the time, Pallas kernels for 9%

profile of v2, /device:TPU:0, one launch (start us, length us, event | category | flops | bytes accessed | tf_op | source)
XLA Modules:
  0.0 126.8 jit_solution(17209516262394489021)
XLA Ops:
  0.0 0.1 pad_add_fusion.ids
  0.1 0.0 copy-start
  0.1 1.1 copy-done
  1.1 0.7 copy-done.1
  1.8 0.6 shard_map.28
  2.4 0.5 collective-permute-start
  2.9 2.6 %collective-permute-start.1 = (f32[392,128]{1,0:T(8,128)S(1)}, f32[392,128]{1,0:T(8,128)S(1)}, u32[]{:S(2)}, u32[]{:S(2)}) collective-permute-start(f32[392,128]{1,0:T(8,128)S(1)} %get-tuple-element.48.refs_0_), channel_id=1, source_target_pairs={{0,16},{8,24},{16,0},{24,8},{1,17},{9,25},{17,1},{25,9},{2,18},{10... | collective-permute-start | bytes 602120 | tf_op jit(solution)/shard_map/ppermute | solution.py:512
  5.5 0.1 collective-permute-start.2
  5.5 1.3 %collective-permute-start.3 = (f32[384,128]{1,0:T(8,128)S(1)}, f32[384,128]{1,0:T(8,128)S(1)}, u32[]{:S(2)}, u32[]{:S(2)}) collective-permute-start(f32[384,128]{1,0:T(8,128)S(1)} %get-tuple-element.50), channel_id=1, source_target_pairs={{7,0},{6,1},{5,2},{15,8},{14,9},{13,10},{23,16},{22,17},{21,18},{3... | collective-permute-start | bytes 589832 | tf_op jit(solution)/shard_map/ppermute | solution.py:517
  6.8 0.0 collective-permute-done.refs_1_
  6.9 4.5 %collective-permute-done.1.refs_2_ = f32[392,128]{1,0:T(8,128)S(1)} collective-permute-done((f32[392,128]{1,0:T(8,128)S(1)}, f32[392,128]{1,0:T(8,128)S(1)}, u32[]{:S(2)}, u32[]{:S(2)}) %collective-permute-start.1) | collective-permute-done | bytes 200736 | tf_op jit(solution)/shard_map/ppermute | solution.py:512
  11.3 3.8 %collective-permute-done.2.refs_3_ = f32[392,128]{1,0:T(8,128)S(1)} collective-permute-done((f32[392,128]{1,0:T(8,128)S(1)}, f32[392,128]{1,0:T(8,128)S(1)}, u32[]{:S(2)}, u32[]{:S(2)}) %collective-permute-start.2) | collective-permute-done | bytes 200736 | tf_op jit(solution)/shard_map/ppermute | solution.py:512
  15.1 2.0 %shard_map.29 = (f32[4,128,128]{2,1,0:T(8,128)S(1)}, f32[4,128,128]{2,1,0:T(8,128)S(1)}, f32[4,128,128]{2,1,0:T(8,128)S(1)}, f32[4,128,128]{2,1,0:T(8,128)S(1)}, f32[136,128]{1,0:T(8,128)S(1)}) custom-call(s32[2]{0:T(128)S(1)} %pad_add_fusion.ids, s32[4,9]{1,0:T(4,128)S(1)} %maximum_convert_fusion.lists, f32[392,128]{1,0:T(8,128)S(1)} %get-tuple-element.48.refs_0_, ...), custom_call_target="tpu_custom_call" | custom-call | tf_op jit(solution)/shard_map/pallas_call | solution.py:499
  17.2 0.0 collective-permute-done.3.moved
  17.2 0.6 shard_map.30.refs_0_
  17.8 3.7 %collective-permute-start.6 = (f32[656,128]{1,0:T(8,128)S(1)}, f32[656,128]{1,0:T(8,128)S(1)}, u32[]{:S(2)}, u32[]{:S(2)}) collective-permute-start(f32[656,128]{1,0:T(8,128)S(1)} %shard_map.30.refs_0_), channel_id=1, source_target_pairs={{0,6},{1,7},{2,0},{3,1},{4,2},{5,3},{6,4},{7,5},{8,14},{9,15},{10,... | collective-permute-start | bytes 1007624 | tf_op jit(solution)/shard_map/ppermute | solution.py:529
  21.5 0.7 collective-permute-start.4
  22.2 1.4 %collective-permute-start.5 = (f32[656,128]{1,0:T(8,128)S(1)}, f32[656,128]{1,0:T(8,128)S(1)}, u32[]{:S(2)}, u32[]{:S(2)}) collective-permute-start(f32[656,128]{1,0:T(8,128)S(1)} %shard_map.30.refs_0_), channel_id=1, source_target_pairs={{0,4},{1,5},{2,6},{3,7},{4,0},{5,1},{6,2},{7,3},{8,12},{9,13},{10,... | collective-permute-start | bytes 1007624 | tf_op jit(solution)/shard_map/ppermute | solution.py:529
  23.6 0.4 collective-permute-start.7
  24.0 6.4 %collective-permute-done.6.refs_3_ = f32[656,128]{1,0:T(8,128)S(1)} collective-permute-done((f32[656,128]{1,0:T(8,128)S(1)}, f32[656,128]{1,0:T(8,128)S(1)}, u32[]{:S(2)}, u32[]{:S(2)}) %collective-permute-start.6) | collective-permute-done | bytes 335904 | tf_op jit(solution)/shard_map/ppermute | solution.py:529
  30.4 0.9 collective-permute-start.10
  31.3 6.6 %collective-permute-done.4.refs_1_ = f32[656,128]{1,0:T(8,128)S(1)} collective-permute-done((f32[656,128]{1,0:T(8,128)S(1)}, f32[656,128]{1,0:T(8,128)S(1)}, u32[]{:S(2)}, u32[]{:S(2)}) %collective-permute-start.4) | collective-permute-done | bytes 335904 | tf_op jit(solution)/shard_map/ppermute | solution.py:529
  37.9 1.5 %collective-permute-start.8 = (f32[656,128]{1,0:T(8,128)S(1)}, f32[656,128]{1,0:T(8,128)S(1)}, u32[]{:S(2)}, u32[]{:S(2)}) collective-permute-start(f32[656,128]{1,0:T(8,128)S(1)} %collective-permute-done.4.refs_1_), channel_id=1, source_target_pairs={{0,1},{1,0},{2,3},{3,2},{4,5},{5,4},{6,7},{7,6},{8,9},{9,8},{10,11... | collective-permute-start | bytes 1007624 | tf_op jit(solution)/shard_map/ppermute | solution.py:532
  39.4 13.2 %collective-permute-done.5.refs_2_ = f32[656,128]{1,0:T(8,128)S(1)} collective-permute-done((f32[656,128]{1,0:T(8,128)S(1)}, f32[656,128]{1,0:T(8,128)S(1)}, u32[]{:S(2)}, u32[]{:S(2)}) %collective-permute-start.5) | collective-permute-done | bytes 335904 | tf_op jit(solution)/shard_map/ppermute | solution.py:529
  52.7 0.0 collective-permute-start.9
  52.7 0.0 collective-permute-done.7.refs_4_
  52.7 0.0 collective-permute-done.10.refs_7_
  52.7 0.0 collective-permute-done.8.refs_5_
  52.7 8.6 %collective-permute-done.9.refs_6_ = f32[656,128]{1,0:T(8,128)S(1)} collective-permute-done((f32[656,128]{1,0:T(8,128)S(1)}, f32[656,128]{1,0:T(8,128)S(1)}, u32[]{:S(2)}, u32[]{:S(2)}) %collective-permute-start.9) | collective-permute-done | bytes 335904 | tf_op jit(solution)/shard_map/ppermute | solution.py:532
  61.3 7.0 %shard_map.31 = (f32[32,128,128]{2,1,0:T(8,128)S(1)}, bf16[1024,1024]{1,0:T(8,128)(2,1)S(1)}, bf16[1024,1024]{1,0:T(8,128)(2,1)S(1)}, f32[8,1024]{1,0:T(8,128)S(...) custom-call(s32[2]{0:T(128)S(1)} %pad_add_fusion.ids, ...), custom_call_target="tpu_custom_call" | custom-call | flops 6442450944 | tf_op jit(solution)/shard_map/pallas_call | solution.py:499
  68.3 0.1 collective-permute-start.11
  68.4 1.2 collective-permute-start.12
  69.5 0.7 collective-permute-start.13
  70.2 4.5 %shard_map.33 = (f32[32,128,128]{2,1,0:T(8,128)S(1)}, f32[32,128,128]{2,1,0:T(8,128)S(1)}) custom-call(f32[32,128,128]{2,1,0:T(8,128)S(1)} %get-tuple-element.60.m_ref.refs_4_, bf16[1024,1024]{1,0:T(8,128)(2,1)S(1)} %get-tuple-element.61.mh, bf16[1024,1024]{1,0:T(8,128)(2,1)S(1)} %get-tuple-element.62.ml, f32[32,128,128]{2,1,0:T(8,128)S(1)} %get-tuple-element.63.s_ref, ...), custom_call_target="tpu_custom_call" | custom-call | flops 6442450944 | tf_op jit(solution)/shard_map/pallas_call | solution.py:499
  74.7 0.0 collective-permute-done.11.refs_1_
  74.7 0.0 collective-permute-done.12.refs_2_
  74.7 0.0 collective-permute-done.13.refs_3_
  74.7 2.3 %shard_map.32 = (f32[8,128]{1,0:T(8,128)S(1)}, f32[4,128,128]{2,1,0:T(8,128)S(1)}, f32[4,128,128]{2,1,0:T(8,128)S(1)}, f32[4,128,128]{2,1,0:T(8,128)S(1)}, f32[4...) custom-call(s32[2]{0:T(128)S(1)} %pad_add_fusion.ids, s32[4,9]{1,0:T(4,128)S(1)} %maximum_convert_fusion.lists, ...), custom_call_target="tpu_custom_call" | custom-call | flops 1610612736 | tf_op jit(solution)/shard_map/pallas_call | solution.py:499
  77.0 7.7 %shard_map.34 = (f32[32,128,128]{2,1,0:T(8,128)S(1)}, bf16[1024,1024]{1,0:T(8,128)(2,1)S(1)}, bf16[1024,1024]{1,0:T(8,128)(2,1)S(1)}, f32[32,128,128]{2,1,0:T(8,...) custom-call(s32[2]{0:T(128)S(1)} %pad_add_fusion.ids, ...), custom_call_target="tpu_custom_call" | custom-call | flops 6442450944 | tf_op jit(solution)/shard_map/pallas_call | solution.py:499
  84.7 0.4 collective-permute-start.14
  85.2 1.1 collective-permute-start.15
  86.3 4.4 %collective-permute-start.17 = (f32[136,128]{1,0:T(8,128)S(1)}, f32[136,128]{1,0:T(8,128)S(1)}, u32[]{:S(2)}, u32[]{:S(2)}) collective-permute-start(f32[136,128]{1,0:T(8,128)S(1)} %get-tuple-element.59.refs_1_.refs_4_.refs_0_), channel_id=1, source_target_pairs={{0,2},{1,3},{2,4},{3,5},{4,6},{5,7},{6,0},{7,1},{8,10},{9,11},{10,... | collective-permute-start | bytes 208904 | tf_op jit(solution)/shard_map/ppermute | solution.py:529
  90.6 0.0 collective-permute-start.18
  90.7 2.3 %collective-permute-start.19 = (f32[136,128]{1,0:T(8,128)S(1)}, f32[136,128]{1,0:T(8,128)S(1)}, u32[]{:S(2)}, u32[]{:S(2)}) collective-permute-start(f32[136,128]{1,0:T(8,128)S(1)} %get-tuple-element.59.refs_1_.refs_4_.refs_0_), channel_id=1, source_target_pairs={{0,6},{1,7},{2,0},{3,1},{4,2},{5,3},{6,4},{7,5},{8,14},{9,15},{10,... | collective-permute-start | bytes 208904 | tf_op jit(solution)/shard_map/ppermute | solution.py:529
  93.0 0.0 collective-permute-done.14.refs_1_
  93.0 0.0 collective-permute-start.16
  93.0 0.0 collective-permute-done.15.refs_2_
  93.0 0.1 collective-permute-start.20
  93.1 0.0 collective-permute-done.17.refs_5_.refs_1_
  93.1 2.0 %collective-permute-start.21 = (f32[136,128]{1,0:T(8,128)S(1)}, f32[136,128]{1,0:T(8,128)S(1)}, u32[]{:S(2)}, u32[]{:S(2)}) collective-permute-start(f32[136,128]{1,0:T(8,128)S(1)} %collective-permute-done.17.refs_5_.refs_1_), channel_id=1, source_target_pairs={{0,1},{1,0},{2,3},{3,2},{4,5},{5,4},{6,7},{7,6},{8,9},{9,8},{10,11... | collective-permute-start | bytes 208904 | tf_op jit(solution)/shard_map/ppermute | solution.py:532
  95.1 1.8 %collective-permute-done.18.refs_6_.refs_2_ = f32[136,128]{1,0:T(8,128)S(1)} collective-permute-done((f32[136,128]{1,0:T(8,128)S(1)}, f32[136,128]{1,0:T(8,128)S(1)}, u32[]{:S(2)}, u32[]{:S(2)}) %collective-permute-start.18) | collective-permute-done | bytes 69664 | tf_op jit(solution)/shard_map/ppermute | solution.py:529
  97.0 0.0 collective-permute-start.22
  97.0 0.0 collective-permute-done.19.refs_7_.refs_3_
  97.0 2.0 %collective-permute-start.23 = (f32[136,128]{1,0:T(8,128)S(1)}, f32[136,128]{1,0:T(8,128)S(1)}, u32[]{:S(2)}, u32[]{:S(2)}) collective-permute-start(f32[136,128]{1,0:T(8,128)S(1)} %collective-permute-done.19.refs_7_.refs_3_), channel_id=1, source_target_pairs={{0,1},{1,0},{2,3},{3,2},{4,5},{5,4},{6,7},{7,6},{8,9},{9,8},{10,11... | collective-permute-start | bytes 208904 | tf_op jit(solution)/shard_map/ppermute | solution.py:532
  99.0 4.4 %shard_map.36 = (f32[32,128,128]{2,1,0:T(8,128)S(1)}, f32[32,128,128]{2,1,0:T(8,128)S(1)}) custom-call(f32[32,128,128]{2,1,0:T(8,128)S(1)} %get-tuple-element.76.m_ref.refs_11_, bf16[1024,1024]{1,0:T(8,128)(2,1)S(1)} %get-tuple-element.77.mh, bf16[1024,1024]{1,0:T(8,128)(2,1)S(1)} %get-tuple-element.78.ml, f32[32,128,128]{2,1,0:T(8,128)S(1)} %get-tuple-element.79.s_ref, ...), custom_call_target="tpu_custom_call" | custom-call | flops 6442450944 | tf_op jit(solution)/shard_map/pallas_call | solution.py:499
  103.4 0.0 collective-permute-done.16.refs_3_
  103.4 0.0 collective-permute-done.20.refs_8_.refs_4_
  103.4 0.0 collective-permute-done.21.refs_9_.refs_5_
  103.4 0.0 collective-permute-done.22.refs_10_.refs_6_
  103.5 0.0 collective-permute-done.23.refs_11_.refs_7_
  103.5 2.3 %shard_map.35 = (f32[8,128]{1,0:T(8,128)S(1)}, f32[4,128,128]{2,1,0:T(8,128)S(1)}, f32[4,128,128]{2,1,0:T(8,128)S(1)}, f32[4,128,128]{2,1,0:T(8,128)S(1)}, f32[4...) custom-call(s32[2]{0:T(128)S(1)} %pad_add_fusion.ids, s32[4,9]{1,0:T(4,128)S(1)} %maximum_convert_fusion.lists, ...), custom_call_target="tpu_custom_call" | custom-call | flops 1610612736 | tf_op jit(solution)/shard_map/pallas_call | solution.py:499
  105.8 9.3 %shard_map.37 = (f32[9,128,128]{2,1,0:T(8,128)S(1)}, f32[9,128,128]{2,1,0:T(8,128)S(1)}, f32[8,128]{1,0:T(8,128)S(1)}) custom-call(s32[2]{0:T(128)S(1)} %pad_add_fusion.ids, s32[4,9]{1,0:T(4,128)S(1)} %maximum_convert_fusion.lists, f32[8,128]{1,0:T(8,128)S(1)} %get-tuple-element.74.coef, f32[136,128]{1,0:T(8,128)S(1)} %get-tuple-element.59.refs_1_.refs_4_.refs_0_, ...), custom_call_target="tpu_custom_call" | custom-call | tf_op jit(solution)/shard_map/pallas_call | solution.py:499
  115.2 10.1 %all_to_all.8 = f32[32,1,128]{2,1,0:T(1,128)S(1)} all-to-all(f32[32,1,128]{2,1,0:T(1,128)S(1)} %broadcast_in_dim.2), channel_id=1, replica_groups=mesh['row'=4,'col'=8] {'row','col'}, dimensions={0} | all-to-all | bytes 32768 | tf_op jit(solution)/shard_map/all_to_all | solution.py:626
  125.2 1.6 %shard_map.38 = f32[1,9,128,128]{3,2,1,0:T(8,128)} custom-call(s32[4,9]{1,0:T(4,128)S(1)} %maximum_convert_fusion.lists, s32[2]{0:T(128)S(1)} %pad_add_fusion.ids, f32[32,128]{1,0:T(8,128)S(1)} %bitcast.7, f32[9,128,128]{2,1,0:T(8,128)S(1)} %get-tuple-element.89.x_ref, f32[9,128,128]{2,1,0:T(8,128)S(1)} %get-tuple-element.90.y_ref), custom_call_target="tpu_custom_call" | custom-call | tf_op jit(solution)/shard_map/pallas_call | solution.py:499
  (8 shorter events, 0.0 us)
Async XLA Ops:
  0.1 1.1 copy-start
  1.1 0.7 copy-start.1
  2.4 4.5 %collective-permute-start = (f32[392,128]{1,0:T(8,128)S(1)}, f32[392,128]{1,0:T(8,128)S(1)}, u32[]{:S(2)}, u32[]{:S(2)}) collective-permute-start(f32[392,128]{1,0:T(8,128)S(1)} %get-tuple-element.48.refs_0_), channel_id=1, source_target_pairs={{0,8},{8,0},{16,24},{24,16},{1,9},{9,1},{17,25},{25,17},{2,10},{10... | collective-permute-start | bytes 602120 | tf_op jit(solution)/shard_map/ppermute | solution.py:512
  2.9 8.4 %collective-permute-start.1 = (f32[392,128]{1,0:T(8,128)S(1)}, f32[392,128]{1,0:T(8,128)S(1)}, u32[]{:S(2)}, u32[]{:S(2)}) collective-permute-start(f32[392,128]{1,0:T(8,128)S(1)} %get-tuple-element.48.refs_0_), channel_id=1, source_target_pairs={{0,16},{8,24},{16,0},{24,8},{1,17},{9,25},{17,1},{25,9},{2,18},{10... | collective-permute-start | bytes 602120 | tf_op jit(solution)/shard_map/ppermute | solution.py:512
  5.5 9.6 %collective-permute-start.2 = (f32[392,128]{1,0:T(8,128)S(1)}, f32[392,128]{1,0:T(8,128)S(1)}, u32[]{:S(2)}, u32[]{:S(2)}) collective-permute-start(f32[392,128]{1,0:T(8,128)S(1)} %get-tuple-element.48.refs_0_), channel_id=1, source_target_pairs={{0,24},{8,16},{16,8},{24,0},{1,25},{9,17},{17,9},{25,1},{2,26},{10... | collective-permute-start | bytes 602120 | tf_op jit(solution)/shard_map/ppermute | solution.py:512
  5.5 11.6 %collective-permute-start.3 = (f32[384,128]{1,0:T(8,128)S(1)}, f32[384,128]{1,0:T(8,128)S(1)}, u32[]{:S(2)}, u32[]{:S(2)}) collective-permute-start(f32[384,128]{1,0:T(8,128)S(1)} %get-tuple-element.50), channel_id=1, source_target_pairs={{7,0},{6,1},{5,2},{15,8},{14,9},{13,10},{23,16},{22,17},{21,18},{3... | collective-permute-start | bytes 589832 | tf_op jit(solution)/shard_map/ppermute | solution.py:517
  17.8 12.6 %collective-permute-start.6 = (f32[656,128]{1,0:T(8,128)S(1)}, f32[656,128]{1,0:T(8,128)S(1)}, u32[]{:S(2)}, u32[]{:S(2)}) collective-permute-start(f32[656,128]{1,0:T(8,128)S(1)} %shard_map.30.refs_0_), channel_id=1, source_target_pairs={{0,6},{1,7},{2,0},{3,1},{4,2},{5,3},{6,4},{7,5},{8,14},{9,15},{10,... | collective-permute-start | bytes 1007624 | tf_op jit(solution)/shard_map/ppermute | solution.py:529
  21.5 16.4 %collective-permute-start.4 = (f32[656,128]{1,0:T(8,128)S(1)}, f32[656,128]{1,0:T(8,128)S(1)}, u32[]{:S(2)}, u32[]{:S(2)}) collective-permute-start(f32[656,128]{1,0:T(8,128)S(1)} %shard_map.30.refs_0_), channel_id=1, source_target_pairs={{0,2},{1,3},{2,4},{3,5},{4,6},{5,7},{6,0},{7,1},{8,10},{9,11},{10,... | collective-permute-start | bytes 1007624 | tf_op jit(solution)/shard_map/ppermute | solution.py:529
  22.2 30.5 %collective-permute-start.5 = (f32[656,128]{1,0:T(8,128)S(1)}, f32[656,128]{1,0:T(8,128)S(1)}, u32[]{:S(2)}, u32[]{:S(2)}) collective-permute-start(f32[656,128]{1,0:T(8,128)S(1)} %shard_map.30.refs_0_), channel_id=1, source_target_pairs={{0,4},{1,5},{2,6},{3,7},{4,0},{5,1},{6,2},{7,3},{8,12},{9,13},{10,... | collective-permute-start | bytes 1007624 | tf_op jit(solution)/shard_map/ppermute | solution.py:529
  23.6 29.1 %collective-permute-start.7 = (f32[656,128]{1,0:T(8,128)S(1)}, f32[656,128]{1,0:T(8,128)S(1)}, u32[]{:S(2)}, u32[]{:S(2)}) collective-permute-start(f32[656,128]{1,0:T(8,128)S(1)} %shard_map.30.refs_0_), channel_id=1, source_target_pairs={{0,1},{1,0},{2,3},{3,2},{4,5},{5,4},{6,7},{7,6},{8,9},{9,8},{10,11... | collective-permute-start | bytes 1007624 | tf_op jit(solution)/shard_map/ppermute | solution.py:532
  30.4 22.3 %collective-permute-start.10 = (f32[656,128]{1,0:T(8,128)S(1)}, f32[656,128]{1,0:T(8,128)S(1)}, u32[]{:S(2)}, u32[]{:S(2)}) collective-permute-start(f32[656,128]{1,0:T(8,128)S(1)} %collective-permute-done.6.refs_3_), channel_id=1, source_target_pairs={{0,1},{1,0},{2,3},{3,2},{4,5},{5,4},{6,7},{7,6},{8,9},{9,8},{10,11... | collective-permute-start | bytes 1007624 | tf_op jit(solution)/shard_map/ppermute | solution.py:532
  37.9 14.8 %collective-permute-start.8 = (f32[656,128]{1,0:T(8,128)S(1)}, f32[656,128]{1,0:T(8,128)S(1)}, u32[]{:S(2)}, u32[]{:S(2)}) collective-permute-start(f32[656,128]{1,0:T(8,128)S(1)} %collective-permute-done.4.refs_1_), channel_id=1, source_target_pairs={{0,1},{1,0},{2,3},{3,2},{4,5},{5,4},{6,7},{7,6},{8,9},{9,8},{10,11... | collective-permute-start | bytes 1007624 | tf_op jit(solution)/shard_map/ppermute | solution.py:532
  52.7 8.6 %collective-permute-start.9 = (f32[656,128]{1,0:T(8,128)S(1)}, f32[656,128]{1,0:T(8,128)S(1)}, u32[]{:S(2)}, u32[]{:S(2)}) collective-permute-start(f32[656,128]{1,0:T(8,128)S(1)} %collective-permute-done.5.refs_2_), channel_id=1, source_target_pairs={{0,1},{1,0},{2,3},{3,2},{4,5},{5,4},{6,7},{7,6},{8,9},{9,8},{10,11... | collective-permute-start | bytes 1007624 | tf_op jit(solution)/shard_map/ppermute | solution.py:532
  68.3 6.4 %collective-permute-start.11 = (f32[136,128]{1,0:T(8,128)S(1)}, f32[136,128]{1,0:T(8,128)S(1)}, u32[]{:S(2)}, u32[]{:S(2)}) collective-permute-start(f32[136,128]{1,0:T(8,128)S(1)} %get-tuple-element.52.refs_0_), channel_id=1, source_target_pairs={{0,8},{8,0},{16,24},{24,16},{1,9},{9,1},{17,25},{25,17},{2,10},{10... | collective-permute-start | bytes 208904 | tf_op jit(solution)/shard_map/ppermute | solution.py:512
  68.4 6.3 %collective-permute-start.12 = (f32[136,128]{1,0:T(8,128)S(1)}, f32[136,128]{1,0:T(8,128)S(1)}, u32[]{:S(2)}, u32[]{:S(2)}) collective-permute-start(f32[136,128]{1,0:T(8,128)S(1)} %get-tuple-element.52.refs_0_), channel_id=1, source_target_pairs={{0,16},{8,24},{16,0},{24,8},{1,17},{9,25},{17,1},{25,9},{2,18},{10... | collective-permute-start | bytes 208904 | tf_op jit(solution)/shard_map/ppermute | solution.py:512
  69.5 5.2 %collective-permute-start.13 = (f32[136,128]{1,0:T(8,128)S(1)}, f32[136,128]{1,0:T(8,128)S(1)}, u32[]{:S(2)}, u32[]{:S(2)}) collective-permute-start(f32[136,128]{1,0:T(8,128)S(1)} %get-tuple-element.52.refs_0_), channel_id=1, source_target_pairs={{0,24},{8,16},{16,8},{24,0},{1,25},{9,17},{17,9},{25,1},{2,26},{10... | collective-permute-start | bytes 208904 | tf_op jit(solution)/shard_map/ppermute | solution.py:512
  84.7 8.3 %collective-permute-start.14 = (f32[136,128]{1,0:T(8,128)S(1)}, f32[136,128]{1,0:T(8,128)S(1)}, u32[]{:S(2)}, u32[]{:S(2)}) collective-permute-start(f32[136,128]{1,0:T(8,128)S(1)} %get-tuple-element.69.refs_0_), channel_id=1, source_target_pairs={{0,8},{8,0},{16,24},{24,16},{1,9},{9,1},{17,25},{25,17},{2,10},{10... | collective-permute-start | bytes 208904 | tf_op jit(solution)/shard_map/ppermute | solution.py:512
  85.2 7.9 %collective-permute-start.15 = (f32[136,128]{1,0:T(8,128)S(1)}, f32[136,128]{1,0:T(8,128)S(1)}, u32[]{:S(2)}, u32[]{:S(2)}) collective-permute-start(f32[136,128]{1,0:T(8,128)S(1)} %get-tuple-element.69.refs_0_), channel_id=1, source_target_pairs={{0,16},{8,24},{16,0},{24,8},{1,17},{9,25},{17,1},{25,9},{2,18},{10... | collective-permute-start | bytes 208904 | tf_op jit(solution)/shard_map/ppermute | solution.py:512
  86.3 6.8 %collective-permute-start.17 = (f32[136,128]{1,0:T(8,128)S(1)}, f32[136,128]{1,0:T(8,128)S(1)}, u32[]{:S(2)}, u32[]{:S(2)}) collective-permute-start(f32[136,128]{1,0:T(8,128)S(1)} %get-tuple-element.59.refs_1_.refs_4_.refs_0_), channel_id=1, source_target_pairs={{0,2},{1,3},{2,4},{3,5},{4,6},{5,7},{6,0},{7,1},{8,10},{9,11},{10,... | collective-permute-start | bytes 208904 | tf_op jit(solution)/shard_map/ppermute | solution.py:529
  90.6 6.3 %collective-permute-start.18 = (f32[136,128]{1,0:T(8,128)S(1)}, f32[136,128]{1,0:T(8,128)S(1)}, u32[]{:S(2)}, u32[]{:S(2)}) collective-permute-start(f32[136,128]{1,0:T(8,128)S(1)} %get-tuple-element.59.refs_1_.refs_4_.refs_0_), channel_id=1, source_target_pairs={{0,4},{1,5},{2,6},{3,7},{4,0},{5,1},{6,2},{7,3},{8,12},{9,13},{10,... | collective-permute-start | bytes 208904 | tf_op jit(solution)/shard_map/ppermute | solution.py:529
  90.7 6.3 %collective-permute-start.19 = (f32[136,128]{1,0:T(8,128)S(1)}, f32[136,128]{1,0:T(8,128)S(1)}, u32[]{:S(2)}, u32[]{:S(2)}) collective-permute-start(f32[136,128]{1,0:T(8,128)S(1)} %get-tuple-element.59.refs_1_.refs_4_.refs_0_), channel_id=1, source_target_pairs={{0,6},{1,7},{2,0},{3,1},{4,2},{5,3},{6,4},{7,5},{8,14},{9,15},{10,... | collective-permute-start | bytes 208904 | tf_op jit(solution)/shard_map/ppermute | solution.py:529
  93.0 10.4 %collective-permute-start.16 = (f32[136,128]{1,0:T(8,128)S(1)}, f32[136,128]{1,0:T(8,128)S(1)}, u32[]{:S(2)}, u32[]{:S(2)}) collective-permute-start(f32[136,128]{1,0:T(8,128)S(1)} %get-tuple-element.69.refs_0_), channel_id=1, source_target_pairs={{0,24},{8,16},{16,8},{24,0},{1,25},{9,17},{17,9},{25,1},{2,26},{10... | collective-permute-start | bytes 208904 | tf_op jit(solution)/shard_map/ppermute | solution.py:512
  93.0 10.4 %collective-permute-start.20 = (f32[136,128]{1,0:T(8,128)S(1)}, f32[136,128]{1,0:T(8,128)S(1)}, u32[]{:S(2)}, u32[]{:S(2)}) collective-permute-start(f32[136,128]{1,0:T(8,128)S(1)} %get-tuple-element.59.refs_1_.refs_4_.refs_0_), channel_id=1, source_target_pairs={{0,1},{1,0},{2,3},{3,2},{4,5},{5,4},{6,7},{7,6},{8,9},{9,8},{10,11... | collective-permute-start | bytes 208904 | tf_op jit(solution)/shard_map/ppermute | solution.py:532
  93.1 10.3 %collective-permute-start.21 = (f32[136,128]{1,0:T(8,128)S(1)}, f32[136,128]{1,0:T(8,128)S(1)}, u32[]{:S(2)}, u32[]{:S(2)}) collective-permute-start(f32[136,128]{1,0:T(8,128)S(1)} %collective-permute-done.17.refs_5_.refs_1_), channel_id=1, source_target_pairs={{0,1},{1,0},{2,3},{3,2},{4,5},{5,4},{6,7},{7,6},{8,9},{9,8},{10,11... | collective-permute-start | bytes 208904 | tf_op jit(solution)/shard_map/ppermute | solution.py:532
  97.0 6.5 %collective-permute-start.22 = (f32[136,128]{1,0:T(8,128)S(1)}, f32[136,128]{1,0:T(8,128)S(1)}, u32[]{:S(2)}, u32[]{:S(2)}) collective-permute-start(f32[136,128]{1,0:T(8,128)S(1)} %collective-permute-done.18.refs_6_.refs_2_), channel_id=1, source_target_pairs={{0,1},{1,0},{2,3},{3,2},{4,5},{5,4},{6,7},{7,6},{8,9},{9,8},{10,11... | collective-permute-start | bytes 208904 | tf_op jit(solution)/shard_map/ppermute | solution.py:532
  97.0 6.5 %collective-permute-start.23 = (f32[136,128]{1,0:T(8,128)S(1)}, f32[136,128]{1,0:T(8,128)S(1)}, u32[]{:S(2)}, u32[]{:S(2)}) collective-permute-start(f32[136,128]{1,0:T(8,128)S(1)} %collective-permute-done.19.refs_7_.refs_3_), channel_id=1, source_target_pairs={{0,1},{1,0},{2,3},{3,2},{4,5},{5,4},{6,7},{7,6},{8,9},{9,8},{10,11... | collective-permute-start | bytes 208904 | tf_op jit(solution)/shard_map/ppermute | solution.py:532

commit v3 on v2

--- a/solution.py
+++ b/solution.py
@@ -67,26 +67,32 @@
     return out
 
 
-SHARE = 4
+PAIR = 8
+FEW, SOME, ALL = 4, 5, 7
+FRONT = 5
+NAMES = FRONT * BW
+TERMS = 16 + PAIR * BW
+HALF = NAMES + 16
 
 
 @functools.lru_cache
-def shares(nq):
-    stored = []
+def stored(nq):
+    out = []
     for b in range(nq):
-        slots = [t for t, d in enumerate(offsets(b, nq)) if (b + d) % nq <= b]
-        stored.append(slots)
-    keep = [slots[:SHARE] for slots in stored]
-    give = [slots[SHARE:] for slots in stored]
-    donors = sorted((b for b in range(nq) if give[b]), key=lambda b: (-len(give[b]), -b))
-    takers = sorted((b for b in range(nq) if len(keep[b]) < SHARE), key=lambda b: len(keep[b]))
-    moves = list(zip(donors, takers))
-    pair = lambda b, t: ((b + offsets(b, nq)[t]) % nq, b)
-    held = [[pair(b, t) for t in keep[b]] for b in range(nq)]
-    for donor, taker in moves:
-        held[taker] += [pair(donor, t) for t in give[donor]]
-    assert len(donors) == len(takers) and all(len(h) == SHARE for h in held)
-    return keep, give, moves, held
+        out.append([t for t, d in enumerate(offsets(b, nq)) if (b + d) % nq <= b])
+    for b in range(nq // 2):
+        assert len(out[b]) <= FEW and len(out[b]) + len(out[nq - 1 - b]) == PAIR
+    return out
+
+
+def counts(nq):
+    return [len(stored(nq)[nq - 1 - p]) for p in range(nq // 2)]
+
+
+def pair_blocks(nq, p):
+    return [
+        ((b + offsets(b, nq)[t]) % nq, b) for b in (nq - 1 - p, p) for t in stored(nq)[b]
+    ]
 
 
 def split(x):
@@ -99,7 +105,15 @@
 
 
 def dot3(ah, al, bh, bl):
-    return mm(ah, bh) + (mm(ah, bl) + mm(al, bh))
+    if bh.shape[1] != BW:
+        return mm(ah, bh) + (mm(ah, bl) + mm(al, bh))
+    if bh.shape[0] == BW:
+        top = jnp.concatenate([bh, bl], axis=1)
+        low = jnp.concatenate([bh, jnp.zeros_like(bl)], axis=1)
+        both = mm(jnp.concatenate([ah, al], axis=1), jnp.concatenate([top, low], axis=0))
+        return both[:, :BW] + both[:, BW:]
+    both = mm(ah, jnp.concatenate([bh, bl], axis=1))
+    return both[:, :BW] + (both[:, BW:] + mm(al, bh))
 
 
 def dotf(a, b):
@@ -234,53 +248,103 @@
     return out
 
 
-def prepare_kernel(nq, width, ids, names, blocks, near, extra, row):
+def prepare_kernel(nq, ids, names, blocks, most, few, row):
     q = ids[1]
-    keep, give, _, _ = shares(nq)
     lane = lax.broadcasted_iota(jnp.int32, (1, BW), 1)
     listed = jnp.zeros((1, BW), f32)
     for t in range(names.shape[1]):
         listed = jnp.where(lane == t, names[0, t].astype(f32), listed)
     listed = jnp.broadcast_to(listed, (8, BW))
-    for i in range(SHARE):
-        near[cut(i), :] = blocks[choose(q, [k[min(i, len(k) - 1)] for k in keep])]
-    near[SHARE * BW :, :] = listed
-    for i in range(width):
-        extra[cut(i), :] = blocks[choose(q, [(g + [0] * width)[i] for g in give])]
+    most[0:8, :] = listed
+    few[0:8, :] = listed
+    for i in range(ALL):
+        block = blocks[choose(q, [(slots + [0] * ALL)[i] for slots in stored(nq)])]
+        most[place(i), :] = block
+        if i < FEW:
+            few[place(i), :] = block
     for i, t in enumerate((0, NEAR, NEAR + 1)):
         row[cut(i), :] = blocks[t]
     row[3 * BW :, :] = listed
 
 
-def share_kernel(nq, width, ids, near, moved, own_pack, out):
+def place(i):
+    return slice(8 + i * BW, 8 + (i + 1) * BW)
+
+
+def at_place(i):
+    return pl.ds(pl.multiple_of(8 + i * BW, 8), BW)
+
+
+def lay(i):
+    start = i * BW + (16 if i >= FRONT else 0)
+    return slice(start, start + BW)
+
+
+def pair_kernel(nq, ids, own, all_in, some_in, few_in, own_pack, pack_in, front, back):
     q = ids[1]
-    count = choose(q, [len(k) for k in shares(nq)[0]])
-    out[0 : SHARE * BW + 8, :] = near[...]
-    out[SHARE * BW + 8 :, :] = own_pack[...]
-    for i in range(1, SHARE):
-
-        @pl.when(i >= count)
-        def _():
-            out[cut(i), :] = moved[pl.ds(pl.multiple_of((i - count) * BW, BW), BW), :]
+    upper = q >= nq // 2
+    count = choose(jnp.where(upper, nq - 1 - q, q), counts(nq))
+
+    def fill(first, second):
+        for i in range(PAIR):
+            out, rows = (front, lay(i)) if i < FRONT else (back, cut(i - FRONT))
+            if i < FEW:
+                out[rows, :] = first[place(i), :]
+                continue
+            if i < (first.shape[0] - 8) // BW:
+
+                @pl.when(i < count)
+                def _(out=out, rows=rows, i=i):
+                    out[rows, :] = first[place(i), :]
+
+            @pl.when(i >= count)
+            def _(out=out, rows=rows, i=i):
+                out[rows, :] = second[at_place(i - count), :]
+
+        front[NAMES : NAMES + 8, :] = first[0:8, :]
+        front[NAMES + 8 : NAMES + 16, :] = second[0:8, :]
+
+    wide = count > SOME
+
+    @pl.when(upper)
+    def _():
+        fill(own, few_in)
+
+    @pl.when(jnp.logical_and(jnp.logical_not(upper), wide))
+    def _():
+        fill(all_in, own)
+
+    @pl.when(jnp.logical_and(jnp.logical_not(upper), jnp.logical_not(wide)))
+    def _():
+        fill(some_in, own)
+
+    terms = (PAIR - FRONT) * BW
+    back[terms : terms + PACK, :] = jnp.where(upper, own_pack[...], pack_in[...])
+    back[terms + PACK :, :] = jnp.where(upper, pack_in[...], own_pack[...])
 
 
 def first_kernel(nq, ids, *refs):
-    parts, refs = refs[:nq], refs[nq:]
+    half = nq // 2
+    fronts, backs, refs = refs[:half], refs[half:nq], refs[nq:]
     own_pack, m_ref, mh, ml, link, s_ref, sh, sl, out_ref, packs, near = refs
     q = ids[1]
-    settle(nq, q, parts, near)
-    for b in range(nq):
-        packs[b] = near[b, SHARE * BW + 8 :, :]
+    own = jnp.minimum(q, nq - 1 - q)
+    for m in range(half):
+        near[m ^ own, 0:HALF, :] = fronts[m][...]
+        near[m ^ own, HALF:, :] = backs[m][...]
     clear_unlinked(mh, ml, nq)
     link[...] = jnp.zeros_like(link)
     index = pair_index(nq)
-    for b, pairs in enumerate(shares(nq)[3]):
-        for i, pair in enumerate(pairs):
-            block = near[b, cut(i), :]
+    for p in range(half):
+        packs[nq - 1 - p] = near[p, TERMS : TERMS + PACK, :]
+        packs[p] = near[p, TERMS + PACK :, :]
+        for i, pair in enumerate(pair_blocks(nq, p)):
+            block = near[p, lay(i), :]
             m_ref[index[pair]] = block
             put_dense(mh, ml, *pair, block)
     for a in range(nq):
-        listed = near[a, SHARE * BW : SHARE * BW + 1, :]
+        row = NAMES if a >= half else NAMES + 8
+        listed = near[min(a, nq - 1 - a), row : row + 1, :]
         present = jnp.where(listed >= 0.0, 1.0, 0.0)
         for t, d in enumerate(offsets(a, nq)):
             b = (a + d) % nq
@@ -288,19 +352,18 @@
     square_part(nq, q, own_pack, m_ref, mh, ml, link, s_ref, sh, sl, out_ref)
 
 
-def assemble(nq, q, coef, packs, x_ref, y_ref, m_old, held, m_ref, mh, ml):
+def assemble(nq, q, c, inv, packs, x_ref, y_ref, m_old, held, m_ref, mh, ml):
     index = pair_index(nq)
-    c = coef[0:1, :]
-    inv = coef[1:2, :]
     settle(nq, q, packs, held)
     clear_unlinked(mh, ml, nq)
     for b in range(nq):
         g, e = unpack_pair(held[b, 0:BW, :], held[b, BW : BW + 1, :])
-        gh, gl = split(g)
-        for (a, b2), place in index.items():
-            if b2 != b:
-                continue
-            fix = dot3(*split(m_old[place]), gh, gl)
+        rows = [a for a in range(nq) if (a, b) in index]
+        stack = jnp.concatenate([m_old[index[(a, b)]] for a in rows], axis=0)
+        fixes = dotf(stack, g)
+        for i, a in enumerate(rows):
+            fix = fixes[cut(i), :]
+            place = index[(a, b)]
             block = x_ref[place] + c * y_ref[place]
             if a == b:
                 block = block + (1.0 + c) * g - (fix + fix.T + e)
@@ -315,7 +378,7 @@
     packs, own_pack, refs = refs[:count], refs[count], refs[count + 1 :]
     x_ref, y_ref, m_old, link, m_ref, mh, ml, s_ref, sh, sl, out_ref, held = refs
     q = ids[1]
-    assemble(nq, q, coef, packs, x_ref, y_ref, m_old, held, m_ref, mh, ml)
+    assemble(nq, q, coef[0:1, :], coef[1:2, :], packs, x_ref, y_ref, m_old, held, m_ref, mh, ml)
     square_part(nq, q, own_pack, m_ref, mh, ml, link, s_ref, sh, sl, out_ref)
 
 
@@ -426,23 +489,47 @@
     cross_tail(nr, nq, ids, lists, d_ref, u_ref, su_ref, v_ref, pack_ref)
 
 
-def last_kernel(nr, nq, count, ids, lists, coef, *refs):
-    packs, refs = refs[:count], refs[count:]
-    own_pack, x_old, y_old, m_old, link, d_ref, u_ref, su_ref, v_ref = refs[:9]
-    x_out, y_out, sums, held, m_ref, mh, ml, col, sq, sqh, sql = refs[9:]
+def last_kernel(nr, nq, count, ids, lists, *refs):
+    parts, packs, refs = refs[:nr], refs[nr : nr + count], refs[nr + count :]
+    x_old, y_old, m_old, link, d_old, u_old, su_old, v_old = refs[:8]
+    x_out, y_out, sums, rows, ends, held, m_ref, mh, ml, col, sq = refs[8:]
     r, q = ids[0], ids[1]
-    assemble(nq, q, coef, packs, x_old, y_old, m_old, held, m_ref, mh, ml)
-    g, e = unpack_pair(own_pack[0:BW, :], own_pack[BW : BW + 1, :])
+    for k in range(nr):
+        rows[k ^ r] = parts[k][...]
+    c, inv = coefficient(nr, nq, q, rows, packs, ends)
+
+    def step(p, s, k):
+        return ((1.0 - 2.0 * c) * p + (1.0 + c) * s - k) * inv
+
+    def told(p):
+        return unpack_pair(rows[p, 0:BW, :], rows[p, BW : BW + 1, :])
+
+    assemble(nq, q, c, inv, packs, x_old, y_old, m_old, held, m_ref, mh, ml)
+    d = m_ref[q]
+    g = jnp.zeros((BW, BW), f32)
+    e = jnp.zeros((BW, BW), f32)
+    cross = []
+    for slot in (7, 8):
+        far = far_row(lists, r, nq, r, slot)
+        edge = r if slot == 8 else far
+        u, su = u_old[edge], su_old[edge]
+        u = step(u, su, dotf(u, told(jnp.maximum(far, r))[0]) + v_old[edge])
+        flipped = u.T
+        mine = r > far
+        cu = jnp.where(mine, u, flipped)
+        cut_ = split(jnp.where(mine, flipped, u))
+        far_d = split(step(d_old[far], *told(far)))
+        t = dot3(*far_d, *split(cu))
+        scu = dotf(cu, d) + t
+        g = g + dot3(*cut_, *split(cu))
+        e = e + dot3(*cut_, *split(t))
+        cross.append((slot, cu, scu, dot3(*far_d, *split(scu))))
     sq[...] = dot3(mh[...], ml[...], mh[:, at(q)], ml[:, at(q)])
     for a in range(nq):
         sq[cut(a), :] = sq[cut(a), :] * link[a : a + 1, at(q)]
     sq[at(q), :] = sq[at(q), :] + g
-    hi, lo = split(sq[...])
-    sqh[...] = hi
-    sql[...] = lo
-    d = m_ref[q]
+    col[...] = dot3(mh[...], ml[...], *split(sq[...]))
     s0 = sq[at(q), :]
-    col[...] = dot3(mh[...], ml[...], hi, lo)
     k0 = col[at(q), :] + dotf(g, d) + e
     i, j = row_col()
     sums[0:1, :] = total(jnp.where(i == j, d - s0, 0.0))
@@ -454,20 +541,16 @@
         if t < 6:
             a = lax.rem(q + jnp.int32(offsets(0, nq)[t] + nq), jnp.int32(nq))
         else:
-            step = jnp.where(lax.rem(q, jnp.int32(2)) == 0, 3, nq - 3)
-            a = lax.rem(q + step, jnp.int32(nq))
+            step_3 = jnp.where(lax.rem(q, jnp.int32(2)) == 0, 3, nq - 3)
+            a = lax.rem(q + step_3, jnp.int32(nq))
         m = mh[at(a), at(q)].astype(f32) + ml[at(a), at(q)].astype(f32)
         s = sq[at(a), :]
         x_out[t] = (m + s) - col[at(a), :]
         y_out[t] = s - 2.0 * m
-    sh, sl = split(s0)
-    for t in (7, 8):
-        far = far_row(lists, r, nq, r, t)
-        edge = r if t == 8 else far
-        u, su = u_ref[edge], su_ref[edge]
-        k = dot3(*split(u), sh, sl) + v_ref[edge]
-        x_out[t] = (u + su) - k
-        y_out[t] = su - 2.0 * u
+    s0 = split(s0)
+    for slot, cu, scu, part in cross:
+        x_out[slot] = (cu + scu) - (dot3(*split(cu), *s0) + part)
+        y_out[slot] = scu - 2.0 * cu
 
 
 def finish_kernel(slots, lists, ids, parts, x_ref, y_ref, out_ref):
@@ -513,24 +596,55 @@
     ]
 
 
-def gather_near(near, extra, own_pack, ids, width, nq):
-    moved = lax.ppermute(extra, "col", shares(nq)[2])
-    (own,) = call(
-        functools.partial(share_kernel, nq, width),
-        [((near.shape[0] + PACK, BW), f32)],
-        (ids, near, moved, own_pack),
+def gather_pairs(most, few, own_pack, ids, nq):
+    half = nq // 2
+    size = [len(slots) for slots in stored(nq)]
+    far = lambda keep: [(i, nq - 1 - i) for i in range(nq) if keep(i)]
+    all_in = lax.ppermute(most, "col", far(lambda i: i >= half and size[i] > SOME))
+    some_in = lax.ppermute(
+        most[: 8 + SOME * BW], "col", far(lambda i: i >= half and size[i] <= SOME)
+    )
+    few_in = lax.ppermute(few, "col", far(lambda i: i < half))
+    pack_in = lax.ppermute(own_pack, "col", far(lambda i: True))
+    front, back = call(
+        functools.partial(pair_kernel, nq),
+        [((HALF, BW), f32), ((TERMS + 2 * PACK - HALF, BW), f32)],
+        (ids, most, all_in, some_in, few_in, own_pack, pack_in),
         1,
     )
-    return gather(own, nq)
-
-
-def gather(x, nq):
-    here = [x] + [
+    backs = tree_gather(back, "col", half, drop_high, nq // half)
+    fronts = tree_gather(front, "col", half, drop_low, nq // half)
+    return fronts + backs
+
+
+def drop_low(m):
+    return m & (m - 1)
+
+
+def drop_high(m):
+    return m ^ (1 << (m.bit_length() - 1))
+
+
+def tree_gather(x, axis, size, parent, repeat=1):
+    depth = lambda m: 0 if m == 0 else 1 + depth(parent(m))
+    got = {0: x}
+    for m in sorted(range(1, size), key=lambda m: (depth(m), -m)):
+        step = m ^ parent(m)
+        got[m] = lax.ppermute(got[parent(m)], axis, [(i, i ^ step) for i in range(size * repeat)])
+    return [got[m] for m in range(size)]
+
+
+def along(x, nq):
+    return [x] + [
         lax.ppermute(x, "col", [(i, (i + 2 * k) % nq) for i in range(nq)])
         for k in range(1, nq // 2)
     ]
-    there = [lax.ppermute(y, "col", [(i, i ^ 1) for i in range(nq)]) for y in here]
-    return here + there
+
+
+def across(parts, nq):
+    return parts + [
+        lax.ppermute(y, "col", [(i, i ^ 1) for i in range(nq)]) for y in parts
+    ]
 
 
 def body(upper_blocks, members):
@@ -541,11 +655,9 @@
     npair = len(pattern(nq))
     ids = jnp.stack([lax.axis_index("row"), lax.axis_index("col")]).astype(jnp.int32)
 
-    width = max(len(g) for g in shares(nq)[1])
-    share = (SHARE * BW + 8, BW)
-    near, extra, row_part = call(
-        functools.partial(prepare_kernel, nq, width),
-        [(share, f32), ((width * BW, BW), f32), ((3 * BW + 8, BW), f32)],
+    most, few, row_part = call(
+        functools.partial(prepare_kernel, nq),
+        [((8 + ALL * BW, BW), f32), ((8 + FEW * BW, BW), f32), ((3 * BW + 8, BW), f32)],
         (ids, members, blocks),
         2,
     )
@@ -564,7 +676,7 @@
         functools.partial(cross_first_kernel, nr, nq), cross_outs, (ids, lists, *row), 2,
         [pltpu.VMEM((nr, 3 * BW + 8, BW), f32)],
     )
-    nears = gather_near(near, extra, own, ids, width, nq)
+    nears = gather_pairs(most, few, own, ids, nq)
     m, mh, ml, link, s, sh, sl, tell, packs = call(
         functools.partial(first_kernel, nq),
         [(listed, f32), (dense, bf16), (dense, bf16), ((nq, order), f32)]
@@ -572,7 +684,7 @@
         + [((nq,) + pack, f32)],
         (ids, *nears, own),
         1,
-        [pltpu.VMEM((nq,) + nears[0].shape, f32)],
+        [pltpu.VMEM((nq // 2, TERMS + 2 * PACK, BW), f32)],
         flops=square_flops,
     )
     packs = [packs]
@@ -585,6 +697,8 @@
             0,
             flops=square_flops,
         )
+        if step == PURIFY - 2:
+            break
         coef, d, u, su, v, own = call(
             functools.partial(cross_kernel, nr, nq, len(packs)),
             [((8, BW), f32)] + cross_outs,
@@ -594,31 +708,32 @@
             flops=square_flops // 4,
         )
         old = packs
-        if step < PURIFY - 2:
-            packs = gather(own, nq)
-            m, mh, ml, s, sh, sl, tell = call(
-                functools.partial(next_kernel, nq, len(old)),
-                [(listed, f32), (dense, bf16), (dense, bf16)] + square_outs,
-                (ids, coef, *old, own, x, y, m, link),
-                1,
-                [pltpu.VMEM((nq, PACK, BW), f32)],
-                flops=square_flops,
-            )
+        straight = along(own, nq)
+        m, mh, ml, s, sh, sl, tell = call(
+            functools.partial(next_kernel, nq, len(old)),
+            [(listed, f32), (dense, bf16), (dense, bf16)] + square_outs,
+            (ids, coef, *old, own, x, y, m, link),
+            1,
+            [pltpu.VMEM((nq, PACK, BW), f32)],
+            flops=square_flops,
+        )
+        tell, *straight = lax.optimization_barrier((tell, *straight))
+        packs = across(straight, nq)
     strip = (order, BW)
     xo, yo, sums = call(
-        functools.partial(last_kernel, nr, nq, len(old)),
+        functools.partial(last_kernel, nr, nq, len(packs)),
         [((slots, BW, BW), f32)] * 2 + [((8, BW), f32)],
-        (ids, lists, coef, *old, own, x, y, m, link, d, u, su, v),
+        (ids, lists, *rows, *packs, x, y, m, link, d, u, su, v),
         2,
         [
+            pltpu.VMEM((nr, PACK, BW), f32),
+            pltpu.VMEM((nq, 8, BW), f32),
             pltpu.VMEM((nq, PACK, BW), f32),
             pltpu.VMEM(listed, f32),
             pltpu.VMEM(dense, bf16),
             pltpu.VMEM(dense, bf16),
             pltpu.VMEM(strip, f32),
             pltpu.VMEM(strip, f32),
-            pltpu.VMEM(strip, bf16),
-            pltpu.VMEM(strip, bf16),
         ],
     )
     lane = jnp.arange(BW) < BW // 2

time: 127 us -> 112 us (0.88)
  waiting for transfers between devices: 45 us -> 19.7 us
  starting transfers between devices: 27.4 us -> 44.3 us
  Pallas kernels: 42.3 us -> 35.6 us
    ppermute x15 -> x17, waiting for transfers between devices: 36.8 us -> 17.6 us  [the longest x6 14.2 us: tree_gather(): lax.ppermute(got[parent(m)], axis, [(i, i ^ step) for i in range(size * r...]
    ppermute x15 -> x17, starting transfers between devices: 20.8 us -> 37.2 us  [the longest x6 15.2 us: tree_gather(): lax.ppermute(got[parent(m)], axis, [(i, i ^ step) for i in range(size * r...]
    pallas_call x11 -> x10, Pallas kernels: 42.3 us -> 35.6 us  [call(): pl.pallas_call(kernel, out_shape=[jax.ShapeDtypeStruct(s, d) for s, d in...]
    ppermute x9, waiting for transfers between devices: 8.25 us -> 2.08 us  [spread(): lax.ppermute(x, axis, [(i, i ^ k) for i in range(size)])]
  transfers between devices with their start and end apart: 24 -> 26, of which waited for: 7 -> 7; matrix products, arithmetic and copies ran while one was open for 0% -> 0% of each run, Pallas kernels for 9% -> 16%
where the time goes in v3:
time: 112 us
  starting transfers between devices  44.3 us (40%)
  Pallas kernels  35.6 us (32%)
  waiting for transfers between devices  19.7 us (18%)
  blocking collectives  10.3 us (9%)
  local copies, waits for them, and re-layouts  1.76 us (2%)
    pallas_call x10, Pallas kernels, call(): pl.pallas_call(kernel, out_shape=[jax.ShapeDtypeStruct(s, d) for s, d in...  35.6 us
    ppermute x6, starting transfers between devices, tree_gather(): lax.ppermute(got[parent(m)], axis, [(i, i ^ step) for i in range(size * r...  15.2 us
    ppermute x6, waiting for transfers between devices, tree_gather(): lax.ppermute(got[parent(m)], axis, [(i, i ^ step) for i in range(size * r...  14.2 us
    all_to_all x1, blocking collectives, body(): lax.all_to_all(jnp.broadcast_to(mine[None], (nr * nq, BW)), ('row', 'col'...  10.3 us
    ppermute x9, starting transfers between devices, spread(): lax.ppermute(x, axis, [(i, i ^ k) for i in range(size)])  7.13 us
    ppermute x1, starting transfers between devices, gather_pairs(): few_in = lax.ppermute(few, 'col', far(lambda i: i < half))  7.12 us
    ppermute x1, starting transfers between devices, gather_pairs(): pack_in = lax.ppermute(own_pack, 'col', far(lambda i: True))  4.94 us
    ppermute x3, starting transfers between devices, along(): lax.ppermute(x, 'col', [(i, (i + 2 * k) % nq) for i in range(nq)])  4.25 us
  transfers between devices with their start and end apart: 26, of which 7 were waited for; matrix products, arithmetic and copies ran while one was open for 0% of the time, Pallas kernels for 16%

profile of v3, /device:TPU:0, one launch (start us, length us, event | category | flops | bytes accessed | tf_op | source)
XLA Modules:
  0.0 112.1 jit_solution(15849158926963348205)
XLA Ops:
  0.0 0.1 pad_add_fusion.ids
  0.1 1.1 copy-done
  1.1 0.7 copy-done.1
  1.8 0.6 shard_map.28
  2.4 0.5 collective-permute-start
  2.9 1.3 %collective-permute-start.3 = (f32[904,128]{1,0:T(8,128)S(1)}, f32[904,128]{1,0:T(8,128)S(1)}, u32[]{:S(2)}, u32[]{:S(2)}) collective-permute-start(f32[904,128]{1,0:T(8,128)S(1)} %get-tuple-element.50.own), channel_id=1, source_target_pairs={{6,1},{7,0},{14,9},{15,8},{22,17},{23,16},{30,25},{31,24}} | collective-permute-start | bytes 1388552 | tf_op jit(solution)/shard_map/ppermute | solution.py:603
  4.2 2.6 %collective-permute-start.1 = (f32[392,128]{1,0:T(8,128)S(1)}, f32[392,128]{1,0:T(8,128)S(1)}, u32[]{:S(2)}, u32[]{:S(2)}) collective-permute-start(f32[392,128]{1,0:T(8,128)S(1)} %get-tuple-element.49.refs_0_), channel_id=1, source_target_pairs={{0,16},{8,24},{16,0},{24,8},{1,17},{9,25},{17,1},{25,9},{2,18},{10... | collective-permute-start | bytes 602120 | tf_op jit(solution)/shard_map/ppermute | solution.py:595
  6.8 0.2 collective-permute-start.2
  7.0 0.7 collective-permute-start.4
  7.7 0.0 collective-permute-done.refs_1_
  7.7 7.1 %collective-permute-start.5 = (f32[520,128]{1,0:T(8,128)S(1)}, f32[520,128]{1,0:T(8,128)S(1)}, u32[]{:S(2)}, u32[]{:S(2)}) collective-permute-start(f32[520,128]{1,0:T(8,128)S(1)} %get-tuple-element.51), channel_id=1, source_target_pairs={{0,7},{1,6},{2,5},{3,4},{8,15},{9,14},{10,13},{11,12},{16,23},{17,... | collective-permute-start | bytes 798728 | tf_op jit(solution)/shard_map/ppermute | solution.py:607
  14.8 0.0 collective-permute-done.1.refs_2_
  14.9 1.7 %collective-permute-done.2.refs_3_ = f32[392,128]{1,0:T(8,128)S(1)} collective-permute-done((f32[392,128]{1,0:T(8,128)S(1)}, f32[392,128]{1,0:T(8,128)S(1)}, u32[]{:S(2)}, u32[]{:S(2)}) %collective-permute-start.2) | collective-permute-done | bytes 200736 | tf_op jit(solution)/shard_map/ppermute | solution.py:595
  16.5 2.1 %shard_map.29 = (f32[4,128,128]{2,1,0:T(8,128)S(1)}, f32[4,128,128]{2,1,0:T(8,128)S(1)}, f32[4,128,128]{2,1,0:T(8,128)S(1)}, f32[4,128,128]{2,1,0:T(8,128)S(1)}, f32[136,128]{1,0:T(8,128)S(1)}) custom-call(s32[2]{0:T(128)S(1)} %pad_add_fusion.ids, s32[4,9]{1,0:T(4,128)S(1)} %maximum_convert_fusion.lists, f32[392,128]{1,0:T(8,128)S(1)} %get-tuple-element.49.refs_0_, ...), custom_call_target="tpu_custom_call" | custom-call | tf_op jit(solution)/shard_map/pallas_call | solution.py:582
  18.6 4.9 %collective-permute-start.6 = (f32[136,128]{1,0:T(8,128)S(1)}, f32[136,128]{1,0:T(8,128)S(1)}, u32[]{:S(2)}, u32[]{:S(2)}) collective-permute-start(f32[136,128]{1,0:T(8,128)S(1)} %get-tuple-element.52.own_pack.refs_8_), channel_id=1, source_target_pairs={{0,7},{1,6},{2,5},{3,4},{4,3},{5,2},{6,1},{7,0},{8,15},{9,14},{10,... | collective-permute-start | bytes 208904 | tf_op jit(solution)/shard_map/ppermute | solution.py:608
  23.6 0.0 collective-permute-done.5.few_in
  23.6 3.0 %collective-permute-done.6.pack_in = f32[136,128]{1,0:T(8,128)S(1)} collective-permute-done((f32[136,128]{1,0:T(8,128)S(1)}, f32[136,128]{1,0:T(8,128)S(1)}, u32[]{:S(2)}, u32[]{:S(2)}) %collective-permute-start.6) | collective-permute-done | bytes 69664 | tf_op jit(solution)/shard_map/ppermute | solution.py:608
  26.5 0.0 collective-permute-done.4.some_in
  26.5 0.0 collective-permute-done.3.all_in
  26.5 0.6 shard_map.30
  27.2 1.5 %collective-permute-start.10 = (f32[656,128]{1,0:T(8,128)S(1)}, f32[656,128]{1,0:T(8,128)S(1)}, u32[]{:S(2)}, u32[]{:S(2)}) collective-permute-start(f32[656,128]{1,0:T(8,128)S(1)} %get-tuple-element.54.refs_4_), channel_id=1, source_target_pairs={{0,1},{1,0},{2,3},{3,2},{4,5},{5,4},{6,7},{7,6},{8,9},{9,8},{10,11... | collective-permute-start | bytes 1007624 | tf_op jit(solution)/shard_map/ppermute | solution.py:633
  28.7 5.7 %collective-permute-start.8 = (f32[656,128]{1,0:T(8,128)S(1)}, f32[656,128]{1,0:T(8,128)S(1)}, u32[]{:S(2)}, u32[]{:S(2)}) collective-permute-start(f32[656,128]{1,0:T(8,128)S(1)} %get-tuple-element.53.refs_0_), channel_id=1, source_target_pairs={{0,2},{1,3},{2,0},{3,1},{4,6},{5,7},{6,4},{7,5},{8,10},{9,11},{10,... | collective-permute-start | bytes 1007624 | tf_op jit(solution)/shard_map/ppermute | solution.py:633
  34.4 0.0 collective-permute-start.11
  34.4 0.1 collective-permute-start.7
  34.6 2.7 %collective-permute-done.10.refs_5_ = f32[656,128]{1,0:T(8,128)S(1)} collective-permute-done((f32[656,128]{1,0:T(8,128)S(1)}, f32[656,128]{1,0:T(8,128)S(1)}, u32[]{:S(2)}, u32[]{:S(2)}) %collective-permute-start.10) | collective-permute-done | bytes 335904 | tf_op jit(solution)/shard_map/ppermute | solution.py:633
  37.2 5.8 %collective-permute-start.12 = (f32[656,128]{1,0:T(8,128)S(1)}, f32[656,128]{1,0:T(8,128)S(1)}, u32[]{:S(2)}, u32[]{:S(2)}) collective-permute-start(f32[656,128]{1,0:T(8,128)S(1)} %collective-permute-done.10.refs_5_), channel_id=1, source_target_pairs={{0,2},{1,3},{2,0},{3,1},{4,6},{5,7},{6,4},{7,5},{8,10},{9,11},{10,... | collective-permute-start | bytes 1007624 | tf_op jit(solution)/shard_map/ppermute | solution.py:633
  43.1 0.0 collective-permute-done.8.refs_2_
  43.1 2.0 %collective-permute-start.9 = (f32[656,128]{1,0:T(8,128)S(1)}, f32[656,128]{1,0:T(8,128)S(1)}, u32[]{:S(2)}, u32[]{:S(2)}) collective-permute-start(f32[656,128]{1,0:T(8,128)S(1)} %collective-permute-done.8.refs_2_), channel_id=1, source_target_pairs={{0,1},{1,0},{2,3},{3,2},{4,5},{5,4},{6,7},{7,6},{8,9},{9,8},{10,11... | collective-permute-start | bytes 1007624 | tf_op jit(solution)/shard_map/ppermute | solution.py:633
  45.1 5.2 %collective-permute-done.11.refs_6_ = f32[656,128]{1,0:T(8,128)S(1)} collective-permute-done((f32[656,128]{1,0:T(8,128)S(1)}, f32[656,128]{1,0:T(8,128)S(1)}, u32[]{:S(2)}, u32[]{:S(2)}) %collective-permute-start.11) | collective-permute-done | bytes 335904 | tf_op jit(solution)/shard_map/ppermute | solution.py:633
  50.3 0.0 collective-permute-done.7.refs_1_
  50.3 6.3 %collective-permute-done.12.refs_7_ = f32[656,128]{1,0:T(8,128)S(1)} collective-permute-done((f32[656,128]{1,0:T(8,128)S(1)}, f32[656,128]{1,0:T(8,128)S(1)}, u32[]{:S(2)}, u32[]{:S(2)}) %collective-permute-start.12) | collective-permute-done | bytes 335904 | tf_op jit(solution)/shard_map/ppermute | solution.py:633
  56.6 0.0 collective-permute-done.9.refs_3_
  56.6 6.8 %shard_map.31 = (f32[32,128,128]{2,1,0:T(8,128)S(1)}, bf16[1024,1024]{1,0:T(8,128)(2,1)S(1)}, bf16[1024,1024]{1,0:T(8,128)(2,1)S(1)}, f32[8,1024]{1,0:T(8,128)S(...) custom-call(s32[2]{0:T(128)S(1)} %pad_add_fusion.ids, ...), custom_call_target="tpu_custom_call" | custom-call | flops 6442450944 | tf_op jit(solution)/shard_map/pallas_call | solution.py:582
  63.4 0.1 collective-permute-start.13
  63.5 1.6 %collective-permute-start.14 = (f32[136,128]{1,0:T(8,128)S(1)}, f32[136,128]{1,0:T(8,128)S(1)}, u32[]{:S(2)}, u32[]{:S(2)}) collective-permute-start(f32[136,128]{1,0:T(8,128)S(1)} %get-tuple-element.55.refs_0_), channel_id=1, source_target_pairs={{0,16},{8,24},{16,0},{24,8},{1,17},{9,25},{17,1},{25,9},{2,18},{10... | collective-permute-start | bytes 208904 | tf_op jit(solution)/shard_map/ppermute | solution.py:595
  65.1 0.3 collective-permute-start.15
  65.4 4.3 %shard_map.33 = (f32[32,128,128]{2,1,0:T(8,128)S(1)}, f32[32,128,128]{2,1,0:T(8,128)S(1)}) custom-call(f32[32,128,128]{2,1,0:T(8,128)S(1)} %get-tuple-element.63.m_ref.refs_4_, bf16[1024,1024]{1,0:T(8,128)(2,1)S(1)} %get-tuple-element.64.mh, bf16[1024,1024]{1,0:T(8,128)(2,1)S(1)} %get-tuple-element.65.ml, f32[32,128,128]{2,1,0:T(8,128)S(1)} %get-tuple-element.66.s_ref, ...), custom_call_target="tpu_custom_call" | custom-call | flops 6442450944 | tf_op jit(solution)/shard_map/pallas_call | solution.py:582
  69.7 0.0 collective-permute-done.13.refs_1_
  69.7 0.0 collective-permute-done.14.refs_2_
  69.8 0.0 collective-permute-done.15.refs_3_
  69.8 2.3 %shard_map.32 = (f32[8,128]{1,0:T(8,128)S(1)}, f32[4,128,128]{2,1,0:T(8,128)S(1)}, f32[4,128,128]{2,1,0:T(8,128)S(1)}, f32[4,128,128]{2,1,0:T(8,128)S(1)}, f32[4...) custom-call(s32[2]{0:T(128)S(1)} %pad_add_fusion.ids, s32[4,9]{1,0:T(4,128)S(1)} %maximum_convert_fusion.lists, ...), custom_call_target="tpu_custom_call" | custom-call | flops 1610612736 | tf_op jit(solution)/shard_map/pallas_call | solution.py:582
  72.1 1.8 %collective-permute-start.16 = (f32[136,128]{1,0:T(8,128)S(1)}, f32[136,128]{1,0:T(8,128)S(1)}, u32[]{:S(2)}, u32[]{:S(2)}) collective-permute-start(f32[136,128]{1,0:T(8,128)S(1)} %get-tuple-element.74.refs_1_.refs_4_), channel_id=1, source_target_pairs={{0,2},{1,3},{2,4},{3,5},{4,6},{5,7},{6,0},{7,1},{8,10},{9,11},{10,... | collective-permute-start | bytes 208904 | tf_op jit(solution)/shard_map/ppermute | solution.py:639
  73.9 0.0 collective-permute-start.17
  73.9 2.4 %collective-permute-start.18 = (f32[136,128]{1,0:T(8,128)S(1)}, f32[136,128]{1,0:T(8,128)S(1)}, u32[]{:S(2)}, u32[]{:S(2)}) collective-permute-start(f32[136,128]{1,0:T(8,128)S(1)} %get-tuple-element.74.refs_1_.refs_4_), channel_id=1, source_target_pairs={{0,6},{1,7},{2,0},{3,1},{4,2},{5,3},{6,4},{7,5},{8,14},{9,15},{10,... | collective-permute-start | bytes 208904 | tf_op jit(solution)/shard_map/ppermute | solution.py:639
  76.3 7.3 %shard_map.34 = (f32[32,128,128]{2,1,0:T(8,128)S(1)}, bf16[1024,1024]{1,0:T(8,128)(2,1)S(1)}, bf16[1024,1024]{1,0:T(8,128)(2,1)S(1)}, f32[32,128,128]{2,1,0:T(8,...) custom-call(s32[2]{0:T(128)S(1)} %pad_add_fusion.ids, ...), custom_call_target="tpu_custom_call" | custom-call | flops 6442450944 | tf_op jit(solution)/shard_map/pallas_call | solution.py:582
  83.6 0.0 collective-permute-done.16.refs_5_
  83.6 0.0 collective-permute-done.17.refs_6_
  83.6 0.0 collective-permute-done.18.refs_7_
  83.6 0.1 collective-permute-start.19
  83.7 1.6 %collective-permute-start.20 = (f32[136,128]{1,0:T(8,128)S(1)}, f32[136,128]{1,0:T(8,128)S(1)}, u32[]{:S(2)}, u32[]{:S(2)}) collective-permute-start(f32[136,128]{1,0:T(8,128)S(1)} %get-tuple-element.73.refs_0_), channel_id=1, source_target_pairs={{0,16},{8,24},{16,0},{24,8},{1,17},{9,25},{17,1},{25,9},{2,18},{10... | collective-permute-start | bytes 208904 | tf_op jit(solution)/shard_map/ppermute | solution.py:595
  85.3 0.3 collective-permute-start.21
  85.6 0.4 collective-permute-start.22
  86.0 1.7 %collective-permute-start.23 = (f32[136,128]{1,0:T(8,128)S(1)}, f32[136,128]{1,0:T(8,128)S(1)}, u32[]{:S(2)}, u32[]{:S(2)}) collective-permute-start(f32[136,128]{1,0:T(8,128)S(1)} %collective-permute-done.16.refs_5_), channel_id=1, source_target_pairs={{0,1},{1,0},{2,3},{3,2},{4,5},{5,4},{6,7},{7,6},{8,9},{9,8},{10,11... | collective-permute-start | bytes 208904 | tf_op jit(solution)/shard_map/ppermute | solution.py:646
  87.6 0.0 collective-permute-done.19.refs_1_
  87.6 0.4 collective-permute-start.24
  88.0 0.4 collective-permute-done.20.refs_2_
  88.4 1.3 %collective-permute-start.25 = (f32[136,128]{1,0:T(8,128)S(1)}, f32[136,128]{1,0:T(8,128)S(1)}, u32[]{:S(2)}, u32[]{:S(2)}) collective-permute-start(f32[136,128]{1,0:T(8,128)S(1)} %collective-permute-done.18.refs_7_), channel_id=1, source_target_pairs={{0,1},{1,0},{2,3},{3,2},{4,5},{5,4},{6,7},{7,6},{8,9},{9,8},{10,11... | collective-permute-start | bytes 208904 | tf_op jit(solution)/shard_map/ppermute | solution.py:646
  89.7 4.3 %shard_map.35 = (f32[32,128,128]{2,1,0:T(8,128)S(1)}, f32[32,128,128]{2,1,0:T(8,128)S(1)}) custom-call(f32[32,128,128]{2,1,0:T(8,128)S(1)} %get-tuple-element.78.m_ref.refs_14_, bf16[1024,1024]{1,0:T(8,128)(2,1)S(1)} %get-tuple-element.79.mh, bf16[1024,1024]{1,0:T(8,128)(2,1)S(1)} %get-tuple-element.80.ml, f32[32,128,128]{2,1,0:T(8,128)S(1)} %get-tuple-element.81.s_ref, ...), custom_call_target="tpu_custom_call" | custom-call | flops 6442450944 | tf_op jit(solution)/shard_map/pallas_call | solution.py:582
  94.0 0.0 collective-permute-done.22.refs_8_
  94.0 0.0 collective-permute-done.23.refs_9_
  94.1 0.4 collective-permute-done.25.refs_11_
  94.5 5.7 %shard_map.36 = (f32[9,128,128]{2,1,0:T(8,128)S(1)}, f32[9,128,128]{2,1,0:T(8,128)S(1)}, f32[8,128]{1,0:T(8,128)S(1)}) custom-call(s32[2]{0:T(128)S(1)} %pad_add_fusion.ids, s32[4,9]{1,0:T(4,128)S(1)} %maximum_convert_fusion.lists, f32[136,128]{1,0:T(8,128)S(1)} %get-tuple-element.73.refs_0_, f32[136,128]{1,0:T(8,128)S(1)} %collective-permute-done.19.refs_1_, ...), custom_call_target="tpu_custom_call" | custom-call | tf_op jit(solution)/shard_map/pallas_call | solution.py:582
  100.2 10.3 %all_to_all.8 = f32[32,1,128]{2,1,0:T(1,128)S(1)} all-to-all(f32[32,1,128]{2,1,0:T(1,128)S(1)} %broadcast_in_dim.2), channel_id=1, replica_groups=mesh['row'=4,'col'=8] {'row','col'}, dimensions={0} | all-to-all | bytes 32768 | tf_op jit(solution)/shard_map/all_to_all | solution.py:741
  110.5 1.6 %shard_map.37 = f32[1,9,128,128]{3,2,1,0:T(8,128)} custom-call(s32[4,9]{1,0:T(4,128)S(1)} %maximum_convert_fusion.lists, s32[2]{0:T(128)S(1)} %pad_add_fusion.ids, f32[32,128]{1,0:T(8,128)S(1)} %bitcast.7, f32[9,128,128]{2,1,0:T(8,128)S(1)} %get-tuple-element.91.x_ref, f32[9,128,128]{2,1,0:T(8,128)S(1)} %get-tuple-element.92.y_ref), custom_call_target="tpu_custom_call" | custom-call | tf_op jit(solution)/shard_map/pallas_call | solution.py:582
  (12 shorter events, 0.1 us)
Async XLA Ops:
  0.1 1.1 copy-start
  1.1 0.7 copy-start.1
  2.4 5.3 %collective-permute-start = (f32[392,128]{1,0:T(8,128)S(1)}, f32[392,128]{1,0:T(8,128)S(1)}, u32[]{:S(2)}, u32[]{:S(2)}) collective-permute-start(f32[392,128]{1,0:T(8,128)S(1)} %get-tuple-element.49.refs_0_), channel_id=1, source_target_pairs={{0,8},{8,0},{16,24},{24,16},{1,9},{9,1},{17,25},{25,17},{2,10},{10... | collective-permute-start | bytes 602120 | tf_op jit(solution)/shard_map/ppermute | solution.py:595
  2.9 23.6 %collective-permute-start.3 = (f32[904,128]{1,0:T(8,128)S(1)}, f32[904,128]{1,0:T(8,128)S(1)}, u32[]{:S(2)}, u32[]{:S(2)}) collective-permute-start(f32[904,128]{1,0:T(8,128)S(1)} %get-tuple-element.50.own), channel_id=1, source_target_pairs={{6,1},{7,0},{14,9},{15,8},{22,17},{23,16},{30,25},{31,24}} | collective-permute-start | bytes 1388552 | tf_op jit(solution)/shard_map/ppermute | solution.py:603
  4.2 10.6 %collective-permute-start.1 = (f32[392,128]{1,0:T(8,128)S(1)}, f32[392,128]{1,0:T(8,128)S(1)}, u32[]{:S(2)}, u32[]{:S(2)}) collective-permute-start(f32[392,128]{1,0:T(8,128)S(1)} %get-tuple-element.49.refs_0_), channel_id=1, source_target_pairs={{0,16},{8,24},{16,0},{24,8},{1,17},{9,25},{17,1},{25,9},{2,18},{10... | collective-permute-start | bytes 602120 | tf_op jit(solution)/shard_map/ppermute | solution.py:595
  6.8 9.7 %collective-permute-start.2 = (f32[392,128]{1,0:T(8,128)S(1)}, f32[392,128]{1,0:T(8,128)S(1)}, u32[]{:S(2)}, u32[]{:S(2)}) collective-permute-start(f32[392,128]{1,0:T(8,128)S(1)} %get-tuple-element.49.refs_0_), channel_id=1, source_target_pairs={{0,24},{8,16},{16,8},{24,0},{1,25},{9,17},{17,9},{25,1},{2,26},{10... | collective-permute-start | bytes 602120 | tf_op jit(solution)/shard_map/ppermute | solution.py:595
  7.0 19.5 %collective-permute-start.4 = (f32[648,128]{1,0:T(8,128)S(1)}, f32[648,128]{1,0:T(8,128)S(1)}, u32[]{:S(2)}, u32[]{:S(2)}) collective-permute-start(f32[648,128]{1,0:T(8,128)S(1)} %slice.25), channel_id=1, source_target_pairs={{4,3},{5,2},{12,11},{13,10},{20,19},{21,18},{28,27},{29,26}} | collective-permute-start | bytes 995336 | tf_op jit(solution)/shard_map/ppermute | solution.py:604
  7.7 15.9 %collective-permute-start.5 = (f32[520,128]{1,0:T(8,128)S(1)}, f32[520,128]{1,0:T(8,128)S(1)}, u32[]{:S(2)}, u32[]{:S(2)}) collective-permute-start(f32[520,128]{1,0:T(8,128)S(1)} %get-tuple-element.51), channel_id=1, source_target_pairs={{0,7},{1,6},{2,5},{3,4},{8,15},{9,14},{10,13},{11,12},{16,23},{17,... | collective-permute-start | bytes 798728 | tf_op jit(solution)/shard_map/ppermute | solution.py:607
  18.6 7.9 %collective-permute-start.6 = (f32[136,128]{1,0:T(8,128)S(1)}, f32[136,128]{1,0:T(8,128)S(1)}, u32[]{:S(2)}, u32[]{:S(2)}) collective-permute-start(f32[136,128]{1,0:T(8,128)S(1)} %get-tuple-element.52.own_pack.refs_8_), channel_id=1, source_target_pairs={{0,7},{1,6},{2,5},{3,4},{4,3},{5,2},{6,1},{7,0},{8,15},{9,14},{10,... | collective-permute-start | bytes 208904 | tf_op jit(solution)/shard_map/ppermute | solution.py:608
  27.2 10.1 %collective-permute-start.10 = (f32[656,128]{1,0:T(8,128)S(1)}, f32[656,128]{1,0:T(8,128)S(1)}, u32[]{:S(2)}, u32[]{:S(2)}) collective-permute-start(f32[656,128]{1,0:T(8,128)S(1)} %get-tuple-element.54.refs_4_), channel_id=1, source_target_pairs={{0,1},{1,0},{2,3},{3,2},{4,5},{5,4},{6,7},{7,6},{8,9},{9,8},{10,11... | collective-permute-start | bytes 1007624 | tf_op jit(solution)/shard_map/ppermute | solution.py:633
  28.7 14.4 %collective-permute-start.8 = (f32[656,128]{1,0:T(8,128)S(1)}, f32[656,128]{1,0:T(8,128)S(1)}, u32[]{:S(2)}, u32[]{:S(2)}) collective-permute-start(f32[656,128]{1,0:T(8,128)S(1)} %get-tuple-element.53.refs_0_), channel_id=1, source_target_pairs={{0,2},{1,3},{2,0},{3,1},{4,6},{5,7},{6,4},{7,5},{8,10},{9,11},{10,... | collective-permute-start | bytes 1007624 | tf_op jit(solution)/shard_map/ppermute | solution.py:633
  34.4 15.9 %collective-permute-start.11 = (f32[656,128]{1,0:T(8,128)S(1)}, f32[656,128]{1,0:T(8,128)S(1)}, u32[]{:S(2)}, u32[]{:S(2)}) collective-permute-start(f32[656,128]{1,0:T(8,128)S(1)} %get-tuple-element.54.refs_4_), channel_id=1, source_target_pairs={{0,2},{1,3},{2,0},{3,1},{4,6},{5,7},{6,4},{7,5},{8,10},{9,11},{10,... | collective-permute-start | bytes 1007624 | tf_op jit(solution)/shard_map/ppermute | solution.py:633
  34.4 15.9 %collective-permute-start.7 = (f32[656,128]{1,0:T(8,128)S(1)}, f32[656,128]{1,0:T(8,128)S(1)}, u32[]{:S(2)}, u32[]{:S(2)}) collective-permute-start(f32[656,128]{1,0:T(8,128)S(1)} %get-tuple-element.53.refs_0_), channel_id=1, source_target_pairs={{0,1},{1,0},{2,3},{3,2},{4,5},{5,4},{6,7},{7,6},{8,9},{9,8},{10,11... | collective-permute-start | bytes 1007624 | tf_op jit(solution)/shard_map/ppermute | solution.py:633
  37.2 19.4 %collective-permute-start.12 = (f32[656,128]{1,0:T(8,128)S(1)}, f32[656,128]{1,0:T(8,128)S(1)}, u32[]{:S(2)}, u32[]{:S(2)}) collective-permute-start(f32[656,128]{1,0:T(8,128)S(1)} %collective-permute-done.10.refs_5_), channel_id=1, source_target_pairs={{0,2},{1,3},{2,0},{3,1},{4,6},{5,7},{6,4},{7,5},{8,10},{9,11},{10,... | collective-permute-start | bytes 1007624 | tf_op jit(solution)/shard_map/ppermute | solution.py:633
  43.1 13.5 %collective-permute-start.9 = (f32[656,128]{1,0:T(8,128)S(1)}, f32[656,128]{1,0:T(8,128)S(1)}, u32[]{:S(2)}, u32[]{:S(2)}) collective-permute-start(f32[656,128]{1,0:T(8,128)S(1)} %collective-permute-done.8.refs_2_), channel_id=1, source_target_pairs={{0,1},{1,0},{2,3},{3,2},{4,5},{5,4},{6,7},{7,6},{8,9},{9,8},{10,11... | collective-permute-start | bytes 1007624 | tf_op jit(solution)/shard_map/ppermute | solution.py:633
  63.4 6.3 %collective-permute-start.13 = (f32[136,128]{1,0:T(8,128)S(1)}, f32[136,128]{1,0:T(8,128)S(1)}, u32[]{:S(2)}, u32[]{:S(2)}) collective-permute-start(f32[136,128]{1,0:T(8,128)S(1)} %get-tuple-element.55.refs_0_), channel_id=1, source_target_pairs={{0,8},{8,0},{16,24},{24,16},{1,9},{9,1},{17,25},{25,17},{2,10},{10... | collective-permute-start | bytes 208904 | tf_op jit(solution)/shard_map/ppermute | solution.py:595
  63.5 6.2 %collective-permute-start.14 = (f32[136,128]{1,0:T(8,128)S(1)}, f32[136,128]{1,0:T(8,128)S(1)}, u32[]{:S(2)}, u32[]{:S(2)}) collective-permute-start(f32[136,128]{1,0:T(8,128)S(1)} %get-tuple-element.55.refs_0_), channel_id=1, source_target_pairs={{0,16},{8,24},{16,0},{24,8},{1,17},{9,25},{17,1},{25,9},{2,18},{10... | collective-permute-start | bytes 208904 | tf_op jit(solution)/shard_map/ppermute | solution.py:595
  65.1 4.7 %collective-permute-start.15 = (f32[136,128]{1,0:T(8,128)S(1)}, f32[136,128]{1,0:T(8,128)S(1)}, u32[]{:S(2)}, u32[]{:S(2)}) collective-permute-start(f32[136,128]{1,0:T(8,128)S(1)} %get-tuple-element.55.refs_0_), channel_id=1, source_target_pairs={{0,24},{8,16},{16,8},{24,0},{1,25},{9,17},{17,9},{25,1},{2,26},{10... | collective-permute-start | bytes 208904 | tf_op jit(solution)/shard_map/ppermute | solution.py:595
  72.1 11.5 %collective-permute-start.16 = (f32[136,128]{1,0:T(8,128)S(1)}, f32[136,128]{1,0:T(8,128)S(1)}, u32[]{:S(2)}, u32[]{:S(2)}) collective-permute-start(f32[136,128]{1,0:T(8,128)S(1)} %get-tuple-element.74.refs_1_.refs_4_), channel_id=1, source_target_pairs={{0,2},{1,3},{2,4},{3,5},{4,6},{5,7},{6,0},{7,1},{8,10},{9,11},{10,... | collective-permute-start | bytes 208904 | tf_op jit(solution)/shard_map/ppermute | solution.py:639
  73.9 9.7 %collective-permute-start.17 = (f32[136,128]{1,0:T(8,128)S(1)}, f32[136,128]{1,0:T(8,128)S(1)}, u32[]{:S(2)}, u32[]{:S(2)}) collective-permute-start(f32[136,128]{1,0:T(8,128)S(1)} %get-tuple-element.74.refs_1_.refs_4_), channel_id=1, source_target_pairs={{0,4},{1,5},{2,6},{3,7},{4,0},{5,1},{6,2},{7,3},{8,12},{9,13},{10,... | collective-permute-start | bytes 208904 | tf_op jit(solution)/shard_map/ppermute | solution.py:639
  73.9 9.7 %collective-permute-start.18 = (f32[136,128]{1,0:T(8,128)S(1)}, f32[136,128]{1,0:T(8,128)S(1)}, u32[]{:S(2)}, u32[]{:S(2)}) collective-permute-start(f32[136,128]{1,0:T(8,128)S(1)} %get-tuple-element.74.refs_1_.refs_4_), channel_id=1, source_target_pairs={{0,6},{1,7},{2,0},{3,1},{4,2},{5,3},{6,4},{7,5},{8,14},{9,15},{10,... | collective-permute-start | bytes 208904 | tf_op jit(solution)/shard_map/ppermute | solution.py:639
  83.6 4.0 %collective-permute-start.19 = (f32[136,128]{1,0:T(8,128)S(1)}, f32[136,128]{1,0:T(8,128)S(1)}, u32[]{:S(2)}, u32[]{:S(2)}) collective-permute-start(f32[136,128]{1,0:T(8,128)S(1)} %get-tuple-element.73.refs_0_), channel_id=1, source_target_pairs={{0,8},{8,0},{16,24},{24,16},{1,9},{9,1},{17,25},{25,17},{2,10},{10... | collective-permute-start | bytes 208904 | tf_op jit(solution)/shard_map/ppermute | solution.py:595
  83.7 4.7 %collective-permute-start.20 = (f32[136,128]{1,0:T(8,128)S(1)}, f32[136,128]{1,0:T(8,128)S(1)}, u32[]{:S(2)}, u32[]{:S(2)}) collective-permute-start(f32[136,128]{1,0:T(8,128)S(1)} %get-tuple-element.73.refs_0_), channel_id=1, source_target_pairs={{0,16},{8,24},{16,0},{24,8},{1,17},{9,25},{17,1},{25,9},{2,18},{10... | collective-permute-start | bytes 208904 | tf_op jit(solution)/shard_map/ppermute | solution.py:595
  85.3 8.7 %collective-permute-start.21 = (f32[136,128]{1,0:T(8,128)S(1)}, f32[136,128]{1,0:T(8,128)S(1)}, u32[]{:S(2)}, u32[]{:S(2)}) collective-permute-start(f32[136,128]{1,0:T(8,128)S(1)} %get-tuple-element.73.refs_0_), channel_id=1, source_target_pairs={{0,24},{8,16},{16,8},{24,0},{1,25},{9,17},{17,9},{25,1},{2,26},{10... | collective-permute-start | bytes 208904 | tf_op jit(solution)/shard_map/ppermute | solution.py:595
  85.6 8.4 %collective-permute-start.22 = (f32[136,128]{1,0:T(8,128)S(1)}, f32[136,128]{1,0:T(8,128)S(1)}, u32[]{:S(2)}, u32[]{:S(2)}) collective-permute-start(f32[136,128]{1,0:T(8,128)S(1)} %get-tuple-element.74.refs_1_.refs_4_), channel_id=1, source_target_pairs={{0,1},{1,0},{2,3},{3,2},{4,5},{5,4},{6,7},{7,6},{8,9},{9,8},{10,11... | collective-permute-start | bytes 208904 | tf_op jit(solution)/shard_map/ppermute | solution.py:646
  86.0 8.1 %collective-permute-start.23 = (f32[136,128]{1,0:T(8,128)S(1)}, f32[136,128]{1,0:T(8,128)S(1)}, u32[]{:S(2)}, u32[]{:S(2)}) collective-permute-start(f32[136,128]{1,0:T(8,128)S(1)} %collective-permute-done.16.refs_5_), channel_id=1, source_target_pairs={{0,1},{1,0},{2,3},{3,2},{4,5},{5,4},{6,7},{7,6},{8,9},{9,8},{10,11... | collective-permute-start | bytes 208904 | tf_op jit(solution)/shard_map/ppermute | solution.py:646
  87.6 6.4 %collective-permute-start.24 = (f32[136,128]{1,0:T(8,128)S(1)}, f32[136,128]{1,0:T(8,128)S(1)}, u32[]{:S(2)}, u32[]{:S(2)}) collective-permute-start(f32[136,128]{1,0:T(8,128)S(1)} %collective-permute-done.17.refs_6_), channel_id=1, source_target_pairs={{0,1},{1,0},{2,3},{3,2},{4,5},{5,4},{6,7},{7,6},{8,9},{9,8},{10,11... | collective-permute-start | bytes 208904 | tf_op jit(solution)/shard_map/ppermute | solution.py:646
  88.4 6.1 %collective-permute-start.25 = (f32[136,128]{1,0:T(8,128)S(1)}, f32[136,128]{1,0:T(8,128)S(1)}, u32[]{:S(2)}, u32[]{:S(2)}) collective-permute-start(f32[136,128]{1,0:T(8,128)S(1)} %collective-permute-done.18.refs_7_), channel_id=1, source_target_pairs={{0,1},{1,0},{2,3},{3,2},{4,5},{5,4},{6,7},{7,6},{8,9},{9,8},{10,11... | collective-permute-start | bytes 208904 | tf_op jit(solution)/shard_map/ppermute | solution.py:646

commit v4 on v3

--- a/solution.py
+++ b/solution.py
@@ -68,11 +68,9 @@
 
 
 PAIR = 8
-FEW, SOME, ALL = 4, 5, 7
-FRONT = 5
-NAMES = FRONT * BW
-TERMS = 16 + PAIR * BW
-HALF = NAMES + 16
+FEW, ALL = 4, 7
+FRONT = 8 + FEW * BW
+TERMS = FRONT + (PAIR - FEW) * BW + 8
 
 
 @functools.lru_cache
@@ -81,7 +79,7 @@
     for b in range(nq):
         out.append([t for t, d in enumerate(offsets(b, nq)) if (b + d) % nq <= b])
     for b in range(nq // 2):
-        assert len(out[b]) <= FEW and len(out[b]) + len(out[nq - 1 - b]) == PAIR
+        assert len(out[b]) <= FEW <= len(out[nq - 1 - b]) == PAIR - len(out[b])
     return out
 
 
@@ -154,16 +152,16 @@
     return slice(q * BW, (q + 1) * BW)
 
 
-def settle(nq, q, parts, held, rows=slice(None)):
+def settle(nq, q, parts, held, start=0, size=PACK):
     if len(parts) == 1:
         for k in range(nq):
-            held[k] = parts[0][k, rows, :]
+            held[k] = parts[0][k, start : start + size, :]
         return
     half = nq // 2
     for k in range(half):
-        for side in range(2):
-            source = lax.rem((q ^ side) + (nq - 2 * k), jnp.int32(nq))
-            held[source] = parts[half * side + k][rows, :]
+        held[q ^ (2 * k)] = parts[k][start : start + size, :]
+        far = k * PACK + start
+        held[q ^ (2 * k + 1)] = parts[half][far : far + size, :]
 
 
 def put_dense(hi_ref, lo_ref, a, b, block):
@@ -248,23 +246,20 @@
     return out
 
 
-def prepare_kernel(nq, ids, names, blocks, most, few, row):
-    q = ids[1]
-    lane = lax.broadcasted_iota(jnp.int32, (1, BW), 1)
-    listed = jnp.zeros((1, BW), f32)
-    for t in range(names.shape[1]):
-        listed = jnp.where(lane == t, names[0, t].astype(f32), listed)
-    listed = jnp.broadcast_to(listed, (8, BW))
-    most[0:8, :] = listed
-    few[0:8, :] = listed
+def prepare_kernel(nq, names, blocks, few, rest, row):
+    q = lax.axis_index("col")
+    lists = names[...].astype(f32)
+    for ref, start in ((few, 0), (row, 3 * BW)):
+        ref[start : start + 8, :] = jnp.zeros((8, BW), f32)
+        ref[start : start + 1, 0 : names.shape[1]] = lists
     for i in range(ALL):
         block = blocks[choose(q, [(slots + [0] * ALL)[i] for slots in stored(nq)])]
-        most[place(i), :] = block
         if i < FEW:
             few[place(i), :] = block
+        else:
+            rest[cut(i - FEW), :] = block
     for i, t in enumerate((0, NEAR, NEAR + 1)):
         row[cut(i), :] = blocks[t]
-    row[3 * BW :, :] = listed
 
 
 def place(i):
@@ -276,62 +271,55 @@
 
 
 def lay(i):
-    start = i * BW + (16 if i >= FRONT else 0)
-    return slice(start, start + BW)
-
-
-def pair_kernel(nq, ids, own, all_in, some_in, few_in, own_pack, pack_in, front, back):
-    q = ids[1]
+    return place(i) if i < FEW else cut_from(FRONT, i - FEW)
+
+
+def cut_from(start, i):
+    return slice(start + i * BW, start + (i + 1) * BW)
+
+
+def back_kernel(nq, few, rest, few_in, rest_in, own_pack, pack_in, back):
+    q = lax.axis_index("col")
     upper = q >= nq // 2
-    count = choose(jnp.where(upper, nq - 1 - q, q), counts(nq))
+    count = choose(jnp.where(upper, nq - 1 - q, q), counts(nq)) - FEW
 
     def fill(first, second):
-        for i in range(PAIR):
-            out, rows = (front, lay(i)) if i < FRONT else (back, cut(i - FRONT))
-            if i < FEW:
-                out[rows, :] = first[place(i), :]
-                continue
-            if i < (first.shape[0] - 8) // BW:
+        for i in range(PAIR - FEW):
+            if i < ALL - FEW:
 
                 @pl.when(i < count)
-                def _(out=out, rows=rows, i=i):
-                    out[rows, :] = first[place(i), :]
+                def _():
+                    back[cut(i), :] = first[cut(i), :]
 
             @pl.when(i >= count)
-            def _(out=out, rows=rows, i=i):
-                out[rows, :] = second[at_place(i - count), :]
-
-        front[NAMES : NAMES + 8, :] = first[0:8, :]
-        front[NAMES + 8 : NAMES + 16, :] = second[0:8, :]
-
-    wide = count > SOME
+            def _():
+                back[cut(i), :] = second[at_place(i - count), :]
+
+        end = (PAIR - FEW) * BW
+        back[end : end + 8, :] = second[0:8, :]
 
     @pl.when(upper)
     def _():
-        fill(own, few_in)
-
-    @pl.when(jnp.logical_and(jnp.logical_not(upper), wide))
+        fill(rest, few_in)
+
+    @pl.when(jnp.logical_not(upper))
     def _():
-        fill(all_in, own)
-
-    @pl.when(jnp.logical_and(jnp.logical_not(upper), jnp.logical_not(wide)))
-    def _():
-        fill(some_in, own)
-
-    terms = (PAIR - FRONT) * BW
+        fill(rest_in, few)
+
+    terms = TERMS - FRONT
     back[terms : terms + PACK, :] = jnp.where(upper, own_pack[...], pack_in[...])
     back[terms + PACK :, :] = jnp.where(upper, pack_in[...], own_pack[...])
 
 
-def first_kernel(nq, ids, *refs):
+def first_kernel(nq, *refs):
     half = nq // 2
     fronts, backs, refs = refs[:half], refs[half:nq], refs[nq:]
     own_pack, m_ref, mh, ml, link, s_ref, sh, sl, out_ref, packs, near = refs
-    q = ids[1]
+    q = lax.axis_index("col")
     own = jnp.minimum(q, nq - 1 - q)
     for m in range(half):
-        near[m ^ own, 0:HALF, :] = fronts[m][...]
-        near[m ^ own, HALF:, :] = backs[m][...]
+        near[m ^ own, 0:FRONT, :] = fronts[m][...]
+        near[m ^ own, FRONT:, :] = backs[m][...]
     clear_unlinked(mh, ml, nq)
     link[...] = jnp.zeros_like(link)
     index = pair_index(nq)
@@ -343,7 +331,7 @@
             m_ref[index[pair]] = block
             put_dense(mh, ml, *pair, block)
     for a in range(nq):
-        row = NAMES if a >= half else NAMES + 8
+        row = 0 if a >= half else TERMS - 8
         listed = near[min(a, nq - 1 - a), row : row + 1, :]
         present = jnp.where(listed >= 0.0, 1.0, 0.0)
         for t, d in enumerate(offsets(a, nq)):
@@ -374,10 +362,10 @@
             put_dense(mh, ml, a, b, block)
 
 
-def next_kernel(nq, count, ids, coef, *refs):
+def next_kernel(nq, count, coef, *refs):
     packs, own_pack, refs = refs[:count], refs[count], refs[count + 1 :]
     x_ref, y_ref, m_old, link, m_ref, mh, ml, s_ref, sh, sl, out_ref, held = refs
-    q = ids[1]
+    q = lax.axis_index("col")
     assemble(nq, q, coef[0:1, :], coef[1:2, :], packs, x_ref, y_ref, m_old, held, m_ref, mh, ml)
     square_part(nq, q, own_pack, m_ref, mh, ml, link, s_ref, sh, sl, out_ref)
 
@@ -402,8 +390,8 @@
     return jnp.minimum(far, e), jnp.maximum(far, e)
 
 
-def cross_tail(nr, nq, ids, lists, d_ref, u_ref, su_ref, v_ref, pack_ref):
-    r = ids[0]
+def cross_tail(nr, nq, lists, d_ref, u_ref, su_ref, v_ref, pack_ref):
+    r = lax.axis_index("row")
     norm = jnp.zeros((BW, BW), f32)
     inner = jnp.zeros((BW, BW), f32)
     for e in range(nr):
@@ -434,10 +422,10 @@
     pack_ref[BW + 3 : BW + 8, :] = jnp.zeros((5, BW), f32)
 
 
-def cross_first_kernel(nr, nq, ids, lists, *refs):
+def cross_first_kernel(nr, nq, lists, *refs):
     parts, refs = refs[:nr], refs[nr:]
     d_ref, u_ref, su_ref, v_ref, pack_ref, row = refs
-    r = ids[0]
+    r = lax.axis_index("row")
     for k in range(nr):
         row[k ^ r] = parts[k][...]
     for e in range(nr):
@@ -447,11 +435,11 @@
         here = row[e, cut(2), :]
         there = row[far, cut(1), :]
         u_ref[e] = jnp.where(far < e, here, there)
-    cross_tail(nr, nq, ids, lists, d_ref, u_ref, su_ref, v_ref, pack_ref)
+    cross_tail(nr, nq, lists, d_ref, u_ref, su_ref, v_ref, pack_ref)
 
 
 def coefficient(nr, nq, q, rows, packs, held):
-    settle(nq, q, packs, held, slice(BW, BW + 8))
+    settle(nq, q, packs, held, BW, 8)
     trace = rows[0, BW + 1 : BW + 2, :]
     norm = rows[0, BW + 2 : BW + 3, :]
     inner = rows[0, BW + 3 : BW + 4, :]
@@ -466,13 +454,13 @@
     return c, 1.0 / (1.0 - c)
 
 
-def cross_kernel(nr, nq, count, ids, lists, *refs):
+def cross_kernel(nr, nq, count, lists, *refs):
     parts, packs, refs = refs[:nr], refs[nr : nr + count], refs[nr + count :]
     d_old, u_old, su_old, v_old, coef, d_ref, u_ref, su_ref, v_ref, pack_ref, held, rows = refs
-    r = ids[0]
+    r = lax.axis_index("row")
     for k in range(nr):
         rows[k ^ r] = parts[k][...]
-    c, inv = coefficient(nr, nq, ids[1], rows, packs, held)
+    c, inv = coefficient(nr, nq, lax.axis_index("col"), rows, packs, held)
     coef[0:1, :] = c
     coef[1:2, :] = inv
     coef[2:8, :] = jnp.zeros((6, BW), f32)
@@ -486,14 +474,14 @@
         u, su = u_old[e], su_old[e]
         k = dotf(u, s0) + v_old[e]
         u_ref[e] = ((1.0 - 2.0 * c) * u + (1.0 + c) * su - k) * inv
-    cross_tail(nr, nq, ids, lists, d_ref, u_ref, su_ref, v_ref, pack_ref)
-
-
-def last_kernel(nr, nq, count, ids, lists, *refs):
+    cross_tail(nr, nq, lists, d_ref, u_ref, su_ref, v_ref, pack_ref)
+
+
+def last_kernel(nr, nq, count, lists, *refs):
     parts, packs, refs = refs[:nr], refs[nr : nr + count], refs[nr + count :]
     x_old, y_old, m_old, link, d_old, u_old, su_old, v_old = refs[:8]
     x_out, y_out, sums, rows, ends, held, m_ref, mh, ml, col, sq = refs[8:]
-    r, q = ids[0], ids[1]
+    r, q = lax.axis_index("row"), lax.axis_index("col")
     for k in range(nr):
         rows[k ^ r] = parts[k][...]
     c, inv = coefficient(nr, nq, q, rows, packs, ends)
@@ -535,8 +523,13 @@
     sums[0:1, :] = total(jnp.where(i == j, d - s0, 0.0))
     sums[1:2, :] = total(jnp.where(i == j, s0 - k0, 0.0))
     sums[2:8, :] = jnp.zeros((6, BW), f32)
-    x_out[0] = (d + s0) - k0
-    y_out[0] = s0 - 2.0 * d
+
+    def put(t, p, s, k):
+        keep = jnp.logical_and(lists[0, t] >= 0, lists[0, t] <= lists[0, 0])
+        x_out[t] = jnp.where(keep, (p + s) - k, 0.0)
+        y_out[t] = jnp.where(keep, s - 2.0 * p, 0.0)
+
+    put(0, d, s0, k0)
     for t in range(1, NEAR):
         if t < 6:
             a = lax.rem(q + jnp.int32(offsets(0, nq)[t] + nq), jnp.int32(nq))
@@ -544,27 +537,21 @@
             step_3 = jnp.where(lax.rem(q, jnp.int32(2)) == 0, 3, nq - 3)
             a = lax.rem(q + step_3, jnp.int32(nq))
         m = mh[at(a), at(q)].astype(f32) + ml[at(a), at(q)].astype(f32)
-        s = sq[at(a), :]
-        x_out[t] = (m + s) - col[at(a), :]
-        y_out[t] = s - 2.0 * m
+        put(t, m, sq[at(a), :], col[at(a), :])
     s0 = split(s0)
     for slot, cu, scu, part in cross:
-        x_out[slot] = (cu + scu) - (dot3(*split(cu), *s0) + part)
-        y_out[slot] = scu - 2.0 * cu
-
-
-def finish_kernel(slots, lists, ids, parts, x_ref, y_ref, out_ref):
+        put(slot, cu, scu, dot3(*split(cu), *s0) + part)
+
+
+def finish_kernel(slots, parts, x_ref, y_ref, out_ref):
     sums = jnp.sum(parts[...], axis=0, keepdims=True)
     half = BW // 2
     low = jnp.broadcast_to(sums[:, 0:1], (1, BW))
     high = jnp.broadcast_to(sums[:, half : half + 1], (1, BW))
     c = high / low
     inv = 1.0 / (1.0 - c)
-    own = lists[0, 0]
     for t in range(slots):
-        a = lists[0, t]
-        keep = jnp.logical_and(a >= 0, a <= own)
-        out_ref[0, t] = jnp.where(keep, (x_ref[t] + c * y_ref[t]) * inv, 0.0)
+        out_ref[0, t] = (x_ref[t] + c * y_ref[t]) * inv
 
 
 def room(args, outs, scratch):
@@ -596,25 +583,25 @@
     ]
 
 
-def gather_pairs(most, few, own_pack, ids, nq):
+def gather_pairs(few, rest, own_pack, nq):
     half = nq // 2
-    size = [len(slots) for slots in stored(nq)]
-    far = lambda keep: [(i, nq - 1 - i) for i in range(nq) if keep(i)]
-    all_in = lax.ppermute(most, "col", far(lambda i: i >= half and size[i] > SOME))
-    some_in = lax.ppermute(
-        most[: 8 + SOME * BW], "col", far(lambda i: i >= half and size[i] <= SOME)
-    )
-    few_in = lax.ppermute(few, "col", far(lambda i: i < half))
-    pack_in = lax.ppermute(own_pack, "col", far(lambda i: True))
-    front, back = call(
-        functools.partial(pair_kernel, nq),
-        [((HALF, BW), f32), ((TERMS + 2 * PACK - HALF, BW), f32)],
-        (ids, most, all_in, some_in, few_in, own_pack, pack_in),
-        1,
-    )
-    backs = tree_gather(back, "col", half, drop_high, nq // half)
-    fronts = tree_gather(front, "col", half, drop_low, nq // half)
-    return fronts + backs
+    more = [len(slots) > FEW for slots in stored(nq)]
+    mirror = [(i, nq - 1 - i) for i in range(nq)]
+    few_in = lax.ppermute(few, "col", mirror)
+    rest_in = lax.ppermute(rest, "col", [pair for pair in mirror if more[pair[0]]])
+    pack_in = lax.ppermute(own_pack, "col", mirror)
+    front = jnp.where(lax.axis_index("col") >= half, few, few_in)
+    fronts = tree_gather(front, "col", half, drop_low, 2, levels=1)
+    rest_in, fronts = lax.optimization_barrier((rest_in, fronts))
+    (back,) = call(
+        functools.partial(back_kernel, nq),
+        [((TERMS + 2 * PACK - FRONT, BW), f32)],
+        (few, rest, few_in, rest_in, own_pack, pack_in),
+        0,
+    )
+    backs = tree_gather(back, "col", half, drop_high, 2)
+    fronts = tree_gather(front, "col", half, drop_low, 2, fronts)
+    return [got[m] for got in (fronts, backs) for m in range(half)]
 
 
 def drop_low(m):
@@ -625,26 +612,26 @@
     return m ^ (1 << (m.bit_length() - 1))
 
 
-def tree_gather(x, axis, size, parent, repeat=1):
+def tree_gather(x, axis, size, parent, repeat=1, got=None, levels=8):
     depth = lambda m: 0 if m == 0 else 1 + depth(parent(m))
-    got = {0: x}
+    got = dict(got or {0: x})
     for m in sorted(range(1, size), key=lambda m: (depth(m), -m)):
+        if m in got or depth(m) > levels:
+            continue
         step = m ^ parent(m)
         got[m] = lax.ppermute(got[parent(m)], axis, [(i, i ^ step) for i in range(size * repeat)])
-    return [got[m] for m in range(size)]
+    return got
 
 
 def along(x, nq):
     return [x] + [
-        lax.ppermute(x, "col", [(i, (i + 2 * k) % nq) for i in range(nq)])
-        for k in range(1, nq // 2)
+        lax.ppermute(x, "col", [(i, i ^ (2 * k)) for i in range(nq)]) for k in range(1, nq // 2)
     ]
 
 
 def across(parts, nq):
-    return parts + [
-        lax.ppermute(y, "col", [(i, i ^ 1) for i in range(nq)]) for y in parts
-    ]
+    joined = jnp.concatenate(parts)
+    return parts + [lax.ppermute(joined, "col", [(i, i ^ 1) for i in range(nq)])]
 
 
 def body(upper_blocks, members):
@@ -653,13 +640,12 @@
     slots = blocks.shape[0]
     order = nq * BW
     npair = len(pattern(nq))
-    ids = jnp.stack([lax.axis_index("row"), lax.axis_index("col")]).astype(jnp.int32)
-
-    most, few, row_part = call(
+
+    few, rest, row_part = call(
         functools.partial(prepare_kernel, nq),
-        [((8 + ALL * BW, BW), f32), ((8 + FEW * BW, BW), f32), ((3 * BW + 8, BW), f32)],
-        (ids, members, blocks),
-        2,
+        [((FRONT, BW), f32), (((ALL - FEW) * BW, BW), f32), ((3 * BW + 8, BW), f32)],
+        (members, blocks),
+        0,
     )
     row = spread(row_part, "row", nr)
     lists = jnp.concatenate([x[3 * BW : 3 * BW + 1, :slots] for x in row]).astype(jnp.int32)
@@ -673,23 +659,23 @@
     square_outs = [(listed, f32), (dense, bf16), (dense, bf16), (pack, f32)]
 
     d, u, su, v, own = call(
-        functools.partial(cross_first_kernel, nr, nq), cross_outs, (ids, lists, *row), 2,
+        functools.partial(cross_first_kernel, nr, nq), cross_outs, (lists, *row), 1,
         [pltpu.VMEM((nr, 3 * BW + 8, BW), f32)],
     )
-    nears = gather_pairs(most, few, own, ids, nq)
+    nears = gather_pairs(few, rest, own, nq)
     m, mh, ml, link, s, sh, sl, tell, packs = call(
         functools.partial(first_kernel, nq),
         [(listed, f32), (dense, bf16), (dense, bf16), ((nq, order), f32)]
         + square_outs
         + [((nq,) + pack, f32)],
-        (ids, *nears, own),
-        1,
+        (*nears, own),
+        0,
         [pltpu.VMEM((nq // 2, TERMS + 2 * PACK, BW), f32)],
         flops=square_flops,
     )
     packs = [packs]
+    rows = spread(tell, "row", nr)
     for step in range(PURIFY - 1):
-        rows = spread(tell, "row", nr)
         x, y = call(
             functools.partial(cube_kernel, nq),
             [(listed, f32)] * 2,
@@ -702,8 +688,8 @@
         coef, d, u, su, v, own = call(
             functools.partial(cross_kernel, nr, nq, len(packs)),
             [((8, BW), f32)] + cross_outs,
-            (ids, lists, *rows, *packs, d, u, su, v),
-            2,
+            (lists, *rows, *packs, d, u, su, v),
+            1,
             [pltpu.VMEM((nq, 8, BW), f32), pltpu.VMEM((nr, PACK, BW), f32)],
             flops=square_flops // 4,
         )
@@ -712,19 +698,20 @@
         m, mh, ml, s, sh, sl, tell = call(
             functools.partial(next_kernel, nq, len(old)),
             [(listed, f32), (dense, bf16), (dense, bf16)] + square_outs,
-            (ids, coef, *old, own, x, y, m, link),
-            1,
+            (coef, *old, own, x, y, m, link),
+            0,
             [pltpu.VMEM((nq, PACK, BW), f32)],
             flops=square_flops,
         )
         tell, *straight = lax.optimization_barrier((tell, *straight))
+        rows = spread(tell, "row", nr)
         packs = across(straight, nq)
     strip = (order, BW)
     xo, yo, sums = call(
         functools.partial(last_kernel, nr, nq, len(packs)),
         [((slots, BW, BW), f32)] * 2 + [((8, BW), f32)],
-        (ids, lists, *rows, *packs, x, y, m, link, d, u, su, v),
-        2,
+        (lists, *rows, *packs, x, y, m, link, d, u, su, v),
+        1,
         [
             pltpu.VMEM((nr, PACK, BW), f32),
             pltpu.VMEM((nq, 8, BW), f32),
@@ -744,8 +731,8 @@
     (out,) = call(
         functools.partial(finish_kernel, slots),
         [((1, slots, BW, BW), f32)],
-        (lists, ids, parts, xo, yo),
-        2,
+        (parts, xo, yo),
+        0,
     )
     return out
 

time: 112 us -> 107 us (0.955)
  starting transfers between devices: 44.3 us -> 34.8 us
  waiting for transfers between devices: 19.7 us -> 27.4 us
  Pallas kernels: 35.6 us -> 33.1 us
    ppermute x11 -> x7, waiting for transfers between devices: 3.44 us -> 12 us  [the longest x1 4.63 us: gather_pairs(): few_in = lax.ppermute(few, 'col', mirror)]
    ppermute x6, starting transfers between devices: 15.2 us -> 10.4 us  [tree_gather(): lax.ppermute(got[parent(m)], axis, [(i, i ^ step) for i in range(size * r...]
    ppermute x11 -> x7, starting transfers between devices: 21.9 us -> 18.7 us  [the longest x1 6.07 us: gather_pairs(): few_in = lax.ppermute(few, 'col', mirror)]
    pallas_call x10, Pallas kernels: 35.6 us -> 33.1 us  [call(): pl.pallas_call(kernel, out_shape=[jax.ShapeDtypeStruct(s, d) for s, d in...]
    ppermute x9, waiting for transfers between devices: 2.08 us -> 0.02 us  [spread(): lax.ppermute(x, axis, [(i, i ^ k) for i in range(size)])]
    ppermute x9, starting transfers between devices: 7.13 us -> 5.73 us  [spread(): lax.ppermute(x, axis, [(i, i ^ k) for i in range(size)])]
    ppermute x6, waiting for transfers between devices: 14.2 us -> 15.4 us  [tree_gather(): lax.ppermute(got[parent(m)], axis, [(i, i ^ step) for i in range(size * r...]
  transfers between devices with their start and end apart: 26 -> 22, of which waited for: 7 -> 7; matrix products, arithmetic and copies ran while one was open for 0% -> 0% of each run, Pallas kernels for 16% -> 17%
where the time goes in v4:
time: 107 us
  starting transfers between devices  34.8 us (33%)
  Pallas kernels  33.1 us (31%)
  waiting for transfers between devices  27.4 us (26%)
  blocking collectives  9.63 us (9%)
  local copies, waits for them, and re-layouts  1.74 us (2%)
    pallas_call x10, Pallas kernels, call(): pl.pallas_call(kernel, out_shape=[jax.ShapeDtypeStruct(s, d) for s, d in...  33.1 us
    ppermute x6, waiting for transfers between devices, tree_gather(): lax.ppermute(got[parent(m)], axis, [(i, i ^ step) for i in range(size * r...  15.4 us
    ppermute x6, starting transfers between devices, tree_gather(): lax.ppermute(got[parent(m)], axis, [(i, i ^ step) for i in range(size * r...  10.4 us
    all_to_all x1, blocking collectives, body(): lax.all_to_all(jnp.broadcast_to(mine[None], (nr * nq, BW)), ('row', 'col'...  9.63 us
    ppermute x1, starting transfers between devices, gather_pairs(): few_in = lax.ppermute(few, 'col', mirror)  6.07 us
    ppermute x9, starting transfers between devices, spread(): lax.ppermute(x, axis, [(i, i ^ k) for i in range(size)])  5.73 us
    ppermute x1, starting transfers between devices, gather_pairs(): pack_in = lax.ppermute(own_pack, 'col', mirror)  5.41 us
    ppermute x1, waiting for transfers between devices, gather_pairs(): few_in = lax.ppermute(few, 'col', mirror)  4.63 us
  transfers between devices with their start and end apart: 22, of which 7 were waited for; matrix products, arithmetic and copies ran while one was open for 0% of the time, Pallas kernels for 17%

profile of v4, /device:TPU:0, one launch (start us, length us, event | category | flops | bytes accessed | tf_op | source)
XLA Modules:
  0.0 107.0 jit_solution(7138860548779010169)
XLA Ops:
  0.0 0.0 copy-start
  0.0 1.1 copy-done
  1.1 0.0 copy-start.1
  1.1 0.7 copy-done.1
  1.8 6.1 %collective-permute-start.4 = (f32[520,128]{1,0:T(8,128)S(1)}, f32[520,128]{1,0:T(8,128)S(1)}, u32[]{:S(2)}, u32[]{:S(2)}) collective-permute-start(f32[520,128]{1,0:T(8,128)S(1)} %get-tuple-element.53.few), channel_id=1, source_target_pairs={{0,7},{1,6},{2,5},{3,4},{4,3},{5,2},{6,1},{7,0},{8,15},{9,14},{10,... | collective-permute-start | bytes 798728 | tf_op jit(solution)/shard_map/ppermute | solution.py:590
  7.8 0.0 collective-permute-start
  7.8 1.5 %collective-permute-start.1 = (f32[392,128]{1,0:T(8,128)S(1)}, f32[392,128]{1,0:T(8,128)S(1)}, u32[]{:S(2)}, u32[]{:S(2)}) collective-permute-start(f32[392,128]{1,0:T(8,128)S(1)} %get-tuple-element.51.refs_0_), channel_id=1, source_target_pairs={{0,16},{8,24},{16,0},{24,8},{1,17},{9,25},{17,1},{25,9},{2,18},{10... | collective-permute-start | bytes 602120 | tf_op jit(solution)/shard_map/ppermute | solution.py:582
  9.3 0.4 collective-permute-start.2
  9.7 4.6 %collective-permute-done.4.few_in = f32[520,128]{1,0:T(8,128)S(1)} collective-permute-done((f32[520,128]{1,0:T(8,128)S(1)}, f32[520,128]{1,0:T(8,128)S(1)}, u32[]{:S(2)}, u32[]{:S(2)}) %collective-permute-start.4) | collective-permute-done | bytes 266272 | tf_op jit(solution)/shard_map/ppermute | solution.py:590
  14.4 1.5 %collective-permute-start.5 = (f32[520,128]{1,0:T(8,128)S(1)}, f32[520,128]{1,0:T(8,128)S(1)}, u32[]{:S(2)}, u32[]{:S(2)}) collective-permute-start(f32[520,128]{1,0:T(8,128)S(1)} %broadcast_select_fusion.refs_0_), channel_id=1, source_target_pairs={{0,1},{1,0},{2,3},{3,2},{4,5},{5,4},{6,7},{7,6},{8,9},{9,8},{10,11... | collective-permute-start | bytes 798728 | tf_op jit(solution)/shard_map/ppermute | solution.py:622
  15.8 5.4 %collective-permute-start.6 = (f32[520,128]{1,0:T(8,128)S(1)}, f32[520,128]{1,0:T(8,128)S(1)}, u32[]{:S(2)}, u32[]{:S(2)}) collective-permute-start(f32[520,128]{1,0:T(8,128)S(1)} %broadcast_select_fusion.refs_0_), channel_id=1, source_target_pairs={{0,2},{1,3},{2,0},{3,1},{4,6},{5,7},{6,4},{7,5},{8,10},{9,11},{10,... | collective-permute-start | bytes 798728 | tf_op jit(solution)/shard_map/ppermute | solution.py:622
  21.2 0.0 collective-permute-done.refs_1_
  21.2 1.3 %collective-permute-start.3 = (f32[384,128]{1,0:T(8,128)S(1)}, f32[384,128]{1,0:T(8,128)S(1)}, u32[]{:S(2)}, u32[]{:S(2)}) collective-permute-start(f32[384,128]{1,0:T(8,128)S(1)} %get-tuple-element.52.rest), channel_id=1, source_target_pairs={{5,2},{6,1},{7,0},{13,10},{14,9},{15,8},{21,18},{22,17},{23,16},{2... | collective-permute-start | bytes 589832 | tf_op jit(solution)/shard_map/ppermute | solution.py:591
  22.5 0.0 collective-permute-done.1.refs_2_
  22.6 0.0 collective-permute-done.2.refs_3_
  22.6 2.1 %shard_map.29 = (f32[4,128,128]{2,1,0:T(8,128)S(1)}, f32[4,128,128]{2,1,0:T(8,128)S(1)}, f32[4,128,128]{2,1,0:T(8,128)S(1)}, f32[4,128,128]{2,1,0:T(8,128)S(1)}, f32[136,128]{1,0:T(8,128)S(1)}) custom-call(s32[4,9]{1,0:T(4,128)S(1)} %maximum_convert_fusion.lists, f32[392,128]{1,0:T(8,128)S(1)} %get-tuple-element.51.refs_0_, ...), custom_call_target="tpu_custom_call" | custom-call | tf_op jit(solution)/shard_map/pallas_call | solution.py:569
  24.7 5.4 %collective-permute-start.8 = (f32[136,128]{1,0:T(8,128)S(1)}, f32[136,128]{1,0:T(8,128)S(1)}, u32[]{:S(2)}, u32[]{:S(2)}) collective-permute-start(f32[136,128]{1,0:T(8,128)S(1)} %get-tuple-element.58.own_pack.refs_8_), channel_id=1, source_target_pairs={{0,7},{1,6},{2,5},{3,4},{4,3},{5,2},{6,1},{7,0},{8,15},{9,14},{10,... | collective-permute-start | bytes 208904 | tf_op jit(solution)/shard_map/ppermute | solution.py:592
  30.1 3.6 %collective-permute-done.3.rest_in = f32[384,128]{1,0:T(8,128)S(1)} collective-permute-done((f32[384,128]{1,0:T(8,128)S(1)}, f32[384,128]{1,0:T(8,128)S(1)}, u32[]{:S(2)}, u32[]{:S(2)}) %collective-permute-start.3) | collective-permute-done | bytes 196640 | tf_op jit(solution)/shard_map/ppermute | solution.py:591
  33.7 0.0 collective-permute-done.5.refs_1_
  33.7 0.0 collective-permute-done.6.refs_2_
  33.7 0.7 collective-permute-done.8.pack_in
  34.5 1.5 %collective-permute-start.9 = (f32[792,128]{1,0:T(8,128)S(1)}, f32[792,128]{1,0:T(8,128)S(1)}, u32[]{:S(2)}, u32[]{:S(2)}) collective-permute-start(f32[792,128]{1,0:T(8,128)S(1)} %shard_map.30.refs_4_), channel_id=1, source_target_pairs={{0,1},{1,0},{2,3},{3,2},{4,5},{5,4},{6,7},{7,6},{8,9},{9,8},{10,11... | collective-permute-start | bytes 1216520 | tf_op jit(solution)/shard_map/ppermute | solution.py:622
  35.9 1.4 %collective-permute-start.10 = (f32[792,128]{1,0:T(8,128)S(1)}, f32[792,128]{1,0:T(8,128)S(1)}, u32[]{:S(2)}, u32[]{:S(2)}) collective-permute-start(f32[792,128]{1,0:T(8,128)S(1)} %shard_map.30.refs_4_), channel_id=1, source_target_pairs={{0,2},{1,3},{2,0},{3,1},{4,6},{5,7},{6,4},{7,5},{8,10},{9,11},{10,... | collective-permute-start | bytes 1216520 | tf_op jit(solution)/shard_map/ppermute | solution.py:622
  37.3 7.1 %collective-permute-done.9.refs_5_ = f32[792,128]{1,0:T(8,128)S(1)} collective-permute-done((f32[792,128]{1,0:T(8,128)S(1)}, f32[792,128]{1,0:T(8,128)S(1)}, u32[]{:S(2)}, u32[]{:S(2)}) %collective-permute-start.9) | collective-permute-done | bytes 405536 | tf_op jit(solution)/shard_map/ppermute | solution.py:622
  44.4 0.7 collective-permute-start.11
  45.1 0.0 collective-permute-start.7
  45.1 6.4 %collective-permute-done.7.refs_3_ = f32[520,128]{1,0:T(8,128)S(1)} collective-permute-done((f32[520,128]{1,0:T(8,128)S(1)}, f32[520,128]{1,0:T(8,128)S(1)}, u32[]{:S(2)}, u32[]{:S(2)}) %collective-permute-start.7) | collective-permute-done | bytes 266272 | tf_op jit(solution)/shard_map/ppermute | solution.py:622
  51.5 0.0 collective-permute-done.10.refs_6_
  51.5 1.9 %collective-permute-done.11.refs_7_ = f32[792,128]{1,0:T(8,128)S(1)} collective-permute-done((f32[792,128]{1,0:T(8,128)S(1)}, f32[792,128]{1,0:T(8,128)S(1)}, u32[]{:S(2)}, u32[]{:S(2)}) %collective-permute-start.11) | collective-permute-done | bytes 405536 | tf_op jit(solution)/shard_map/ppermute | solution.py:622
  53.4 6.3 %shard_map.31 = (f32[32,128,128]{2,1,0:T(8,128)S(1)}, bf16[1024,1024]{1,0:T(8,128)(2,1)S(1)}, bf16[1024,1024]{1,0:T(8,128)(2,1)S(1)}, f32[8,1024]{1,0:T(8,128)S(...) custom-call(f32[520,128]{1,0:T(8,128)S(1)} %broadcast_select_fusion., ...), custom_call_target="tpu_custom_call" | custom-call | flops 6442450944 | tf_op jit(solution)/shard_map/pallas_call | solution.py:569
  59.7 0.1 collective-permute-start.12
  59.8 1.6 %collective-permute-start.13 = (f32[136,128]{1,0:T(8,128)S(1)}, f32[136,128]{1,0:T(8,128)S(1)}, u32[]{:S(2)}, u32[]{:S(2)}) collective-permute-start(f32[136,128]{1,0:T(8,128)S(1)} %get-tuple-element.59.refs_0_), channel_id=1, source_target_pairs={{0,16},{8,24},{16,0},{24,8},{1,17},{9,25},{17,1},{25,9},{2,18},{10... | collective-permute-start | bytes 208904 | tf_op jit(solution)/shard_map/ppermute | solution.py:582
  61.3 0.3 collective-permute-start.14
  61.6 4.4 %shard_map.33 = (f32[32,128,128]{2,1,0:T(8,128)S(1)}, f32[32,128,128]{2,1,0:T(8,128)S(1)}) custom-call(f32[32,128,128]{2,1,0:T(8,128)S(1)} %get-tuple-element.67.m_ref.refs_4_, bf16[1024,1024]{1,0:T(8,128)(2,1)S(1)} %get-tuple-element.68.mh, bf16[1024,1024]{1,0:T(8,128)(2,1)S(1)} %get-tuple-element.69.ml, f32[32,128,128]{2,1,0:T(8,128)S(1)} %get-tuple-element.70.s_ref, ...), custom_call_target="tpu_custom_call" | custom-call | flops 6442450944 | tf_op jit(solution)/shard_map/pallas_call | solution.py:569
  66.0 0.0 collective-permute-done.12.refs_1_
  66.0 0.0 collective-permute-done.13.refs_2_
  66.0 0.0 collective-permute-done.14.refs_3_
  66.0 2.3 %shard_map.32 = (f32[8,128]{1,0:T(8,128)S(1)}, f32[4,128,128]{2,1,0:T(8,128)S(1)}, f32[4,128,128]{2,1,0:T(8,128)S(1)}, f32[4,128,128]{2,1,0:T(8,128)S(1)}, f32[4...) custom-call(s32[4,9]{1,0:T(4,128)S(1)} %maximum_convert_fusion.lists, f32[136,128]{1,0:T(8,128)S(1)} %get-tuple-element.59.refs_0_, ...), custom_call_target="tpu_custom_call" | custom-call | flops 1610612736 | tf_op jit(solution)/shard_map/pallas_call | solution.py:569
  68.3 0.6 collective-permute-start.15
  68.9 1.4 %collective-permute-start.16 = (f32[136,128]{1,0:T(8,128)S(1)}, f32[136,128]{1,0:T(8,128)S(1)}, u32[]{:S(2)}, u32[]{:S(2)}) collective-permute-start(f32[136,128]{1,0:T(8,128)S(1)} %get-tuple-element.78.refs_1_.refs_4_), channel_id=1, source_target_pairs={{0,4},{1,5},{2,6},{3,7},{4,0},{5,1},{6,2},{7,3},{8,12},{9,13},{10,... | collective-permute-start | bytes 208904 | tf_op jit(solution)/shard_map/ppermute | solution.py:628
  70.4 2.4 %collective-permute-start.17 = (f32[136,128]{1,0:T(8,128)S(1)}, f32[136,128]{1,0:T(8,128)S(1)}, u32[]{:S(2)}, u32[]{:S(2)}) collective-permute-start(f32[136,128]{1,0:T(8,128)S(1)} %get-tuple-element.78.refs_1_.refs_4_), channel_id=1, source_target_pairs={{0,6},{1,7},{2,4},{3,5},{4,2},{5,3},{6,0},{7,1},{8,14},{9,15},{10,... | collective-permute-start | bytes 208904 | tf_op jit(solution)/shard_map/ppermute | solution.py:628
  72.8 7.0 %shard_map.34 = (f32[32,128,128]{2,1,0:T(8,128)S(1)}, bf16[1024,1024]{1,0:T(8,128)(2,1)S(1)}, bf16[1024,1024]{1,0:T(8,128)(2,1)S(1)}, f32[32,128,128]{2,1,0:T(8,...) custom-call(f32[8,128]{1,0:T(8,128)S(1)} %get-tuple-element.65.coef, ...), custom_call_target="tpu_custom_call" | custom-call | flops 6442450944 | tf_op jit(solution)/shard_map/pallas_call | solution.py:569
  79.8 0.0 collective-permute-done.15.refs_5_
  79.8 0.0 collective-permute-done.16.refs_6_
  79.9 0.0 collective-permute-done.17.refs_7_
  79.9 0.1 collective-permute-start.18
  79.9 1.6 %collective-permute-start.19 = (f32[136,128]{1,0:T(8,128)S(1)}, f32[136,128]{1,0:T(8,128)S(1)}, u32[]{:S(2)}, u32[]{:S(2)}) collective-permute-start(f32[136,128]{1,0:T(8,128)S(1)} %get-tuple-element.77.refs_0_), channel_id=1, source_target_pairs={{0,16},{8,24},{16,0},{24,8},{1,17},{9,25},{17,1},{25,9},{2,18},{10... | collective-permute-start | bytes 208904 | tf_op jit(solution)/shard_map/ppermute | solution.py:582
  81.5 0.3 collective-permute-start.20
  81.8 1.5 %collective-permute-start.21 = (f32[544,128]{1,0:T(8,128)S(1)}, f32[544,128]{1,0:T(8,128)S(1)}, u32[]{:S(2)}, u32[]{:S(2)}) collective-permute-start(f32[544,128]{1,0:T(8,128)S(1)} %pad_maximum_fusion), channel_id=1, source_target_pairs={{0,1},{1,0},{2,3},{3,2},{4,5},{5,4},{6,7},{7,6},{8,9},{9,8},{10,11... | collective-permute-start | bytes 835592 | tf_op jit(solution)/shard_map/ppermute | solution.py:634
  83.3 4.4 %shard_map.35 = (f32[32,128,128]{2,1,0:T(8,128)S(1)}, f32[32,128,128]{2,1,0:T(8,128)S(1)}) custom-call(f32[32,128,128]{2,1,0:T(8,128)S(1)} %get-tuple-element.82.m_ref.refs_11_, bf16[1024,1024]{1,0:T(8,128)(2,1)S(1)} %get-tuple-element.83.mh, bf16[1024,1024]{1,0:T(8,128)(2,1)S(1)} %get-tuple-element.84.ml, f32[32,128,128]{2,1,0:T(8,128)S(1)} %get-tuple-element.85.s_ref, ...), custom_call_target="tpu_custom_call" | custom-call | flops 6442450944 | tf_op jit(solution)/shard_map/pallas_call | solution.py:569
  87.7 0.0 collective-permute-done.18.refs_1_
  87.7 0.0 collective-permute-done.19.refs_2_
  87.7 0.0 collective-permute-done.20.refs_3_
  87.7 3.1 %collective-permute-done.21.refs_8_ = f32[544,128]{1,0:T(8,128)S(1)} collective-permute-done((f32[544,128]{1,0:T(8,128)S(1)}, f32[544,128]{1,0:T(8,128)S(1)}, u32[]{:S(2)}, u32[]{:S(2)}) %collective-permute-start.21) | collective-permute-done | bytes 278560 | tf_op jit(solution)/shard_map/ppermute | solution.py:634
  90.8 5.6 %shard_map.36 = (f32[9,128,128]{2,1,0:T(8,128)S(1)}, f32[9,128,128]{2,1,0:T(8,128)S(1)}, f32[8,128]{1,0:T(8,128)S(1)}) custom-call(s32[4,9]{1,0:T(4,128)S(1)} %maximum_convert_fusion.lists, f32[136,128]{1,0:T(8,128)S(1)} %get-tuple-element.77.refs_0_, f32[136,128]{1,0:T(8,128)S(1)} %collective-permute-done.18.refs_1_, ...), custom_call_target="tpu_custom_call" | custom-call | tf_op jit(solution)/shard_map/pallas_call | solution.py:569
  96.4 9.6 %all_to_all.8 = f32[32,1,128]{2,1,0:T(1,128)S(1)} all-to-all(f32[32,1,128]{2,1,0:T(1,128)S(1)} %broadcast_in_dim.2), channel_id=1, replica_groups=mesh['row'=4,'col'=8] {'row','col'}, dimensions={0} | all-to-all | bytes 32768 | tf_op jit(solution)/shard_map/all_to_all | solution.py:728
  106.0 1.0 shard_map.37
  (11 shorter events, 0.2 us)
Async XLA Ops:
  0.0 1.1 copy-start
  1.1 0.7 copy-start.1
  1.8 12.6 %collective-permute-start.4 = (f32[520,128]{1,0:T(8,128)S(1)}, f32[520,128]{1,0:T(8,128)S(1)}, u32[]{:S(2)}, u32[]{:S(2)}) collective-permute-start(f32[520,128]{1,0:T(8,128)S(1)} %get-tuple-element.53.few), channel_id=1, source_target_pairs={{0,7},{1,6},{2,5},{3,4},{4,3},{5,2},{6,1},{7,0},{8,15},{9,14},{10,... | collective-permute-start | bytes 798728 | tf_op jit(solution)/shard_map/ppermute | solution.py:590
  7.8 13.4 %collective-permute-start = (f32[392,128]{1,0:T(8,128)S(1)}, f32[392,128]{1,0:T(8,128)S(1)}, u32[]{:S(2)}, u32[]{:S(2)}) collective-permute-start(f32[392,128]{1,0:T(8,128)S(1)} %get-tuple-element.51.refs_0_), channel_id=1, source_target_pairs={{0,8},{8,0},{16,24},{24,16},{1,9},{9,1},{17,25},{25,17},{2,10},{10... | collective-permute-start | bytes 602120 | tf_op jit(solution)/shard_map/ppermute | solution.py:582
  7.8 14.7 %collective-permute-start.1 = (f32[392,128]{1,0:T(8,128)S(1)}, f32[392,128]{1,0:T(8,128)S(1)}, u32[]{:S(2)}, u32[]{:S(2)}) collective-permute-start(f32[392,128]{1,0:T(8,128)S(1)} %get-tuple-element.51.refs_0_), channel_id=1, source_target_pairs={{0,16},{8,24},{16,0},{24,8},{1,17},{9,25},{17,1},{25,9},{2,18},{10... | collective-permute-start | bytes 602120 | tf_op jit(solution)/shard_map/ppermute | solution.py:582
  9.3 13.2 %collective-permute-start.2 = (f32[392,128]{1,0:T(8,128)S(1)}, f32[392,128]{1,0:T(8,128)S(1)}, u32[]{:S(2)}, u32[]{:S(2)}) collective-permute-start(f32[392,128]{1,0:T(8,128)S(1)} %get-tuple-element.51.refs_0_), channel_id=1, source_target_pairs={{0,24},{8,16},{16,8},{24,0},{1,25},{9,17},{17,9},{25,1},{2,26},{10... | collective-permute-start | bytes 602120 | tf_op jit(solution)/shard_map/ppermute | solution.py:582
  14.4 19.3 %collective-permute-start.5 = (f32[520,128]{1,0:T(8,128)S(1)}, f32[520,128]{1,0:T(8,128)S(1)}, u32[]{:S(2)}, u32[]{:S(2)}) collective-permute-start(f32[520,128]{1,0:T(8,128)S(1)} %broadcast_select_fusion.refs_0_), channel_id=1, source_target_pairs={{0,1},{1,0},{2,3},{3,2},{4,5},{5,4},{6,7},{7,6},{8,9},{9,8},{10,11... | collective-permute-start | bytes 798728 | tf_op jit(solution)/shard_map/ppermute | solution.py:622
  15.8 17.8 %collective-permute-start.6 = (f32[520,128]{1,0:T(8,128)S(1)}, f32[520,128]{1,0:T(8,128)S(1)}, u32[]{:S(2)}, u32[]{:S(2)}) collective-permute-start(f32[520,128]{1,0:T(8,128)S(1)} %broadcast_select_fusion.refs_0_), channel_id=1, source_target_pairs={{0,2},{1,3},{2,0},{3,1},{4,6},{5,7},{6,4},{7,5},{8,10},{9,11},{10,... | collective-permute-start | bytes 798728 | tf_op jit(solution)/shard_map/ppermute | solution.py:622
  21.2 12.4 %collective-permute-start.3 = (f32[384,128]{1,0:T(8,128)S(1)}, f32[384,128]{1,0:T(8,128)S(1)}, u32[]{:S(2)}, u32[]{:S(2)}) collective-permute-start(f32[384,128]{1,0:T(8,128)S(1)} %get-tuple-element.52.rest), channel_id=1, source_target_pairs={{5,2},{6,1},{7,0},{13,10},{14,9},{15,8},{21,18},{22,17},{23,16},{2... | collective-permute-start | bytes 589832 | tf_op jit(solution)/shard_map/ppermute | solution.py:591
  24.7 9.7 %collective-permute-start.8 = (f32[136,128]{1,0:T(8,128)S(1)}, f32[136,128]{1,0:T(8,128)S(1)}, u32[]{:S(2)}, u32[]{:S(2)}) collective-permute-start(f32[136,128]{1,0:T(8,128)S(1)} %get-tuple-element.58.own_pack.refs_8_), channel_id=1, source_target_pairs={{0,7},{1,6},{2,5},{3,4},{4,3},{5,2},{6,1},{7,0},{8,15},{9,14},{10,... | collective-permute-start | bytes 208904 | tf_op jit(solution)/shard_map/ppermute | solution.py:592
  34.5 9.9 %collective-permute-start.9 = (f32[792,128]{1,0:T(8,128)S(1)}, f32[792,128]{1,0:T(8,128)S(1)}, u32[]{:S(2)}, u32[]{:S(2)}) collective-permute-start(f32[792,128]{1,0:T(8,128)S(1)} %shard_map.30.refs_4_), channel_id=1, source_target_pairs={{0,1},{1,0},{2,3},{3,2},{4,5},{5,4},{6,7},{7,6},{8,9},{9,8},{10,11... | collective-permute-start | bytes 1216520 | tf_op jit(solution)/shard_map/ppermute | solution.py:622
  35.9 15.6 %collective-permute-start.10 = (f32[792,128]{1,0:T(8,128)S(1)}, f32[792,128]{1,0:T(8,128)S(1)}, u32[]{:S(2)}, u32[]{:S(2)}) collective-permute-start(f32[792,128]{1,0:T(8,128)S(1)} %shard_map.30.refs_4_), channel_id=1, source_target_pairs={{0,2},{1,3},{2,0},{3,1},{4,6},{5,7},{6,4},{7,5},{8,10},{9,11},{10,... | collective-permute-start | bytes 1216520 | tf_op jit(solution)/shard_map/ppermute | solution.py:622
  44.4 9.0 %collective-permute-start.11 = (f32[792,128]{1,0:T(8,128)S(1)}, f32[792,128]{1,0:T(8,128)S(1)}, u32[]{:S(2)}, u32[]{:S(2)}) collective-permute-start(f32[792,128]{1,0:T(8,128)S(1)} %collective-permute-done.9.refs_5_), channel_id=1, source_target_pairs={{0,2},{1,3},{2,0},{3,1},{4,6},{5,7},{6,4},{7,5},{8,10},{9,11},{10,... | collective-permute-start | bytes 1216520 | tf_op jit(solution)/shard_map/ppermute | solution.py:622
  45.1 6.4 %collective-permute-start.7 = (f32[520,128]{1,0:T(8,128)S(1)}, f32[520,128]{1,0:T(8,128)S(1)}, u32[]{:S(2)}, u32[]{:S(2)}) collective-permute-start(f32[520,128]{1,0:T(8,128)S(1)} %collective-permute-done.6.refs_2_), channel_id=1, source_target_pairs={{0,1},{1,0},{2,3},{3,2},{4,5},{5,4},{6,7},{7,6},{8,9},{9,8},{10,11... | collective-permute-start | bytes 798728 | tf_op jit(solution)/shard_map/ppermute | solution.py:622
  59.7 6.3 %collective-permute-start.12 = (f32[136,128]{1,0:T(8,128)S(1)}, f32[136,128]{1,0:T(8,128)S(1)}, u32[]{:S(2)}, u32[]{:S(2)}) collective-permute-start(f32[136,128]{1,0:T(8,128)S(1)} %get-tuple-element.59.refs_0_), channel_id=1, source_target_pairs={{0,8},{8,0},{16,24},{24,16},{1,9},{9,1},{17,25},{25,17},{2,10},{10... | collective-permute-start | bytes 208904 | tf_op jit(solution)/shard_map/ppermute | solution.py:582
  59.8 6.2 %collective-permute-start.13 = (f32[136,128]{1,0:T(8,128)S(1)}, f32[136,128]{1,0:T(8,128)S(1)}, u32[]{:S(2)}, u32[]{:S(2)}) collective-permute-start(f32[136,128]{1,0:T(8,128)S(1)} %get-tuple-element.59.refs_0_), channel_id=1, source_target_pairs={{0,16},{8,24},{16,0},{24,8},{1,17},{9,25},{17,1},{25,9},{2,18},{10... | collective-permute-start | bytes 208904 | tf_op jit(solution)/shard_map/ppermute | solution.py:582
  61.3 4.7 %collective-permute-start.14 = (f32[136,128]{1,0:T(8,128)S(1)}, f32[136,128]{1,0:T(8,128)S(1)}, u32[]{:S(2)}, u32[]{:S(2)}) collective-permute-start(f32[136,128]{1,0:T(8,128)S(1)} %get-tuple-element.59.refs_0_), channel_id=1, source_target_pairs={{0,24},{8,16},{16,8},{24,0},{1,25},{9,17},{17,9},{25,1},{2,26},{10... | collective-permute-start | bytes 208904 | tf_op jit(solution)/shard_map/ppermute | solution.py:582
  68.3 11.5 %collective-permute-start.15 = (f32[136,128]{1,0:T(8,128)S(1)}, f32[136,128]{1,0:T(8,128)S(1)}, u32[]{:S(2)}, u32[]{:S(2)}) collective-permute-start(f32[136,128]{1,0:T(8,128)S(1)} %get-tuple-element.78.refs_1_.refs_4_), channel_id=1, source_target_pairs={{0,2},{1,3},{2,0},{3,1},{4,6},{5,7},{6,4},{7,5},{8,10},{9,11},{10,... | collective-permute-start | bytes 208904 | tf_op jit(solution)/shard_map/ppermute | solution.py:628
  68.9 10.9 %collective-permute-start.16 = (f32[136,128]{1,0:T(8,128)S(1)}, f32[136,128]{1,0:T(8,128)S(1)}, u32[]{:S(2)}, u32[]{:S(2)}) collective-permute-start(f32[136,128]{1,0:T(8,128)S(1)} %get-tuple-element.78.refs_1_.refs_4_), channel_id=1, source_target_pairs={{0,4},{1,5},{2,6},{3,7},{4,0},{5,1},{6,2},{7,3},{8,12},{9,13},{10,... | collective-permute-start | bytes 208904 | tf_op jit(solution)/shard_map/ppermute | solution.py:628
  70.4 9.5 %collective-permute-start.17 = (f32[136,128]{1,0:T(8,128)S(1)}, f32[136,128]{1,0:T(8,128)S(1)}, u32[]{:S(2)}, u32[]{:S(2)}) collective-permute-start(f32[136,128]{1,0:T(8,128)S(1)} %get-tuple-element.78.refs_1_.refs_4_), channel_id=1, source_target_pairs={{0,6},{1,7},{2,4},{3,5},{4,2},{5,3},{6,0},{7,1},{8,14},{9,15},{10,... | collective-permute-start | bytes 208904 | tf_op jit(solution)/shard_map/ppermute | solution.py:628
  79.9 7.8 %collective-permute-start.18 = (f32[136,128]{1,0:T(8,128)S(1)}, f32[136,128]{1,0:T(8,128)S(1)}, u32[]{:S(2)}, u32[]{:S(2)}) collective-permute-start(f32[136,128]{1,0:T(8,128)S(1)} %get-tuple-element.77.refs_0_), channel_id=1, source_target_pairs={{0,8},{8,0},{16,24},{24,16},{1,9},{9,1},{17,25},{25,17},{2,10},{10... | collective-permute-start | bytes 208904 | tf_op jit(solution)/shard_map/ppermute | solution.py:582
  79.9 7.8 %collective-permute-start.19 = (f32[136,128]{1,0:T(8,128)S(1)}, f32[136,128]{1,0:T(8,128)S(1)}, u32[]{:S(2)}, u32[]{:S(2)}) collective-permute-start(f32[136,128]{1,0:T(8,128)S(1)} %get-tuple-element.77.refs_0_), channel_id=1, source_target_pairs={{0,16},{8,24},{16,0},{24,8},{1,17},{9,25},{17,1},{25,9},{2,18},{10... | collective-permute-start | bytes 208904 | tf_op jit(solution)/shard_map/ppermute | solution.py:582
  81.5 6.2 %collective-permute-start.20 = (f32[136,128]{1,0:T(8,128)S(1)}, f32[136,128]{1,0:T(8,128)S(1)}, u32[]{:S(2)}, u32[]{:S(2)}) collective-permute-start(f32[136,128]{1,0:T(8,128)S(1)} %get-tuple-element.77.refs_0_), channel_id=1, source_target_pairs={{0,24},{8,16},{16,8},{24,0},{1,25},{9,17},{17,9},{25,1},{2,26},{10... | collective-permute-start | bytes 208904 | tf_op jit(solution)/shard_map/ppermute | solution.py:582
  81.8 9.0 %collective-permute-start.21 = (f32[544,128]{1,0:T(8,128)S(1)}, f32[544,128]{1,0:T(8,128)S(1)}, u32[]{:S(2)}, u32[]{:S(2)}) collective-permute-start(f32[544,128]{1,0:T(8,128)S(1)} %pad_maximum_fusion), channel_id=1, source_target_pairs={{0,1},{1,0},{2,3},{3,2},{4,5},{5,4},{6,7},{7,6},{8,9},{9,8},{10,11... | collective-permute-start | bytes 835592 | tf_op jit(solution)/shard_map/ppermute | solution.py:634

commit v5 on v4

--- a/solution.py
+++ b/solution.py
@@ -647,7 +647,8 @@
         (members, blocks),
         0,
     )
-    row = spread(row_part, "row", nr)
+    row = tree_gather(row_part, "row", nr, drop_low)
+    row = [row[k] for k in range(nr)]
     lists = jnp.concatenate([x[3 * BW : 3 * BW + 1, :slots] for x in row]).astype(jnp.int32)
 
     square_flops = 6 * order**3

time: 107 us -> 107 us (level)
    ppermute x6 -> x9, waiting for transfers between devices: 15.4 us -> 20.3 us  [tree_gather(): lax.ppermute(got[parent(m)], axis, [(i, i ^ step) for i in range(size * r...]
    ppermute x1, waiting for transfers between devices: 4.63 us -> 0.04 us  [gather_pairs(): few_in = lax.ppermute(few, 'col', mirror)]
    ppermute x9 -> x6, starting transfers between devices: 5.73 us -> 3.87 us  [spread(): lax.ppermute(x, axis, [(i, i ^ k) for i in range(size)])]
    ppermute x6 -> x9, starting transfers between devices: 10.4 us -> 11.9 us  [tree_gather(): lax.ppermute(got[parent(m)], axis, [(i, i ^ step) for i in range(size * r...]
where the time goes in v5:
time: 107 us
  starting transfers between devices  34.5 us (32%)
  Pallas kernels  33.1 us (31%)
  waiting for transfers between devices  27.8 us (26%)
  blocking collectives  9.62 us (9%)
  local copies, waits for them, and re-layouts  1.74 us (2%)
    pallas_call x10, Pallas kernels, call(): pl.pallas_call(kernel, out_shape=[jax.ShapeDtypeStruct(s, d) for s, d in...  33.1 us
    ppermute x9, waiting for transfers between devices, tree_gather(): lax.ppermute(got[parent(m)], axis, [(i, i ^ step) for i in range(size * r...  20.3 us
    ppermute x9, starting transfers between devices, tree_gather(): lax.ppermute(got[parent(m)], axis, [(i, i ^ step) for i in range(size * r...  11.9 us
    all_to_all x1, blocking collectives, body(): lax.all_to_all(jnp.broadcast_to(mine[None], (nr * nq, BW)), ('row', 'col'...  9.62 us
    ppermute x1, starting transfers between devices, gather_pairs(): few_in = lax.ppermute(few, 'col', mirror)  6.07 us
    ppermute x1, starting transfers between devices, gather_pairs(): pack_in = lax.ppermute(own_pack, 'col', mirror)  5.41 us
    ppermute x3, starting transfers between devices, along(): lax.ppermute(x, 'col', [(i, i ^ 2 * k) for i in range(nq)])  4.45 us
    ppermute x6, starting transfers between devices, spread(): lax.ppermute(x, axis, [(i, i ^ k) for i in range(size)])  3.87 us
  transfers between devices with their start and end apart: 22, of which 7 were waited for; matrix products, arithmetic and copies ran while one was open for 0% of the time, Pallas kernels for 17%

profile of v5, /device:TPU:0, one launch (start us, length us, event | category | flops | bytes accessed | tf_op | source)
XLA Modules:
  0.0 107.0 jit_solution(6449267841030853276)
XLA Ops:
  0.0 0.0 copy-start
  0.0 1.1 copy-done
  1.1 0.0 copy-start.1
  1.1 0.7 copy-done.1
  1.8 6.1 %collective-permute-start.4 = (f32[520,128]{1,0:T(8,128)S(1)}, f32[520,128]{1,0:T(8,128)S(1)}, u32[]{:S(2)}, u32[]{:S(2)}) collective-permute-start(f32[520,128]{1,0:T(8,128)S(1)} %get-tuple-element.53.few), channel_id=1, source_target_pairs={{0,7},{1,6},{2,5},{3,4},{4,3},{5,2},{6,1},{7,0},{8,15},{9,14},{10,... | collective-permute-start | bytes 798728 | tf_op jit(solution)/shard_map/ppermute | solution.py:590
  7.8 1.5 %collective-permute-start.1 = (f32[392,128]{1,0:T(8,128)S(1)}, f32[392,128]{1,0:T(8,128)S(1)}, u32[]{:S(2)}, u32[]{:S(2)}) collective-permute-start(f32[392,128]{1,0:T(8,128)S(1)} %get-tuple-element.51.refs_0_), channel_id=1, source_target_pairs={{0,16},{8,24},{16,0},{24,8},{1,17},{9,25},{17,1},{25,9},{2,18},{10... | collective-permute-start | bytes 602120 | tf_op jit(solution)/shard_map/ppermute | solution.py:622
  9.3 0.0 collective-permute-start
  9.3 5.0 %collective-permute-done.1.refs_2_ = f32[392,128]{1,0:T(8,128)S(1)} collective-permute-done((f32[392,128]{1,0:T(8,128)S(1)}, f32[392,128]{1,0:T(8,128)S(1)}, u32[]{:S(2)}, u32[]{:S(2)}) %collective-permute-start.1) | collective-permute-done | bytes 200736 | tf_op jit(solution)/shard_map/ppermute | solution.py:622
  14.3 0.0 collective-permute-start.2
  14.3 0.0 collective-permute-done.4.few_in
  14.4 1.5 %collective-permute-start.5 = (f32[520,128]{1,0:T(8,128)S(1)}, f32[520,128]{1,0:T(8,128)S(1)}, u32[]{:S(2)}, u32[]{:S(2)}) collective-permute-start(f32[520,128]{1,0:T(8,128)S(1)} %broadcast_select_fusion.refs_0_), channel_id=1, source_target_pairs={{0,1},{1,0},{2,3},{3,2},{4,5},{5,4},{6,7},{7,6},{8,9},{9,8},{10,11... | collective-permute-start | bytes 798728 | tf_op jit(solution)/shard_map/ppermute | solution.py:622
  15.8 5.4 %collective-permute-start.6 = (f32[520,128]{1,0:T(8,128)S(1)}, f32[520,128]{1,0:T(8,128)S(1)}, u32[]{:S(2)}, u32[]{:S(2)}) collective-permute-start(f32[520,128]{1,0:T(8,128)S(1)} %broadcast_select_fusion.refs_0_), channel_id=1, source_target_pairs={{0,2},{1,3},{2,0},{3,1},{4,6},{5,7},{6,4},{7,5},{8,10},{9,11},{10,... | collective-permute-start | bytes 798728 | tf_op jit(solution)/shard_map/ppermute | solution.py:622
  21.2 1.3 %collective-permute-start.3 = (f32[384,128]{1,0:T(8,128)S(1)}, f32[384,128]{1,0:T(8,128)S(1)}, u32[]{:S(2)}, u32[]{:S(2)}) collective-permute-start(f32[384,128]{1,0:T(8,128)S(1)} %get-tuple-element.52.rest), channel_id=1, source_target_pairs={{5,2},{6,1},{7,0},{13,10},{14,9},{15,8},{21,18},{22,17},{23,16},{2... | collective-permute-start | bytes 589832 | tf_op jit(solution)/shard_map/ppermute | solution.py:591
  22.5 0.0 collective-permute-done.refs_1_
  22.6 0.0 collective-permute-done.2.refs_3_
  22.6 2.1 %shard_map.29 = (f32[4,128,128]{2,1,0:T(8,128)S(1)}, f32[4,128,128]{2,1,0:T(8,128)S(1)}, f32[4,128,128]{2,1,0:T(8,128)S(1)}, f32[4,128,128]{2,1,0:T(8,128)S(1)}, f32[136,128]{1,0:T(8,128)S(1)}) custom-call(s32[4,9]{1,0:T(4,128)S(1)} %maximum_convert_fusion.lists, f32[392,128]{1,0:T(8,128)S(1)} %get-tuple-element.51.refs_0_, ...), custom_call_target="tpu_custom_call" | custom-call | tf_op jit(solution)/shard_map/pallas_call | solution.py:569
  24.7 5.4 %collective-permute-start.8 = (f32[136,128]{1,0:T(8,128)S(1)}, f32[136,128]{1,0:T(8,128)S(1)}, u32[]{:S(2)}, u32[]{:S(2)}) collective-permute-start(f32[136,128]{1,0:T(8,128)S(1)} %get-tuple-element.58.own_pack.refs_8_), channel_id=1, source_target_pairs={{0,7},{1,6},{2,5},{3,4},{4,3},{5,2},{6,1},{7,0},{8,15},{9,14},{10,... | collective-permute-start | bytes 208904 | tf_op jit(solution)/shard_map/ppermute | solution.py:592
  30.1 3.6 %collective-permute-done.3.rest_in = f32[384,128]{1,0:T(8,128)S(1)} collective-permute-done((f32[384,128]{1,0:T(8,128)S(1)}, f32[384,128]{1,0:T(8,128)S(1)}, u32[]{:S(2)}, u32[]{:S(2)}) %collective-permute-start.3) | collective-permute-done | bytes 196640 | tf_op jit(solution)/shard_map/ppermute | solution.py:591
  33.7 0.0 collective-permute-done.5.refs_1_
  33.7 0.0 collective-permute-done.6.refs_2_
  33.7 0.7 collective-permute-done.8.pack_in
  34.5 1.5 %collective-permute-start.9 = (f32[792,128]{1,0:T(8,128)S(1)}, f32[792,128]{1,0:T(8,128)S(1)}, u32[]{:S(2)}, u32[]{:S(2)}) collective-permute-start(f32[792,128]{1,0:T(8,128)S(1)} %shard_map.30.refs_4_), channel_id=1, source_target_pairs={{0,1},{1,0},{2,3},{3,2},{4,5},{5,4},{6,7},{7,6},{8,9},{9,8},{10,11... | collective-permute-start | bytes 1216520 | tf_op jit(solution)/shard_map/ppermute | solution.py:622
  35.9 1.3 %collective-permute-start.10 = (f32[792,128]{1,0:T(8,128)S(1)}, f32[792,128]{1,0:T(8,128)S(1)}, u32[]{:S(2)}, u32[]{:S(2)}) collective-permute-start(f32[792,128]{1,0:T(8,128)S(1)} %shard_map.30.refs_4_), channel_id=1, source_target_pairs={{0,2},{1,3},{2,0},{3,1},{4,6},{5,7},{6,4},{7,5},{8,10},{9,11},{10,... | collective-permute-start | bytes 1216520 | tf_op jit(solution)/shard_map/ppermute | solution.py:622
  37.3 7.1 %collective-permute-done.9.refs_5_ = f32[792,128]{1,0:T(8,128)S(1)} collective-permute-done((f32[792,128]{1,0:T(8,128)S(1)}, f32[792,128]{1,0:T(8,128)S(1)}, u32[]{:S(2)}, u32[]{:S(2)}) %collective-permute-start.9) | collective-permute-done | bytes 405536 | tf_op jit(solution)/shard_map/ppermute | solution.py:622
  44.4 0.7 collective-permute-start.11
  45.1 0.0 collective-permute-start.7
  45.1 6.4 %collective-permute-done.7.refs_3_ = f32[520,128]{1,0:T(8,128)S(1)} collective-permute-done((f32[520,128]{1,0:T(8,128)S(1)}, f32[520,128]{1,0:T(8,128)S(1)}, u32[]{:S(2)}, u32[]{:S(2)}) %collective-permute-start.7) | collective-permute-done | bytes 266272 | tf_op jit(solution)/shard_map/ppermute | solution.py:622
  51.5 0.0 collective-permute-done.10.refs_6_
  51.5 1.9 %collective-permute-done.11.refs_7_ = f32[792,128]{1,0:T(8,128)S(1)} collective-permute-done((f32[792,128]{1,0:T(8,128)S(1)}, f32[792,128]{1,0:T(8,128)S(1)}, u32[]{:S(2)}, u32[]{:S(2)}) %collective-permute-start.11) | collective-permute-done | bytes 405536 | tf_op jit(solution)/shard_map/ppermute | solution.py:622
  53.4 6.3 %shard_map.31 = (f32[32,128,128]{2,1,0:T(8,128)S(1)}, bf16[1024,1024]{1,0:T(8,128)(2,1)S(1)}, bf16[1024,1024]{1,0:T(8,128)(2,1)S(1)}, f32[8,1024]{1,0:T(8,128)S(...) custom-call(f32[520,128]{1,0:T(8,128)S(1)} %broadcast_select_fusion., ...), custom_call_target="tpu_custom_call" | custom-call | flops 6442450944 | tf_op jit(solution)/shard_map/pallas_call | solution.py:569
  59.7 0.1 collective-permute-start.12
  59.8 1.6 %collective-permute-start.13 = (f32[136,128]{1,0:T(8,128)S(1)}, f32[136,128]{1,0:T(8,128)S(1)}, u32[]{:S(2)}, u32[]{:S(2)}) collective-permute-start(f32[136,128]{1,0:T(8,128)S(1)} %get-tuple-element.59.refs_0_), channel_id=1, source_target_pairs={{0,16},{8,24},{16,0},{24,8},{1,17},{9,25},{17,1},{25,9},{2,18},{10... | collective-permute-start | bytes 208904 | tf_op jit(solution)/shard_map/ppermute | solution.py:582
  61.3 0.3 collective-permute-start.14
  61.6 4.4 %shard_map.33 = (f32[32,128,128]{2,1,0:T(8,128)S(1)}, f32[32,128,128]{2,1,0:T(8,128)S(1)}) custom-call(f32[32,128,128]{2,1,0:T(8,128)S(1)} %get-tuple-element.67.m_ref.refs_4_, bf16[1024,1024]{1,0:T(8,128)(2,1)S(1)} %get-tuple-element.68.mh, bf16[1024,1024]{1,0:T(8,128)(2,1)S(1)} %get-tuple-element.69.ml, f32[32,128,128]{2,1,0:T(8,128)S(1)} %get-tuple-element.70.s_ref, ...), custom_call_target="tpu_custom_call" | custom-call | flops 6442450944 | tf_op jit(solution)/shard_map/pallas_call | solution.py:569
  66.0 0.0 collective-permute-done.12.refs_1_
  66.0 0.0 collective-permute-done.13.refs_2_
  66.0 0.0 collective-permute-done.14.refs_3_
  66.0 2.3 %shard_map.32 = (f32[8,128]{1,0:T(8,128)S(1)}, f32[4,128,128]{2,1,0:T(8,128)S(1)}, f32[4,128,128]{2,1,0:T(8,128)S(1)}, f32[4,128,128]{2,1,0:T(8,128)S(1)}, f32[4...) custom-call(s32[4,9]{1,0:T(4,128)S(1)} %maximum_convert_fusion.lists, f32[136,128]{1,0:T(8,128)S(1)} %get-tuple-element.59.refs_0_, ...), custom_call_target="tpu_custom_call" | custom-call | flops 1610612736 | tf_op jit(solution)/shard_map/pallas_call | solution.py:569
  68.3 0.6 collective-permute-start.15
  68.9 1.5 %collective-permute-start.16 = (f32[136,128]{1,0:T(8,128)S(1)}, f32[136,128]{1,0:T(8,128)S(1)}, u32[]{:S(2)}, u32[]{:S(2)}) collective-permute-start(f32[136,128]{1,0:T(8,128)S(1)} %get-tuple-element.78.refs_1_.refs_4_), channel_id=1, source_target_pairs={{0,4},{1,5},{2,6},{3,7},{4,0},{5,1},{6,2},{7,3},{8,12},{9,13},{10,... | collective-permute-start | bytes 208904 | tf_op jit(solution)/shard_map/ppermute | solution.py:628
  70.4 2.4 %collective-permute-start.17 = (f32[136,128]{1,0:T(8,128)S(1)}, f32[136,128]{1,0:T(8,128)S(1)}, u32[]{:S(2)}, u32[]{:S(2)}) collective-permute-start(f32[136,128]{1,0:T(8,128)S(1)} %get-tuple-element.78.refs_1_.refs_4_), channel_id=1, source_target_pairs={{0,6},{1,7},{2,4},{3,5},{4,2},{5,3},{6,0},{7,1},{8,14},{9,15},{10,... | collective-permute-start | bytes 208904 | tf_op jit(solution)/shard_map/ppermute | solution.py:628
  72.8 7.0 %shard_map.34 = (f32[32,128,128]{2,1,0:T(8,128)S(1)}, bf16[1024,1024]{1,0:T(8,128)(2,1)S(1)}, bf16[1024,1024]{1,0:T(8,128)(2,1)S(1)}, f32[32,128,128]{2,1,0:T(8,...) custom-call(f32[8,128]{1,0:T(8,128)S(1)} %get-tuple-element.65.coef, ...), custom_call_target="tpu_custom_call" | custom-call | flops 6442450944 | tf_op jit(solution)/shard_map/pallas_call | solution.py:569
  79.8 0.0 collective-permute-done.15.refs_5_
  79.8 0.0 collective-permute-done.16.refs_6_
  79.9 0.0 collective-permute-done.17.refs_7_
  79.9 0.1 collective-permute-start.18
  79.9 1.6 %collective-permute-start.19 = (f32[136,128]{1,0:T(8,128)S(1)}, f32[136,128]{1,0:T(8,128)S(1)}, u32[]{:S(2)}, u32[]{:S(2)}) collective-permute-start(f32[136,128]{1,0:T(8,128)S(1)} %get-tuple-element.77.refs_0_), channel_id=1, source_target_pairs={{0,16},{8,24},{16,0},{24,8},{1,17},{9,25},{17,1},{25,9},{2,18},{10... | collective-permute-start | bytes 208904 | tf_op jit(solution)/shard_map/ppermute | solution.py:582
  81.5 0.3 collective-permute-start.20
  81.8 1.5 %collective-permute-start.21 = (f32[544,128]{1,0:T(8,128)S(1)}, f32[544,128]{1,0:T(8,128)S(1)}, u32[]{:S(2)}, u32[]{:S(2)}) collective-permute-start(f32[544,128]{1,0:T(8,128)S(1)} %pad_maximum_fusion), channel_id=1, source_target_pairs={{0,1},{1,0},{2,3},{3,2},{4,5},{5,4},{6,7},{7,6},{8,9},{9,8},{10,11... | collective-permute-start | bytes 835592 | tf_op jit(solution)/shard_map/ppermute | solution.py:634
  83.3 4.4 %shard_map.35 = (f32[32,128,128]{2,1,0:T(8,128)S(1)}, f32[32,128,128]{2,1,0:T(8,128)S(1)}) custom-call(f32[32,128,128]{2,1,0:T(8,128)S(1)} %get-tuple-element.82.m_ref.refs_11_, bf16[1024,1024]{1,0:T(8,128)(2,1)S(1)} %get-tuple-element.83.mh, bf16[1024,1024]{1,0:T(8,128)(2,1)S(1)} %get-tuple-element.84.ml, f32[32,128,128]{2,1,0:T(8,128)S(1)} %get-tuple-element.85.s_ref, ...), custom_call_target="tpu_custom_call" | custom-call | flops 6442450944 | tf_op jit(solution)/shard_map/pallas_call | solution.py:569
  87.7 0.0 collective-permute-done.18.refs_1_
  87.7 0.0 collective-permute-done.19.refs_2_
  87.7 0.0 collective-permute-done.20.refs_3_
  87.7 3.1 %collective-permute-done.21.refs_8_ = f32[544,128]{1,0:T(8,128)S(1)} collective-permute-done((f32[544,128]{1,0:T(8,128)S(1)}, f32[544,128]{1,0:T(8,128)S(1)}, u32[]{:S(2)}, u32[]{:S(2)}) %collective-permute-start.21) | collective-permute-done | bytes 278560 | tf_op jit(solution)/shard_map/ppermute | solution.py:634
  90.8 5.6 %shard_map.36 = (f32[9,128,128]{2,1,0:T(8,128)S(1)}, f32[9,128,128]{2,1,0:T(8,128)S(1)}, f32[8,128]{1,0:T(8,128)S(1)}) custom-call(s32[4,9]{1,0:T(4,128)S(1)} %maximum_convert_fusion.lists, f32[136,128]{1,0:T(8,128)S(1)} %get-tuple-element.77.refs_0_, f32[136,128]{1,0:T(8,128)S(1)} %collective-permute-done.18.refs_1_, ...), custom_call_target="tpu_custom_call" | custom-call | tf_op jit(solution)/shard_map/pallas_call | solution.py:569
  96.4 9.6 %all_to_all.8 = f32[32,1,128]{2,1,0:T(1,128)S(1)} all-to-all(f32[32,1,128]{2,1,0:T(1,128)S(1)} %broadcast_in_dim.2), channel_id=1, replica_groups=mesh['row'=4,'col'=8] {'row','col'}, dimensions={0} | all-to-all | bytes 32768 | tf_op jit(solution)/shard_map/all_to_all | solution.py:729
  106.0 1.0 shard_map.37
  (11 shorter events, 0.2 us)
Async XLA Ops:
  0.0 1.1 copy-start
  1.1 0.7 copy-start.1
  1.8 12.6 %collective-permute-start.4 = (f32[520,128]{1,0:T(8,128)S(1)}, f32[520,128]{1,0:T(8,128)S(1)}, u32[]{:S(2)}, u32[]{:S(2)}) collective-permute-start(f32[520,128]{1,0:T(8,128)S(1)} %get-tuple-element.53.few), channel_id=1, source_target_pairs={{0,7},{1,6},{2,5},{3,4},{4,3},{5,2},{6,1},{7,0},{8,15},{9,14},{10,... | collective-permute-start | bytes 798728 | tf_op jit(solution)/shard_map/ppermute | solution.py:590
  7.8 6.4 %collective-permute-start.1 = (f32[392,128]{1,0:T(8,128)S(1)}, f32[392,128]{1,0:T(8,128)S(1)}, u32[]{:S(2)}, u32[]{:S(2)}) collective-permute-start(f32[392,128]{1,0:T(8,128)S(1)} %get-tuple-element.51.refs_0_), channel_id=1, source_target_pairs={{0,16},{8,24},{16,0},{24,8},{1,17},{9,25},{17,1},{25,9},{2,18},{10... | collective-permute-start | bytes 602120 | tf_op jit(solution)/shard_map/ppermute | solution.py:622
  9.3 13.2 %collective-permute-start = (f32[392,128]{1,0:T(8,128)S(1)}, f32[392,128]{1,0:T(8,128)S(1)}, u32[]{:S(2)}, u32[]{:S(2)}) collective-permute-start(f32[392,128]{1,0:T(8,128)S(1)} %get-tuple-element.51.refs_0_), channel_id=1, source_target_pairs={{0,8},{8,0},{16,24},{24,16},{1,9},{9,1},{17,25},{25,17},{2,10},{10... | collective-permute-start | bytes 602120 | tf_op jit(solution)/shard_map/ppermute | solution.py:622
  14.3 8.3 %collective-permute-start.2 = (f32[392,128]{1,0:T(8,128)S(1)}, f32[392,128]{1,0:T(8,128)S(1)}, u32[]{:S(2)}, u32[]{:S(2)}) collective-permute-start(f32[392,128]{1,0:T(8,128)S(1)} %collective-permute-done.1.refs_2_), channel_id=1, source_target_pairs={{0,8},{8,0},{16,24},{24,16},{1,9},{9,1},{17,25},{25,17},{2,10},{10... | collective-permute-start | bytes 602120 | tf_op jit(solution)/shard_map/ppermute | solution.py:622
  14.4 19.3 %collective-permute-start.5 = (f32[520,128]{1,0:T(8,128)S(1)}, f32[520,128]{1,0:T(8,128)S(1)}, u32[]{:S(2)}, u32[]{:S(2)}) collective-permute-start(f32[520,128]{1,0:T(8,128)S(1)} %broadcast_select_fusion.refs_0_), channel_id=1, source_target_pairs={{0,1},{1,0},{2,3},{3,2},{4,5},{5,4},{6,7},{7,6},{8,9},{9,8},{10,11... | collective-permute-start | bytes 798728 | tf_op jit(solution)/shard_map/ppermute | solution.py:622
  15.8 17.8 %collective-permute-start.6 = (f32[520,128]{1,0:T(8,128)S(1)}, f32[520,128]{1,0:T(8,128)S(1)}, u32[]{:S(2)}, u32[]{:S(2)}) collective-permute-start(f32[520,128]{1,0:T(8,128)S(1)} %broadcast_select_fusion.refs_0_), channel_id=1, source_target_pairs={{0,2},{1,3},{2,0},{3,1},{4,6},{5,7},{6,4},{7,5},{8,10},{9,11},{10,... | collective-permute-start | bytes 798728 | tf_op jit(solution)/shard_map/ppermute | solution.py:622
  21.2 12.4 %collective-permute-start.3 = (f32[384,128]{1,0:T(8,128)S(1)}, f32[384,128]{1,0:T(8,128)S(1)}, u32[]{:S(2)}, u32[]{:S(2)}) collective-permute-start(f32[384,128]{1,0:T(8,128)S(1)} %get-tuple-element.52.rest), channel_id=1, source_target_pairs={{5,2},{6,1},{7,0},{13,10},{14,9},{15,8},{21,18},{22,17},{23,16},{2... | collective-permute-start | bytes 589832 | tf_op jit(solution)/shard_map/ppermute | solution.py:591
  24.7 9.7 %collective-permute-start.8 = (f32[136,128]{1,0:T(8,128)S(1)}, f32[136,128]{1,0:T(8,128)S(1)}, u32[]{:S(2)}, u32[]{:S(2)}) collective-permute-start(f32[136,128]{1,0:T(8,128)S(1)} %get-tuple-element.58.own_pack.refs_8_), channel_id=1, source_target_pairs={{0,7},{1,6},{2,5},{3,4},{4,3},{5,2},{6,1},{7,0},{8,15},{9,14},{10,... | collective-permute-start | bytes 208904 | tf_op jit(solution)/shard_map/ppermute | solution.py:592
  34.5 9.9 %collective-permute-start.9 = (f32[792,128]{1,0:T(8,128)S(1)}, f32[792,128]{1,0:T(8,128)S(1)}, u32[]{:S(2)}, u32[]{:S(2)}) collective-permute-start(f32[792,128]{1,0:T(8,128)S(1)} %shard_map.30.refs_4_), channel_id=1, source_target_pairs={{0,1},{1,0},{2,3},{3,2},{4,5},{5,4},{6,7},{7,6},{8,9},{9,8},{10,11... | collective-permute-start | bytes 1216520 | tf_op jit(solution)/shard_map/ppermute | solution.py:622
  35.9 15.6 %collective-permute-start.10 = (f32[792,128]{1,0:T(8,128)S(1)}, f32[792,128]{1,0:T(8,128)S(1)}, u32[]{:S(2)}, u32[]{:S(2)}) collective-permute-start(f32[792,128]{1,0:T(8,128)S(1)} %shard_map.30.refs_4_), channel_id=1, source_target_pairs={{0,2},{1,3},{2,0},{3,1},{4,6},{5,7},{6,4},{7,5},{8,10},{9,11},{10,... | collective-permute-start | bytes 1216520 | tf_op jit(solution)/shard_map/ppermute | solution.py:622
  44.4 9.0 %collective-permute-start.11 = (f32[792,128]{1,0:T(8,128)S(1)}, f32[792,128]{1,0:T(8,128)S(1)}, u32[]{:S(2)}, u32[]{:S(2)}) collective-permute-start(f32[792,128]{1,0:T(8,128)S(1)} %collective-permute-done.9.refs_5_), channel_id=1, source_target_pairs={{0,2},{1,3},{2,0},{3,1},{4,6},{5,7},{6,4},{7,5},{8,10},{9,11},{10,... | collective-permute-start | bytes 1216520 | tf_op jit(solution)/shard_map/ppermute | solution.py:622
  45.1 6.4 %collective-permute-start.7 = (f32[520,128]{1,0:T(8,128)S(1)}, f32[520,128]{1,0:T(8,128)S(1)}, u32[]{:S(2)}, u32[]{:S(2)}) collective-permute-start(f32[520,128]{1,0:T(8,128)S(1)} %collective-permute-done.6.refs_2_), channel_id=1, source_target_pairs={{0,1},{1,0},{2,3},{3,2},{4,5},{5,4},{6,7},{7,6},{8,9},{9,8},{10,11... | collective-permute-start | bytes 798728 | tf_op jit(solution)/shard_map/ppermute | solution.py:622
  59.7 6.3 %collective-permute-start.12 = (f32[136,128]{1,0:T(8,128)S(1)}, f32[136,128]{1,0:T(8,128)S(1)}, u32[]{:S(2)}, u32[]{:S(2)}) collective-permute-start(f32[136,128]{1,0:T(8,128)S(1)} %get-tuple-element.59.refs_0_), channel_id=1, source_target_pairs={{0,8},{8,0},{16,24},{24,16},{1,9},{9,1},{17,25},{25,17},{2,10},{10... | collective-permute-start | bytes 208904 | tf_op jit(solution)/shard_map/ppermute | solution.py:582
  59.8 6.2 %collective-permute-start.13 = (f32[136,128]{1,0:T(8,128)S(1)}, f32[136,128]{1,0:T(8,128)S(1)}, u32[]{:S(2)}, u32[]{:S(2)}) collective-permute-start(f32[136,128]{1,0:T(8,128)S(1)} %get-tuple-element.59.refs_0_), channel_id=1, source_target_pairs={{0,16},{8,24},{16,0},{24,8},{1,17},{9,25},{17,1},{25,9},{2,18},{10... | collective-permute-start | bytes 208904 | tf_op jit(solution)/shard_map/ppermute | solution.py:582
  61.3 4.7 %collective-permute-start.14 = (f32[136,128]{1,0:T(8,128)S(1)}, f32[136,128]{1,0:T(8,128)S(1)}, u32[]{:S(2)}, u32[]{:S(2)}) collective-permute-start(f32[136,128]{1,0:T(8,128)S(1)} %get-tuple-element.59.refs_0_), channel_id=1, source_target_pairs={{0,24},{8,16},{16,8},{24,0},{1,25},{9,17},{17,9},{25,1},{2,26},{10... | collective-permute-start | bytes 208904 | tf_op jit(solution)/shard_map/ppermute | solution.py:582
  68.3 11.5 %collective-permute-start.15 = (f32[136,128]{1,0:T(8,128)S(1)}, f32[136,128]{1,0:T(8,128)S(1)}, u32[]{:S(2)}, u32[]{:S(2)}) collective-permute-start(f32[136,128]{1,0:T(8,128)S(1)} %get-tuple-element.78.refs_1_.refs_4_), channel_id=1, source_target_pairs={{0,2},{1,3},{2,0},{3,1},{4,6},{5,7},{6,4},{7,5},{8,10},{9,11},{10,... | collective-permute-start | bytes 208904 | tf_op jit(solution)/shard_map/ppermute | solution.py:628
  68.9 10.9 %collective-permute-start.16 = (f32[136,128]{1,0:T(8,128)S(1)}, f32[136,128]{1,0:T(8,128)S(1)}, u32[]{:S(2)}, u32[]{:S(2)}) collective-permute-start(f32[136,128]{1,0:T(8,128)S(1)} %get-tuple-element.78.refs_1_.refs_4_), channel_id=1, source_target_pairs={{0,4},{1,5},{2,6},{3,7},{4,0},{5,1},{6,2},{7,3},{8,12},{9,13},{10,... | collective-permute-start | bytes 208904 | tf_op jit(solution)/shard_map/ppermute | solution.py:628
  70.4 9.5 %collective-permute-start.17 = (f32[136,128]{1,0:T(8,128)S(1)}, f32[136,128]{1,0:T(8,128)S(1)}, u32[]{:S(2)}, u32[]{:S(2)}) collective-permute-start(f32[136,128]{1,0:T(8,128)S(1)} %get-tuple-element.78.refs_1_.refs_4_), channel_id=1, source_target_pairs={{0,6},{1,7},{2,4},{3,5},{4,2},{5,3},{6,0},{7,1},{8,14},{9,15},{10,... | collective-permute-start | bytes 208904 | tf_op jit(solution)/shard_map/ppermute | solution.py:628
  79.9 7.8 %collective-permute-start.18 = (f32[136,128]{1,0:T(8,128)S(1)}, f32[136,128]{1,0:T(8,128)S(1)}, u32[]{:S(2)}, u32[]{:S(2)}) collective-permute-start(f32[136,128]{1,0:T(8,128)S(1)} %get-tuple-element.77.refs_0_), channel_id=1, source_target_pairs={{0,8},{8,0},{16,24},{24,16},{1,9},{9,1},{17,25},{25,17},{2,10},{10... | collective-permute-start | bytes 208904 | tf_op jit(solution)/shard_map/ppermute | solution.py:582
  79.9 7.8 %collective-permute-start.19 = (f32[136,128]{1,0:T(8,128)S(1)}, f32[136,128]{1,0:T(8,128)S(1)}, u32[]{:S(2)}, u32[]{:S(2)}) collective-permute-start(f32[136,128]{1,0:T(8,128)S(1)} %get-tuple-element.77.refs_0_), channel_id=1, source_target_pairs={{0,16},{8,24},{16,0},{24,8},{1,17},{9,25},{17,1},{25,9},{2,18},{10... | collective-permute-start | bytes 208904 | tf_op jit(solution)/shard_map/ppermute | solution.py:582
  81.5 6.2 %collective-permute-start.20 = (f32[136,128]{1,0:T(8,128)S(1)}, f32[136,128]{1,0:T(8,128)S(1)}, u32[]{:S(2)}, u32[]{:S(2)}) collective-permute-start(f32[136,128]{1,0:T(8,128)S(1)} %get-tuple-element.77.refs_0_), channel_id=1, source_target_pairs={{0,24},{8,16},{16,8},{24,0},{1,25},{9,17},{17,9},{25,1},{2,26},{10... | collective-permute-start | bytes 208904 | tf_op jit(solution)/shard_map/ppermute | solution.py:582
  81.8 9.0 %collective-permute-start.21 = (f32[544,128]{1,0:T(8,128)S(1)}, f32[544,128]{1,0:T(8,128)S(1)}, u32[]{:S(2)}, u32[]{:S(2)}) collective-permute-start(f32[544,128]{1,0:T(8,128)S(1)} %pad_maximum_fusion), channel_id=1, source_target_pairs={{0,1},{1,0},{2,3},{3,2},{4,5},{5,4},{6,7},{7,6},{8,9},{9,8},{10,11... | collective-permute-start | bytes 835592 | tf_op jit(solution)/shard_map/ppermute | solution.py:634
